TPU v7x, 512 devices: a whole 4x8x8 slice. The times are simulated.
512 devices in a mesh: gx: 32 (over x, y), yz: 16 (over z, core).
Axes of the slice: x: 4, y: 8, z: 8, core: 2. Of those that a mesh axis runs over, the one named last changes fastest.
Arguments:
- state: float32 [27, 128, 128, 128], P(None, 'gx', 'yz'), may hold values from -6 to 6
- mix_weights: float32 [32, 16, 4, 27, 1024], P('gx', 'yz'), may hold values from -6 to 6
- mix_frac: float32 [32, 16, 4, 1024], P('gx', 'yz'), as said below
- mix_index: int32 [32, 16, 1024], P('gx', 'yz'), may hold values from 0 to 4095, as said below
- mix_count: int32 [32, 16], P('gx', 'yz'), may hold values from 128 to 1024, as said below
- vol_matrix: float32 [27, 27], replicated, may hold values from -0.6 to 0.6
- face_matrix: float32 [27, 54], replicated, may hold values from -0.5 to 0.5
- mat_matrix: float32 [4, 27, 27], replicated, may hold values from -0.6 to 0.6
Outputs:
- field: float32 [27, 128, 128, 128], P(None, 'gx', 'yz')
- weights_out: float32 [32, 16, 4, 27, 1024], P('gx', 'yz')
Inputs may be any that keep to these rules, and one draw needn't show every extreme that they name: `mix_index`: within one device's list the entries are distinct zone numbers of that device's block. `mix_count`: one device has 1024 live slots and another 1024 // 8. `mix_frac`: Positive; the 4 fractions of a slot sum to one.
All inputs are finite; a program needn't handle non-finite values.
Results may differ from a plain program's by a relative error of at most 0.0001.
Values sent between devices are 32-bit elements; how exact they have to be, the bound alone decides.
No kernel may reach another device: no remote copies, remote signals or barrier semaphores. Data moves between devices by JAX's collectives and lax.ppermute only.
A program may use at most 128 MiB of HBM per device.

v0:
```python
import jax
import jax.numpy as jnp
from jax import lax
from jax.sharding import PartitionSpec as P

SWEEPS = 4


highest = lax.Precision.HIGHEST
SECTIONS = ((0.0, 1.0), (0.75, 0.25), (1.0 / 3.0, 2.0 / 3.0))


def extended(shard, sides, width):
    for axis, dim in sides:
        devices, length = (lax.axis_size(axis), shard.shape[dim])
        up = [(i, (i + 1) % devices) for i in range(devices - 1)]
        down = [(j, i) for i, j in up]
        last = lax.slice_in_dim(shard, length - width, length, axis=dim)
        leading = lax.slice_in_dim(shard, 0, width, axis=dim)
        before = lax.ppermute(last, axis, up)
        after = lax.ppermute(leading, axis, down)
        shard = jnp.concatenate([before, shard, after], axis=dim)
    return shard


def jump_rates(field, lattice, x_jumps, y_jumps, volume, lifting):
    nx_cells, ny_cells, nz_cells = (field.shape[1], field.shape[2], field.shape[3])
    zeros_rim = jnp.zeros((3, 3, nx_cells, ny_cells, 1), field.dtype)
    below_z = jnp.concatenate([zeros_rim, lattice[:, :, 2, :, :, :-1]], axis=-1)
    above_z = jnp.concatenate([lattice[:, :, 0, :, :, 1:], zeros_rim], axis=-1)
    jumps = [
        x_jumps[0],
        x_jumps[1],
        y_jumps[0],
        y_jumps[1],
        below_z - lattice[:, :, 0],
        above_z - lattice[:, :, 2],
    ]
    stacked = jnp.concatenate([jump.reshape(9, -1) for jump in jumps], axis=0)
    return jnp.dot(volume, field.reshape(27, -1), precision=highest) + jnp.dot(
        lifting, stacked, precision=highest
    )


def trace_rates(field, volume, lifting):
    nx_cells, ny_cells, nz_cells = (field.shape[1], field.shape[2], field.shape[3])
    lattice = field.reshape(3, 3, 3, nx_cells, ny_cells, nz_cells)
    x_planes = jnp.stack(
        [
            lattice[0, :, :, 0].reshape(9, ny_cells, nz_cells),
            lattice[2, :, :, nx_cells - 1].reshape(9, ny_cells, nz_cells),
        ],
        axis=1,
    )
    x_ext = extended(x_planes, (("gx", 1),), 1)
    y_planes = jnp.stack(
        [
            lattice[:, 0, :, :, 0].reshape(9, nx_cells, nz_cells),
            lattice[:, 2, :, :, ny_cells - 1].reshape(9, nx_cells, nz_cells),
        ],
        axis=2,
    )
    y_ext = extended(y_planes, (("yz", 2),), 1)
    low_x = x_ext[:, 0].reshape(3, 3, 1, ny_cells, nz_cells)
    high_x = x_ext[:, 3].reshape(3, 3, 1, ny_cells, nz_cells)
    low_y = y_ext[:, :, 0].reshape(3, 3, nx_cells, 1, nz_cells)
    high_y = y_ext[:, :, 3].reshape(3, 3, nx_cells, 1, nz_cells)
    below_x = jnp.concatenate([low_x, lattice[2, :, :, :-1]], axis=2)
    above_x = jnp.concatenate([lattice[0, :, :, 1:], high_x], axis=2)
    below_y = jnp.concatenate([low_y, lattice[:, 2, :, :, :-1]], axis=3)
    above_y = jnp.concatenate([lattice[:, 0, :, :, 1:], high_y], axis=3)
    x_jumps = (below_x - lattice[0], above_x - lattice[2])
    y_jumps = (below_y - lattice[:, 0], above_y - lattice[:, 2])
    return jump_rates(field, lattice, x_jumps, y_jumps, volume, lifting)


def sweep_rates(weights_now, resid, mat_matrix):
    iterate = weights_now
    for sweep in range(SWEEPS):
        iterate = weights_now + jnp.einsum("mpq,mqs->mps", mat_matrix, iterate, precision=highest)
    return iterate - weights_now + resid[None]


def blocked_rates(weights_now, resid, mat_matrix, live_count, width):
    block_count = (live_count + width - 1) // width

    def advance(step, total):
        first = step * width
        w_block = lax.dynamic_slice_in_dim(weights_now, first, width, 2)
        r_block = lax.dynamic_slice_in_dim(resid, first, width, 1)
        keep = first + jnp.arange(width, dtype=jnp.int32) < live_count
        result = jnp.where(keep[None, None], sweep_rates(w_block, r_block, mat_matrix), 0.0)
        return lax.dynamic_update_slice_in_dim(total, result, first, 2)

    return lax.fori_loop(jnp.int32(0), block_count, advance, jnp.zeros_like(weights_now))


def place(field, zone_ids, live, closure):
    flat_field = field.reshape(27, -1)
    current = jnp.take(flat_field, zone_ids, axis=1)
    return (
        flat_field.at[:, zone_ids].set(jnp.where(live[None], closure, current)).reshape(field.shape)
    )


def on_device(
    state, mix_weights, mix_frac, mix_index, mix_count, vol_matrix, face_matrix, mat_matrix
):
    capacity = mix_index.shape[-1]
    materials = mix_weights.shape[2]
    zone_ids = mix_index.reshape(capacity)
    live_count = mix_count.reshape(())
    live = jnp.arange(capacity, dtype=jnp.int32) < live_count
    w_start = mix_weights.reshape(materials, 27, capacity)
    fractions = mix_frac.reshape(materials, capacity)
    width = 128
    field = state
    w_now = w_start
    for old_part, new_part in SECTIONS:
        rate = trace_rates(field, vol_matrix, face_matrix)
        resid = jnp.take(rate, zone_ids, axis=1)
        rate_w = blocked_rates(w_now, resid, mat_matrix, live_count, width)
        w_next = old_part * w_start + new_part * (w_now + rate_w)
        field = old_part * state + new_part * (field + rate.reshape(state.shape))
        closure = jnp.sum(fractions[:, None, :] * w_next, axis=0)
        field = place(field, zone_ids, live, closure)
        w_now = w_next
    return (field, w_now.reshape(mix_weights.shape))


def solution(mesh):
    placed = (
        P(None, "gx", "yz", None),
        P("gx", "yz", None, None, None),
        P("gx", "yz", None, None),
        P("gx", "yz", None),
        P("gx", "yz"),
        P(),
        P(),
        P(),
    )
    return jax.shard_map(
        on_device,
        mesh=mesh,
        in_specs=placed,
        out_specs=(P(None, "gx", "yz", None), P("gx", "yz", None, None, None)),
        check_vma=False,
    )
```

profile of v0, /device:TPU:354, one launch (start us, length us, event | category | flops | bytes accessed | tf_op | source)
XLA Modules:
  0.0 179.1 jit_solution(14515141304654706858)
XLA Ops:
  0.7 1.1 fusion.63
  1.7 1.9 %collective-permute-start.2 = (f32[9,4,1,128]{3,1,0,2:T(4,128)S(1)}, f32[9,4,1,128]{3,1,0,2:T(4,128)S(1)}, u32[]{:S(2)}, u32[]{:S(2)}) collective-permute-start(f32[9,4,1,128]{3,1,0,2:T(4,128)S(1)} %bitcast.489), channel_id=1, source_target_pairs={{0,1},{1,2},{2,3},{3,4},{4,5},{5,6},{6,7},{7,8},{8,9},{9,10},{10,1... | collective-permute-start | bytes 55304 | tf_op jit(solution)/shard_map/ppermute | solution.py:20
  3.7 3.6 %collective-permute-start.3 = (f32[9,4,1,128]{3,1,0,2:T(4,128)S(1)}, f32[9,4,1,128]{3,1,0,2:T(4,128)S(1)}, u32[]{:S(2)}, u32[]{:S(2)}) collective-permute-start(f32[9,4,1,128]{3,1,0,2:T(4,128)S(1)} %bitcast.488), channel_id=1, source_target_pairs={{1,0},{2,1},{3,2},{4,3},{5,4},{6,5},{7,6},{8,7},{9,8},{10,9},{11,1... | collective-permute-start | bytes 55304 | tf_op jit(solution)/shard_map/ppermute | solution.py:21
  7.3 1.4 fusion.64
  8.7 2.6 %collective-permute-start = (f32[9,1,8,128]{3,2,0,1:T(8,128)}, f32[9,1,8,128]{3,2,0,1:T(8,128)}, u32[]{:S(2)}, u32[]{:S(2)}) collective-permute-start(f32[9,1,8,128]{3,2,0,1:T(8,128)} %bitcast.13), channel_id=1, source_target_pairs={{0,16},{16,32},{32,48},{48,64},{64,80},{80,96},{96,112},{112,128},... | collective-permute-start | bytes 110600 | tf_op jit(solution)/shard_map/ppermute | solution.py:20
  11.3 4.5 %collective-permute-start.1 = (f32[9,1,8,128]{3,2,0,1:T(8,128)}, f32[9,1,8,128]{3,2,0,1:T(8,128)}, u32[]{:S(2)}, u32[]{:S(2)}) collective-permute-start(f32[9,1,8,128]{3,2,0,1:T(8,128)} %bitcast.17), channel_id=1, source_target_pairs={{16,0},{32,16},{48,32},{64,48},{80,64},{96,80},{112,96},{128,112},... | collective-permute-start | bytes 110600 | tf_op jit(solution)/shard_map/ppermute | solution.py:21
  15.8 1.0 slice_bitcast_fusion.16
  16.8 1.0 fusion.62
  17.8 1.7 slice_bitcast_fusion.24
  19.5 1.0 slice_bitcast_fusion.18
  22.9 0.9 pad_maximum_fusion
  24.0 1.5 concatenate.97
  25.5 0.7 convolution_bitcast_fusion.12
  26.2 1.3 convolution_add_fusion.2
  27.5 2.0 %copy.166 = f32[27,4096]{0,1:T(8,128)} copy(f32[27,4096]{1,0:T(8,128)S(1)} %convolution_add_fusion.2) | data formatting | bytes 884736 | tf_op jit(solution)/shard_map/add | solution.py:40
  29.5 4.4 %gather_fusion = f32[1024,27]{1,0:T(8,128)S(1)} fusion(f32[27,4096]{0,1:T(8,128)} %copy.166, s32[1024]{0:T(1024)S(1)} %fusion.51), kind=kCustom, calls=%fused_computation.clone | custom fusion | bytes 225280 | tf_op jit(solution)/shard_map/jit(_take)/gather | solution.py:121
  34.5 13.0 %while.30 = (s32[]{:T(128)}, f32[4,27,1024]{2,0,1:T(4,128)S(1)}, s32[]{:T(128)}, s32[]{:T(128)}, f32[4,27,1024]{2,0,1:T(4,128)S(1)}, /*index=5*/f32[4,27,27]{2,1...) while((s32[]{:T(128)}, f32[4,27,1024]{2,0,1:T(4,128)S(1)}, ...), condition=%wide.region_1.3_spmd, body=%wide.region_0.0_spmd.sunk | while | flops 18012932 | bytes 928239 | solution.py:95
  47.6 1.0 multiply_reduce_fusion.2
  48.5 1.0 copy.172
  49.7 0.8 fusion.35
  50.5 1.7 copy.165
  52.2 7.5 %scatter_custom_fusion = f32[27,4096]{0,1:T(8,128)S(1)} fusion(f32[27,4096]{0,1:T(8,128)S(1)} %bitcast.425, s32[1024]{0:T(1024)S(1)} %bitcast.492, f32[27,1024]{0,1:T(8,128)S(1)} %copy-done.11, f32[]{:T(128)} %constant.17.clone.6, pred[1024]{0:T(1024)(128)(4,1)S(1)} %get-tuple-element.317, pred[1024]{0:T(1024)(128)(4,1)S(1)} %get-tuple-element.316, ...), kind=kCustom, calls=%fused_computation.69 | custom fusion | flops 55296 | bytes 3069956 | tf_op jit(solution)/shard_map/scatter | solution.py:102
  60.6 0.7 slice_bitcast_fusion.10
  62.0 0.7 fusion.59
  62.7 0.7 slice_bitcast_fusion.22
  63.4 3.1 %fusion.65 = f32[4096,27]{0,1:T(8,128)} fusion(f32[27,4096]{0,1:T(8,128)S(1)} %scatter_custom_fusion, f32[27,27]{1,0:T(8,128)S(1)} %copy-done.24), kind=kOutput, calls=%fused_computation.165 | convolution fusion | flops 35831808 | bytes 887652 | tf_op jit(solution)/shard_map/dot_general | solution.py:40
  66.5 2.1 %collective-permute-start.7 = (f32[9,4,1,128]{3,1,0,2:T(4,128)}, f32[9,4,1,128]{3,1,0,2:T(4,128)S(1)}, u32[]{:S(2)}, u32[]{:S(2)}) collective-permute-start(f32[9,4,1,128]{3,1,0,2:T(4,128)} %bitcast.53), channel_id=1, source_target_pairs={{1,0},{2,1},{3,2},{4,3},{5,4},{6,5},{7,6},{8,7},{9,8},{10,9},{11,1... | collective-permute-start | bytes 55304 | tf_op jit(solution)/shard_map/ppermute | solution.py:21
  68.8 1.0 squeeze.117
  69.8 2.5 %collective-permute-start.6 = (f32[9,4,1,128]{3,1,0,2:T(4,128)S(1)}, f32[9,4,1,128]{3,1,0,2:T(4,128)S(1)}, u32[]{:S(2)}, u32[]{:S(2)}) collective-permute-start(f32[9,4,1,128]{3,1,0,2:T(4,128)S(1)} %bitcast.490), channel_id=1, source_target_pairs={{0,1},{1,2},{2,3},{3,4},{4,5},{5,6},{6,7},{7,8},{8,9},{9,10},{10,1... | collective-permute-start | bytes 55304 | tf_op jit(solution)/shard_map/ppermute | solution.py:20
  72.4 1.9 %collective-permute-start.4 = (f32[9,1,8,128]{3,2,0,1:T(8,128)S(1)}, f32[9,1,8,128]{3,2,0,1:T(8,128)S(1)}, u32[]{:S(2)}, u32[]{:S(2)}) collective-permute-start(f32[9,1,8,128]{3,2,0,1:T(8,128)S(1)} %bitcast.480), channel_id=1, source_target_pairs={{0,16},{16,32},{32,48},{48,64},{64,80},{80,96},{96,112},{112,128},... | collective-permute-start | bytes 110600 | tf_op jit(solution)/shard_map/ppermute | solution.py:20
  74.3 5.1 %collective-permute-start.5 = (f32[9,1,8,128]{3,2,0,1:T(8,128)S(1)}, f32[9,1,8,128]{3,2,0,1:T(8,128)S(1)}, u32[]{:S(2)}, u32[]{:S(2)}) collective-permute-start(f32[9,1,8,128]{3,2,0,1:T(8,128)S(1)} %bitcast.478), channel_id=1, source_target_pairs={{16,0},{32,16},{48,32},{64,48},{80,64},{96,80},{112,96},{128,112},... | collective-permute-start | bytes 110600 | tf_op jit(solution)/shard_map/ppermute | solution.py:21
  79.8 1.3 collective-permute-done.5
  81.1 0.8 slice_subtract_fusion.2
  81.9 4.1 %concatenate.108 = f32[54,4096]{1,0:T(8,128)S(1)} concatenate(f32[9,4096]{1,0:T(8,128)} %get-tuple-element.263, f32[9,4096]{1,0:T(8,128)} %get-tuple-element.262, f32[9,4096]{1,0:T(8,128)S(1)} %sub.96, f32[9,4096]{1,0:T(8,128)S(1)} %sub.97, f32[9,4096]{1,0:T(8,128)S(1)} %reshape.177, f32[9,4096]{1,0:T(8,128)S(1)} %reshape.178), dimensions={0} | concatenate | bytes 1769472 | tf_op jit(solution)/shard_map/concatenate | solution.py:39
  86.1 1.5 add_multiply_fusion.1
  88.3 4.0 %gather_fusion.1 = f32[1024,27]{1,0:T(8,128)} fusion(f32[27,4096]{0,1:T(8,128)S(1)} %copy.184, s32[1024]{0:T(1024)S(1)} %fusion.51), kind=kCustom, calls=%fused_computation.2.clone | custom fusion | bytes 225280 | tf_op jit(solution)/shard_map/jit(_take)/gather | solution.py:121
  92.3 1.2 select_bitcast_fusion.1
  93.8 13.0 %while.31 = (s32[]{:T(128)}, f32[4,27,1024]{2,0,1:T(4,128)S(1)}, s32[]{:T(128)}, s32[]{:T(128)}, f32[4,27,1024]{2,0,1:T(4,128)S(1)}, /*index=5*/f32[4,27,27]{2,1...) while((s32[]{:T(128)}, f32[4,27,1024]{2,0,1:T(4,128)S(1)}, ...), condition=%wide.region_5.7_spmd, body=%wide.region_4.6_spmd.sunk | while | flops 18012932 | bytes 928239 | solution.py:95
  106.9 1.1 multiply_reduce_fusion.1
  108.0 1.0 copy.190
  109.1 0.8 bitcast_add_fusion.1
  110.0 1.7 copy.183
  111.6 7.5 %scatter_custom_fusion.1 = f32[27,4096]{0,1:T(8,128)S(1)} fusion(f32[27,4096]{0,1:T(8,128)S(1)} %bitcast.426, s32[1024]{0:T(1024)S(1)} %bitcast.493, f32[27,1024]{0,1:T(8,128)S(1)} %copy-done.12, f32[]{:T(128)} %constant.17.clone.6, pred[1024]{0:T(1024)(128)(4,1)S(1)} %get-tuple-element.317, pred[1024]{0:T(1024)(128)(4,1)S(1)} %get-tuple-element.316, ...), kind=kCustom, calls=%fused_computation.66 | custom fusion | flops 55296 | bytes 3069956 | tf_op jit(solution)/shard_map/scatter | solution.py:102
  120.0 0.7 slice_bitcast_fusion.4
  121.4 0.7 fusion.56
  122.2 0.7 slice_bitcast_fusion.20
  122.9 3.1 %fusion.66 = f32[4096,27]{0,1:T(8,128)} fusion(f32[27,4096]{0,1:T(8,128)S(1)} %scatter_custom_fusion.1, f32[27,27]{1,0:T(8,128)S(1)} %copy-done.25), kind=kOutput, calls=%fused_computation.166 | convolution fusion | flops 35831808 | bytes 887652 | tf_op jit(solution)/shard_map/dot_general | solution.py:40
  126.0 2.1 %collective-permute-start.11 = (f32[9,4,1,128]{3,1,0,2:T(4,128)}, f32[9,4,1,128]{3,1,0,2:T(4,128)S(1)}, u32[]{:S(2)}, u32[]{:S(2)}) collective-permute-start(f32[9,4,1,128]{3,1,0,2:T(4,128)} %bitcast.78), channel_id=1, source_target_pairs={{1,0},{2,1},{3,2},{4,3},{5,4},{6,5},{7,6},{8,7},{9,8},{10,9},{11,1... | collective-permute-start | bytes 55304 | tf_op jit(solution)/shard_map/ppermute | solution.py:21
  128.3 1.0 squeeze.127
  129.2 2.5 %collective-permute-start.10 = (f32[9,4,1,128]{3,1,0,2:T(4,128)S(1)}, f32[9,4,1,128]{3,1,0,2:T(4,128)S(1)}, u32[]{:S(2)}, u32[]{:S(2)}) collective-permute-start(f32[9,4,1,128]{3,1,0,2:T(4,128)S(1)} %bitcast.491), channel_id=1, source_target_pairs={{0,1},{1,2},{2,3},{3,4},{4,5},{5,6},{6,7},{7,8},{8,9},{9,10},{10,1... | collective-permute-start | bytes 55304 | tf_op jit(solution)/shard_map/ppermute | solution.py:20
  131.8 1.9 %collective-permute-start.8 = (f32[9,1,8,128]{3,2,0,1:T(8,128)S(1)}, f32[9,1,8,128]{3,2,0,1:T(8,128)S(1)}, u32[]{:S(2)}, u32[]{:S(2)}) collective-permute-start(f32[9,1,8,128]{3,2,0,1:T(8,128)S(1)} %bitcast.481), channel_id=1, source_target_pairs={{0,16},{16,32},{32,48},{48,64},{64,80},{80,96},{96,112},{112,128},... | collective-permute-start | bytes 110600 | tf_op jit(solution)/shard_map/ppermute | solution.py:20
  133.8 5.1 %collective-permute-start.9 = (f32[9,1,8,128]{3,2,0,1:T(8,128)S(1)}, f32[9,1,8,128]{3,2,0,1:T(8,128)S(1)}, u32[]{:S(2)}, u32[]{:S(2)}) collective-permute-start(f32[9,1,8,128]{3,2,0,1:T(8,128)S(1)} %bitcast.479), channel_id=1, source_target_pairs={{16,0},{32,16},{48,32},{64,48},{80,64},{96,80},{112,96},{128,112},... | collective-permute-start | bytes 110600 | tf_op jit(solution)/shard_map/ppermute | solution.py:21
  139.3 1.3 collective-permute-done.9
  140.6 0.8 slice_subtract_fusion
  141.4 4.1 %concatenate.119 = f32[54,4096]{1,0:T(8,128)S(1)} concatenate(f32[9,4096]{1,0:T(8,128)} %get-tuple-element.261, f32[9,4096]{1,0:T(8,128)} %get-tuple-element.260, f32[9,4096]{1,0:T(8,128)S(1)} %sub.102, f32[9,4096]{1,0:T(8,128)S(1)} %sub.103, f32[9,4096]{1,0:T(8,128)S(1)} %reshape.180, f32[9,4096]{1,0:T(8,128)S(1)} %reshape.181), dimensions={0} | concatenate | bytes 1769472 | tf_op jit(solution)/shard_map/concatenate | solution.py:39
  145.6 1.5 add_multiply_fusion
  147.8 4.0 %gather_fusion.2 = f32[1024,27]{1,0:T(8,128)} fusion(f32[27,4096]{0,1:T(8,128)S(1)} %copy.202, s32[1024]{0:T(1024)S(1)} %fusion.51), kind=kCustom, calls=%fused_computation.4.clone | custom fusion | bytes 225280 | tf_op jit(solution)/shard_map/jit(_take)/gather | solution.py:121
  151.7 1.2 select_bitcast_fusion
  153.3 13.0 %while.32 = (s32[]{:T(128)}, f32[4,27,1024]{2,0,1:T(4,128)S(1)}, s32[]{:T(128)}, s32[]{:T(128)}, f32[4,27,1024]{2,0,1:T(4,128)S(1)}, /*index=5*/f32[4,27,27]{2,1...) while((s32[]{:T(128)}, f32[4,27,1024]{2,0,1:T(4,128)S(1)}, ...), condition=%wide.region_9.11_spmd, body=%wide.region_8.10_spmd.sunk | while | flops 18012932 | bytes 928239 | solution.py:95
  166.4 1.1 fusion.55
  167.8 0.8 bitcast_add_fusion
  168.6 1.7 copy.201
  170.3 7.3 %scatter_custom_fusion.2 = f32[27,4096]{0,1:T(8,128)S(1)} fusion(f32[27,4096]{0,1:T(8,128)S(1)} %bitcast.435, s32[1024]{0:T(1024)S(1)} %bitcast.494, f32[27,1024]{0,1:T(8,128)S(1)} %copy.208, f32[]{:T(128)} %constant.17.clone.6, pred[1024]{0:T(1024)(128)(4,1)S(1)} %get-tuple-element.317, pred[1024]{0:T(1024)(128)(4,1)S(1)} %get-tuple-element.316, ...), kind=kCustom, calls=%fused_computation.63 | custom fusion | flops 55296 | bytes 3069956 | tf_op jit(solution)/shard_map/scatter | solution.py:102
  177.6 1.4 copy.209
  (346 shorter events, 45.6 us)
Async XLA Ops:
  0.6 24.9 %copy-start = (f32[27,54]{1,0:T(8,128)S(1)}, f32[27,54]{1,0:T(8,128)}, u32[]{:S(2)}) copy-start(f32[27,54]{1,0:T(8,128)} %param.22) | copy-start | bytes 17500
  0.6 19.8 %copy-start.1 = (f32[27,4,8,128]{3,2,1,0:T(8,128)S(1)}, f32[27,4,8,128]{3,2,1,0:T(8,128)}, u32[]{:S(2)}) copy-start(f32[27,4,8,128]{3,2,1,0:T(8,128)} %param.16) | copy-start | bytes 1327108
  0.7 19.9 %copy-start.30 = (s32[1,1,1024]{2,1,0:T(1,128)S(1)}, s32[1,1,1024]{2,1,0:T(1,128)}, u32[]{:S(2)}) copy-start(s32[1,1,1024]{2,1,0:T(1,128)} %param.19) | copy-start | bytes 12292
  1.7 20.7 %collective-permute-start.2 = (f32[9,4,1,128]{3,1,0,2:T(4,128)S(1)}, f32[9,4,1,128]{3,1,0,2:T(4,128)S(1)}, u32[]{:S(2)}, u32[]{:S(2)}) collective-permute-start(f32[9,4,1,128]{3,1,0,2:T(4,128)S(1)} %bitcast.489), channel_id=1, source_target_pairs={{0,1},{1,2},{2,3},{3,4},{4,5},{5,6},{6,7},{7,8},{8,9},{9,10},{10,1... | collective-permute-start | bytes 55304 | tf_op jit(solution)/shard_map/ppermute | solution.py:20
  3.7 18.7 %collective-permute-start.3 = (f32[9,4,1,128]{3,1,0,2:T(4,128)S(1)}, f32[9,4,1,128]{3,1,0,2:T(4,128)S(1)}, u32[]{:S(2)}, u32[]{:S(2)}) collective-permute-start(f32[9,4,1,128]{3,1,0,2:T(4,128)S(1)} %bitcast.488), channel_id=1, source_target_pairs={{1,0},{2,1},{3,2},{4,3},{5,4},{6,5},{7,6},{8,7},{9,8},{10,9},{11,1... | collective-permute-start | bytes 55304 | tf_op jit(solution)/shard_map/ppermute | solution.py:21
  8.7 13.9 %collective-permute-start = (f32[9,1,8,128]{3,2,0,1:T(8,128)}, f32[9,1,8,128]{3,2,0,1:T(8,128)}, u32[]{:S(2)}, u32[]{:S(2)}) collective-permute-start(f32[9,1,8,128]{3,2,0,1:T(8,128)} %bitcast.13), channel_id=1, source_target_pairs={{0,16},{16,32},{32,48},{48,64},{64,80},{80,96},{96,112},{112,128},... | collective-permute-start | bytes 110600 | tf_op jit(solution)/shard_map/ppermute | solution.py:20
  11.3 11.3 %collective-permute-start.1 = (f32[9,1,8,128]{3,2,0,1:T(8,128)}, f32[9,1,8,128]{3,2,0,1:T(8,128)}, u32[]{:S(2)}, u32[]{:S(2)}) collective-permute-start(f32[9,1,8,128]{3,2,0,1:T(8,128)} %bitcast.17), channel_id=1, source_target_pairs={{16,0},{32,16},{48,32},{64,48},{80,64},{96,80},{112,96},{128,112},... | collective-permute-start | bytes 110600 | tf_op jit(solution)/shard_map/ppermute | solution.py:21
  21.5 0.8 copy-start.29
  22.0 0.9 copy-start.19
  29.5 5.0 %copy-start.2 = (f32[1,1,4,27,1024]{4,2,3,1,0:T(4,128)S(1)}, f32[1,1,4,27,1024]{4,2,3,1,0:T(4,128)}, u32[]{:S(2)}) copy-start(f32[1,1,4,27,1024]{4,2,3,1,0:T(4,128)} %param.17) | copy-start | bytes 1327108
  34.5 13.0 %copy-start.26 = (f32[1,1,4,1024]{3,2,1,0:T(4,128)S(1)}, f32[1,1,4,1024]{3,2,1,0:T(4,128)}, u32[]{:S(2)}) copy-start(f32[1,1,4,1024]{3,2,1,0:T(4,128)} %param.18) | copy-start | bytes 49156
  49.7 2.5 %copy-start.11 = (f32[27,1024]{0,1:T(8,128)S(1)}, f32[27,1024]{0,1:T(8,128)}, u32[]{:S(2)}) copy-start(f32[27,1024]{0,1:T(8,128)} %copy.172) | copy-start | bytes 331780
  60.3 3.1 %copy-start.24 = (f32[27,27]{1,0:T(8,128)S(1)}, f32[27,27]{1,0:T(8,128)}, u32[]{:S(2)}) copy-start(f32[27,27]{1,0:T(8,128)} %param.21) | copy-start | bytes 8752
  66.5 3.3 %copy-start.31 = (f32[3,1,3,4,1,128]{5,4,3,2,1,0:T(1,128)S(1)}, f32[3,1,3,4,1,128]{5,4,3,2,1,0:T(1,128)}, u32[]{:S(2)}) copy-start(f32[3,1,3,4,1,128]{5,4,3,2,1,0:T(1,128)} %get-tuple-element.287) | copy-start | bytes 55300
  66.5 5.8 %copy-start.17 = (f32[3,1,3,4,8,128]{5,4,3,2,1,0:T(8,128)S(1)}, f32[3,1,3,4,8,128]{5,4,3,2,1,0:T(8,128)}, u32[]{:S(2)}) copy-start(f32[3,1,3,4,8,128]{5,4,3,2,1,0:T(8,128)} %get-tuple-element.283) | copy-start | bytes 442372
  66.5 12.9 %copy-start.15 = (f32[3,3,4,7,128]{4,3,2,1,0:T(8,128)S(1)}, f32[3,3,4,7,128]{4,3,2,1,0:T(8,128)}, u32[]{:S(2)}) copy-start(f32[3,3,4,7,128]{4,3,2,1,0:T(8,128)} %get-tuple-element.284) | copy-start | bytes 387076
  66.5 13.0 %copy-start.13 = (f32[3,3,4,7,128]{4,3,2,1,0:T(8,128)S(1)}, f32[3,3,4,7,128]{4,3,2,1,0:T(8,128)}, u32[]{:S(2)}) copy-start(f32[3,3,4,7,128]{4,3,2,1,0:T(8,128)} %get-tuple-element.285) | copy-start | bytes 387076
  66.5 12.9 %collective-permute-start.7 = (f32[9,4,1,128]{3,1,0,2:T(4,128)}, f32[9,4,1,128]{3,1,0,2:T(4,128)S(1)}, u32[]{:S(2)}, u32[]{:S(2)}) collective-permute-start(f32[9,4,1,128]{3,1,0,2:T(4,128)} %bitcast.53), channel_id=1, source_target_pairs={{1,0},{2,1},{3,2},{4,3},{5,4},{6,5},{7,6},{8,7},{9,8},{10,9},{11,1... | collective-permute-start | bytes 55304 | tf_op jit(solution)/shard_map/ppermute | solution.py:21
  68.7 11.0 %copy-start.22 = (f32[3,3,3,8,128]{4,3,2,1,0:T(8,128)S(1)}, f32[3,3,3,8,128]{4,3,2,1,0:T(8,128)}, u32[]{:S(2)}) copy-start(f32[3,3,3,8,128]{4,3,2,1,0:T(8,128)} %get-tuple-element.289) | copy-start | bytes 331780
  69.7 11.3 %copy-start.20 = (f32[3,3,3,8,128]{4,3,2,1,0:T(8,128)S(1)}, f32[3,3,3,8,128]{4,3,2,1,0:T(8,128)}, u32[]{:S(2)}) copy-start(f32[3,3,3,8,128]{4,3,2,1,0:T(8,128)} %get-tuple-element.288) | copy-start | bytes 331780
  69.8 9.7 %collective-permute-start.6 = (f32[9,4,1,128]{3,1,0,2:T(4,128)S(1)}, f32[9,4,1,128]{3,1,0,2:T(4,128)S(1)}, u32[]{:S(2)}, u32[]{:S(2)}) collective-permute-start(f32[9,4,1,128]{3,1,0,2:T(4,128)S(1)} %bitcast.490), channel_id=1, source_target_pairs={{0,1},{1,2},{2,3},{3,4},{4,5},{5,6},{6,7},{7,8},{8,9},{9,10},{10,1... | collective-permute-start | bytes 55304 | tf_op jit(solution)/shard_map/ppermute | solution.py:20
  72.4 7.3 %collective-permute-start.4 = (f32[9,1,8,128]{3,2,0,1:T(8,128)S(1)}, f32[9,1,8,128]{3,2,0,1:T(8,128)S(1)}, u32[]{:S(2)}, u32[]{:S(2)}) collective-permute-start(f32[9,1,8,128]{3,2,0,1:T(8,128)S(1)} %bitcast.480), channel_id=1, source_target_pairs={{0,16},{16,32},{32,48},{48,64},{64,80},{80,96},{96,112},{112,128},... | collective-permute-start | bytes 110600 | tf_op jit(solution)/shard_map/ppermute | solution.py:20
  74.3 6.8 %collective-permute-start.5 = (f32[9,1,8,128]{3,2,0,1:T(8,128)S(1)}, f32[9,1,8,128]{3,2,0,1:T(8,128)S(1)}, u32[]{:S(2)}, u32[]{:S(2)}) collective-permute-start(f32[9,1,8,128]{3,2,0,1:T(8,128)S(1)} %bitcast.478), channel_id=1, source_target_pairs={{16,0},{32,16},{48,32},{64,48},{80,64},{96,80},{112,96},{128,112},... | collective-permute-start | bytes 110600 | tf_op jit(solution)/shard_map/ppermute | solution.py:21
  81.1 5.0 %copy-start.7 = (f32[4096,27]{0,1:T(8,128)S(1)}, f32[4096,27]{0,1:T(8,128)}, u32[]{:S(2)}) copy-start(f32[4096,27]{0,1:T(8,128)} %fusion.65) | copy-start | bytes 1327108
  88.3 5.5 %copy-start.5 = (f32[4,27,1024]{2,0,1:T(4,128)S(1)}, f32[4,27,1024]{2,0,1:T(4,128)}, u32[]{:S(2)}) copy-start(f32[4,27,1024]{2,0,1:T(4,128)} %get-tuple-element.487) | copy-start | bytes 1327108
  93.8 13.1 %copy-start.3 = (f32[1,1,4,27,1024]{4,2,3,1,0:T(4,128)S(1)}, f32[1,1,4,27,1024]{4,2,3,1,0:T(4,128)}, u32[]{:S(2)}) copy-start(f32[1,1,4,27,1024]{4,2,3,1,0:T(4,128)} %param.17) | copy-start | bytes 1327108
  93.8 13.1 %copy-start.27 = (f32[1,1,4,1024]{3,2,1,0:T(4,128)S(1)}, f32[1,1,4,1024]{3,2,1,0:T(4,128)}, u32[]{:S(2)}) copy-start(f32[1,1,4,1024]{3,2,1,0:T(4,128)} %param.18) | copy-start | bytes 49156
  106.9 2.1 %copy-start.10 = (f32[27,4096]{1,0:T(8,128)S(1)}, f32[27,4096]{1,0:T(8,128)}, u32[]{:S(2)}) copy-start(f32[27,4096]{1,0:T(8,128)} %get-tuple-element.308) | copy-start | bytes 1327108
  109.1 2.5 %copy-start.12 = (f32[27,1024]{0,1:T(8,128)S(1)}, f32[27,1024]{0,1:T(8,128)}, u32[]{:S(2)}) copy-start(f32[27,1024]{0,1:T(8,128)} %copy.190) | copy-start | bytes 331780
  119.8 3.1 %copy-start.25 = (f32[27,27]{1,0:T(8,128)S(1)}, f32[27,27]{1,0:T(8,128)}, u32[]{:S(2)}) copy-start(f32[27,27]{1,0:T(8,128)} %param.21) | copy-start | bytes 8752
  126.0 3.3 %copy-start.32 = (f32[3,1,3,4,1,128]{5,4,3,2,1,0:T(1,128)S(1)}, f32[3,1,3,4,1,128]{5,4,3,2,1,0:T(1,128)}, u32[]{:S(2)}) copy-start(f32[3,1,3,4,1,128]{5,4,3,2,1,0:T(1,128)} %get-tuple-element.273) | copy-start | bytes 55300
  126.0 5.8 %copy-start.18 = (f32[3,1,3,4,8,128]{5,4,3,2,1,0:T(8,128)S(1)}, f32[3,1,3,4,8,128]{5,4,3,2,1,0:T(8,128)}, u32[]{:S(2)}) copy-start(f32[3,1,3,4,8,128]{5,4,3,2,1,0:T(8,128)} %get-tuple-element.269) | copy-start | bytes 442372
  126.0 12.9 %copy-start.16 = (f32[3,3,4,7,128]{4,3,2,1,0:T(8,128)S(1)}, f32[3,3,4,7,128]{4,3,2,1,0:T(8,128)}, u32[]{:S(2)}) copy-start(f32[3,3,4,7,128]{4,3,2,1,0:T(8,128)} %get-tuple-element.270) | copy-start | bytes 387076
  126.0 13.0 %copy-start.14 = (f32[3,3,4,7,128]{4,3,2,1,0:T(8,128)S(1)}, f32[3,3,4,7,128]{4,3,2,1,0:T(8,128)}, u32[]{:S(2)}) copy-start(f32[3,3,4,7,128]{4,3,2,1,0:T(8,128)} %get-tuple-element.271) | copy-start | bytes 387076
  126.0 12.9 %collective-permute-start.11 = (f32[9,4,1,128]{3,1,0,2:T(4,128)}, f32[9,4,1,128]{3,1,0,2:T(4,128)S(1)}, u32[]{:S(2)}, u32[]{:S(2)}) collective-permute-start(f32[9,4,1,128]{3,1,0,2:T(4,128)} %bitcast.78), channel_id=1, source_target_pairs={{1,0},{2,1},{3,2},{4,3},{5,4},{6,5},{7,6},{8,7},{9,8},{10,9},{11,1... | collective-permute-start | bytes 55304 | tf_op jit(solution)/shard_map/ppermute | solution.py:21
  128.2 11.0 %copy-start.23 = (f32[3,3,3,8,128]{4,3,2,1,0:T(8,128)S(1)}, f32[3,3,3,8,128]{4,3,2,1,0:T(8,128)}, u32[]{:S(2)}) copy-start(f32[3,3,3,8,128]{4,3,2,1,0:T(8,128)} %get-tuple-element.275) | copy-start | bytes 331780
  129.2 11.3 %copy-start.21 = (f32[3,3,3,8,128]{4,3,2,1,0:T(8,128)S(1)}, f32[3,3,3,8,128]{4,3,2,1,0:T(8,128)}, u32[]{:S(2)}) copy-start(f32[3,3,3,8,128]{4,3,2,1,0:T(8,128)} %get-tuple-element.274) | copy-start | bytes 331780
  129.2 9.7 %collective-permute-start.10 = (f32[9,4,1,128]{3,1,0,2:T(4,128)S(1)}, f32[9,4,1,128]{3,1,0,2:T(4,128)S(1)}, u32[]{:S(2)}, u32[]{:S(2)}) collective-permute-start(f32[9,4,1,128]{3,1,0,2:T(4,128)S(1)} %bitcast.491), channel_id=1, source_target_pairs={{0,1},{1,2},{2,3},{3,4},{4,5},{5,6},{6,7},{7,8},{8,9},{9,10},{10,1... | collective-permute-start | bytes 55304 | tf_op jit(solution)/shard_map/ppermute | solution.py:20
  131.8 7.3 %collective-permute-start.8 = (f32[9,1,8,128]{3,2,0,1:T(8,128)S(1)}, f32[9,1,8,128]{3,2,0,1:T(8,128)S(1)}, u32[]{:S(2)}, u32[]{:S(2)}) collective-permute-start(f32[9,1,8,128]{3,2,0,1:T(8,128)S(1)} %bitcast.481), channel_id=1, source_target_pairs={{0,16},{16,32},{32,48},{48,64},{64,80},{80,96},{96,112},{112,128},... | collective-permute-start | bytes 110600 | tf_op jit(solution)/shard_map/ppermute | solution.py:20
  133.8 6.8 %collective-permute-start.9 = (f32[9,1,8,128]{3,2,0,1:T(8,128)S(1)}, f32[9,1,8,128]{3,2,0,1:T(8,128)S(1)}, u32[]{:S(2)}, u32[]{:S(2)}) collective-permute-start(f32[9,1,8,128]{3,2,0,1:T(8,128)S(1)} %bitcast.479), channel_id=1, source_target_pairs={{16,0},{32,16},{48,32},{64,48},{80,64},{96,80},{112,96},{128,112},... | collective-permute-start | bytes 110600 | tf_op jit(solution)/shard_map/ppermute | solution.py:21
  140.6 5.0 %copy-start.8 = (f32[4096,27]{0,1:T(8,128)S(1)}, f32[4096,27]{0,1:T(8,128)}, u32[]{:S(2)}) copy-start(f32[4096,27]{0,1:T(8,128)} %fusion.66) | copy-start | bytes 1327108
  147.7 5.5 %copy-start.6 = (f32[4,27,1024]{2,0,1:T(4,128)S(1)}, f32[4,27,1024]{2,0,1:T(4,128)}, u32[]{:S(2)}) copy-start(f32[4,27,1024]{2,0,1:T(4,128)} %get-tuple-element.520) | copy-start | bytes 1327108
  153.3 13.0 %copy-start.4 = (f32[1,1,4,27,1024]{4,2,3,1,0:T(4,128)S(1)}, f32[1,1,4,27,1024]{4,2,3,1,0:T(4,128)}, u32[]{:S(2)}) copy-start(f32[1,1,4,27,1024]{4,2,3,1,0:T(4,128)} %param.17) | copy-start | bytes 1327108
  153.3 13.0 %copy-start.28 = (f32[1,1,4,1024]{3,2,1,0:T(4,128)S(1)}, f32[1,1,4,1024]{3,2,1,0:T(4,128)}, u32[]{:S(2)}) copy-start(f32[1,1,4,1024]{3,2,1,0:T(4,128)} %param.18) | copy-start | bytes 49156
  166.3 1.3 copy-start.9
where the time goes:
time: 180 us; the launch traced here: 179 us
  local copies, waits for them, and re-layouts  55.8 us (31%)
  other arithmetic  49.8 us (28%)
  starting transfers between devices  35.9 us (20%)
  matrix products  30.4 us (17%)
  between operations  2.57 us (1%)
  waiting for transfers between devices  2.55 us (1%)
  loops' own time  2.06 us (1%)
    ppermute x6, starting transfers between devices, extended(): after = lax.ppermute(leading, axis, down)  22.5 us
    scatter x3, other arithmetic, place(): flat_field.at[:, zone_ids].set(jnp.where(live[None], closure, current))  22.3 us
    dot_general x96, matrix products, sweep_rates(): jnp.einsum('mpq,mqs->mps', mat_matrix, iterate, precision=highest)  19.2 us
    lt x24, other arithmetic, advance(): keep = first + jnp.arange(width, dtype=jnp.int32) < live_count  15.7 us
    ppermute x6, starting transfers between devices, extended(): before = lax.ppermute(last, axis, up)  13.4 us
    gather x3, local copies, waits for them, and re-layouts, on_device(): resid = jnp.take(rate, zone_ids, axis=1)  12.4 us
    concatenate x3, local copies, waits for them, and re-layouts, jump_rates(): stacked = jnp.concatenate([jump.reshape(9, -1) for jump in jumps], axis=0)  9.79 us
    dot_general x3, matrix products, jump_rates(): jnp.dot(volume, field.reshape(27, -1), precision=highest)  7.49 us
  transfers between devices with their start and end apart: 12, of which 2 were waited for; matrix products, arithmetic and copies ran while one was open for 6% of the time, Pallas kernels for 0%

commit v1 on v0

v1 whole, which is shorter than its diff:
```python
import numpy as np
import jax
import jax.numpy as jnp
from jax import lax
from jax.experimental import pallas as pl
from jax.experimental.pallas import tpu as pltpu
from jax.sharding import PartitionSpec as P

F32 = jnp.float32
BF16 = jnp.bfloat16
CX, CY, CZ = 4, 8, 128
ROWS = CX * CY
ZONES = ROWS * CZ
SLOTS = 1024
GROUP = 256
GROUPS = ZONES // GROUP
HIGHEST = lax.Precision.HIGHEST


def face_dofs(face, own):
    axis, high = divmod(face, 2)
    at = (2 if high else 0) if own else (0 if high else 2)
    dofs = []
    for p in range(3):
        for q in range(3):
            abc = [p, q]
            abc.insert(axis, at)
            dofs.append(abc[0] * 9 + abc[1] * 3 + abc[2])
    return dofs


def selections():
    sel = np.zeros((64, 7 * 128 + 4 * 64), np.float32)
    for face in range(6):
        for q in range(9):
            row = 9 * face + q
            for copy in range(4):
                sel[row, copy * 32 + face_dofs(face, True)[q]] -= 1.0
                sel[row, (face + 1) * 128 + copy * 32 + face_dofs(face, False)[q]] += 1.0
                if face < 4:
                    sel[row, 7 * 128 + face * 64 + copy * 16 + q] += 1.0
    return sel


def halves(x):
    hi = x.astype(BF16)
    lo = (x - hi.astype(F32)).astype(BF16)
    return hi, lo


def stack_right(x):
    hi, lo = halves(x)
    return jnp.concatenate([hi, lo, hi, lo], axis=0)


def stack_left(x, half):
    hi = x.astype(BF16).astype(F32)
    lane = lax.broadcasted_iota(jnp.int32, x.shape, 1)
    return jnp.where(lane < half, hi, x - hi).astype(BF16)


def dot(a, b):
    return jnp.dot(a, b, preferred_element_type=F32)


def block(r):
    return slice(r * CZ, (r + 1) * CZ)


def interior(v_ref, wg_ref, g_ref, out_ref):
    for x in range(CX):
        cols = slice(x * 1024, (x + 1) * 1024)
        g_ref[:, cols] = dot(wg_ref[...], stack_right(v_ref[:, cols]))
    lane = lax.broadcasted_iota(jnp.int32, (32, CZ), 1)
    for x in range(CX):
        for y in range(CY):
            r = x * CY + y
            total = g_ref[0:32, block(r)]
            if x > 0:
                total += g_ref[32:64, block(r - CY)]
            if x < CX - 1:
                total += g_ref[64:96, block(r + CY)]
            if y > 0:
                total += g_ref[96:128, block(r - 1)]
            if y < CY - 1:
                total += g_ref[128:160, block(r + 1)]
            below = pltpu.roll(g_ref[160:192, block(r)], 1, 1)
            above = pltpu.roll(g_ref[192:224, block(r)], CZ - 1, 1)
            total += jnp.where(lane == 0, 0.0, below)
            total += jnp.where(lane == CZ - 1, 0.0, above)
            out_ref[:, block(r)] = total


def lane_hot(idx):
    place = lax.broadcasted_iota(jnp.int32, (GROUP, SLOTS), 0)
    return jnp.where(place == (idx & (GROUP - 1)), 1.0, 0.0).astype(BF16)


def to_slots(r_ref, hot, idx):
    total = jnp.zeros((32, SLOTS), F32)
    group = lax.shift_right_logical(idx, 8)
    for g in range(GROUPS):
        hi, lo = halves(r_ref[:, g * GROUP:(g + 1) * GROUP])
        both = dot(jnp.concatenate([hi, lo], axis=0), hot)
        total = jnp.where(group == g, both[0:32] + both[32:64], total)
    return total


def first_kernel(state_ref, v_ref, xlo_ref, xhi_ref, ylo_ref, yhi_ref):
    for q in range(9):
        xlo_ref[q * 8:q * 8 + 8, :] = state_ref[q * 32:q * 32 + 8, :]
        xhi_ref[q * 8:q * 8 + 8, :] = state_ref[(18 + q) * 32 + 24:(18 + q) * 32 + 32, :]
        low, high = face_dofs(2, True)[q], face_dofs(3, True)[q]
        ylo_ref[q * 4:q * 4 + 4, :] = state_ref[pl.ds(low * 32, 4, stride=8), :]
        yhi_ref[q * 4:q * 4 + 4, :] = state_ref[pl.ds(high * 32 + 7, 4, stride=8), :]
    v_ref[24:32, :] = jnp.zeros((8, ZONES), F32)
    for r in range(ROWS):
        v_ref[0:27, block(r)] = state_ref[pl.ds(r, 27, stride=32), :]


def mixed_kernel(
    count_ref, v_ref, w_ref, frac_ref, idx_ref, vol_ref, face_ref, mat_ref, sel_ref,
    int_ref, u_ref, c2_ref, c3_ref, fm_ref, wg_ref, fh_ref, pp_ref, b3_ref,
    g_ref, small_ref, diag_ref, wpad_ref, c_ref,
):
    small_ref[...] = jnp.zeros((32, 128), F32)
    small_ref[0:27, 0:54] = face_ref[...]
    f_hi, f_lo = halves(small_ref[:, 0:64])
    laid = dot(f_hi, sel_ref[...]) + dot(f_lo, sel_ref[...])
    small_ref[...] = jnp.zeros((32, 128), F32)
    small_ref[0:27, 0:27] = vol_ref[...]
    vol = small_ref[...]
    vol4 = vol + pltpu.roll(vol, 32, 1)
    vol4 = vol4 + pltpu.roll(vol4, 64, 1)
    wg_ref[0:32, :] = stack_left(laid[:, 0:128] + vol4, 64)
    for k in range(1, 7):
        wg_ref[32 * k:32 * k + 32, :] = stack_left(laid[:, 128 * k:128 * k + 128], 64)
    for k in range(4):
        first = 7 * 128 + 64 * k
        fh_ref[32 * k:32 * k + 32, :] = stack_left(laid[:, first:first + 64], 32)
    interior(v_ref, wg_ref, g_ref, int_ref)

    for m in range(4):
        small_ref[0:27, 0:27] = mat_ref[m]
        small = small_ref[...]
        diag_ref[32 * m:32 * m + 32, :] = pltpu.roll(small, 32 * m, 1) if m else small
    m1 = diag_ref[...]
    row = lax.broadcasted_iota(jnp.int32, (128, 128), 0)
    column = lax.broadcasted_iota(jnp.int32, (128, 128), 1)
    eye = jnp.where(row == column, 1.0, 0.0)
    m2 = jnp.dot(m1, m1, precision=HIGHEST)
    p1 = eye + m1 + m2 + jnp.dot(m1 + m2, m2, precision=HIGHEST)
    p2 = jnp.dot(p1, p1, precision=HIGHEST)
    p3 = jnp.dot(p2, p1, precision=HIGHEST)
    q2 = 0.75 * eye + 0.25 * p2
    q3 = (1.0 / 3.0) * eye + 0.5 * p1 + (1.0 / 6.0) * p3

    def stacked(matrix, m):
        rows = matrix[32 * m:32 * m + 32, :]
        for shift in (32, 64):
            rows = rows + pltpu.roll(rows, shift, 1)
        return stack_left(rows, 64)

    for m in range(4):
        pp_ref[32 * m:32 * m + 32, :] = stacked(p1, m)
        pp_ref[128 + 32 * m:128 + 32 * m + 32, :] = stacked(p2, m)

    idx = idx_ref[...]
    slot = lax.broadcasted_iota(jnp.int32, (1, SLOTS), 1)
    live = slot < count_ref[0, 0]
    frac = frac_ref[...]
    c_ref[...] = jnp.zeros((112, SLOTS), F32)
    wpad_ref[...] = jnp.zeros((32, SLOTS), F32)
    sums = [0.0, 0.0, 0.0]
    for m in range(4):
        wpad_ref[0:27, :] = w_ref[m]
        left = jnp.concatenate([stacked(p1, m), stacked(q2, m), stacked(q3, m)], axis=0)
        values = dot(left, stack_right(wpad_ref[...]))
        for k in range(3):
            sums[k] = sums[k] + frac[m:m + 1, :] * values[32 * k:32 * k + 32]
        b3_ref[m] = values[64:96]
    for k in range(3):
        c_ref[32 * k:32 * k + 32, :] = jnp.where(live, sums[k], 0.0)
    c_ref[96:100, :] = jnp.where(live, frac, 0.0)
    c_ref[100:101, :] = jnp.where(live, 1.0, 0.0)

    hot = lane_hot(idx)
    group = lax.shift_right_logical(idx, 8)
    hi, lo = halves(c_ref[...])
    both = jnp.concatenate([hi, lo], axis=0)
    for g in range(GROUPS):
        cols = slice(g * GROUP, (g + 1) * GROUP)
        here = jnp.where(group == g, 1.0, 0.0).astype(BF16)
        dense = lax.dot_general(
            both * here, hot, (((1,), (1,)), ((), ())), preferred_element_type=F32
        )
        dense = dense[0:112] + dense[112:224]
        u_ref[:, cols] = jnp.where(dense[100:101] > 0.5, dense[0:32], v_ref[:, cols])
        c2_ref[:, cols] = dense[32:64]
        c3_ref[:, cols] = dense[64:96]
        fm_ref[:, cols] = dense[96:104]


def halo_add(int_ref, fh_ref, xlo_ref, xhi_ref, ylo_ref, yhi_ref, pad_ref, rate_ref):
    pad_ref[...] = jnp.zeros((16, 3072), F32)
    for y in range(CY):
        pad_ref[0:9, block(y)] = xlo_ref[pl.ds(y, 9, stride=8), :]
        pad_ref[0:9, block(CY + y)] = xhi_ref[pl.ds(y, 9, stride=8), :]
    for x in range(CX):
        pad_ref[0:9, block(16 + x)] = ylo_ref[pl.ds(x, 9, stride=4), :]
        pad_ref[0:9, block(20 + x)] = yhi_ref[pl.ds(x, 9, stride=4), :]
    x_low = dot(fh_ref[0:32, :], stack_right(pad_ref[:, 0:1024]))
    x_high = dot(fh_ref[32:64, :], stack_right(pad_ref[:, 1024:2048]))
    y_low = dot(fh_ref[64:96, :], stack_right(pad_ref[:, 2048:2560]))
    y_high = dot(fh_ref[96:128, :], stack_right(pad_ref[:, 2560:3072]))
    for x in range(CX):
        for y in range(CY):
            r = x * CY + y
            total = int_ref[:, block(r)]
            if x == 0:
                total += x_low[:, block(y)]
            if x == CX - 1:
                total += x_high[:, block(y)]
            if y == 0:
                total += y_low[:, block(x)]
            if y == CY - 1:
                total += y_high[:, block(x)]
            rate_ref[:, block(r)] = total


def step_kernel(
    part, int_ref, u_ref, fh_ref, xl_ref, xh_ref, yl_ref, yh_ref,
    v_ref, rate_ref, xlo_ref, xhi_ref, ylo_ref, yhi_ref, pad_ref,
):
    halo_add(int_ref, fh_ref, xl_ref, xh_ref, yl_ref, yh_ref, pad_ref, rate_ref)
    v_ref[...] = u_ref[...] + part * rate_ref[...]
    for y in range(CY):
        xlo_ref[pl.ds(y, 9, stride=8), :] = v_ref[0:9, block(y)]
        xhi_ref[pl.ds(y, 9, stride=8), :] = v_ref[18:27, block(24 + y)]
    for x in range(CX):
        for a in range(3):
            ylo_ref[pl.ds(12 * a + x, 3, stride=4), :] = v_ref[9 * a:9 * a + 3, block(8 * x)]
            yhi_ref[pl.ds(12 * a + x, 3, stride=4), :] = v_ref[9 * a + 6:9 * a + 9, block(8 * x + 7)]


def between_one(
    v0_ref, v1_ref, r_ref, c2_ref, c3_ref, fm_ref, idx_ref, wg_ref, pp_ref, b3_ref,
    int_ref, u_ref, c3_out, b3_out, g_ref,
):
    interior(v1_ref, wg_ref, g_ref, int_ref)
    for x in range(CX):
        cols = slice(x * 1024, (x + 1) * 1024)
        q = dot(pp_ref[...], stack_right(r_ref[:, cols]))
        f = fm_ref[:, cols]
        s1 = sum(f[m:m + 1] * q[32 * m:32 * m + 32] for m in range(4))
        s2 = sum(f[m:m + 1] * q[128 + 32 * m:160 + 32 * m] for m in range(4))
        bulk = 0.75 * v0_ref[:, cols] + 0.25 * v1_ref[:, cols]
        u_ref[:, cols] = jnp.where(f[4:5] > 0.5, c2_ref[:, cols] + 0.25 * s1, bulk)
        c3_out[:, cols] = c3_ref[:, cols] + (1.0 / 6.0) * s2
    idx = idx_ref[...]
    at = stack_right(to_slots(r_ref, lane_hot(idx), idx))
    for m in range(4):
        b3_out[m] = b3_ref[m] + (1.0 / 6.0) * dot(pp_ref[128 + 32 * m:160 + 32 * m, :], at)


def between_two(
    v0_ref, v2_ref, r_ref, c3_ref, fm_ref, idx_ref, wg_ref, pp_ref, b3_ref,
    int_ref, u_ref, b3_out, g_ref,
):
    interior(v2_ref, wg_ref, g_ref, int_ref)
    for x in range(CX):
        cols = slice(x * 1024, (x + 1) * 1024)
        q = dot(pp_ref[0:128, :], stack_right(r_ref[:, cols]))
        f = fm_ref[:, cols]
        s1 = sum(f[m:m + 1] * q[32 * m:32 * m + 32] for m in range(4))
        bulk = (1.0 / 3.0) * v0_ref[:, cols] + (2.0 / 3.0) * v2_ref[:, cols]
        u_ref[:, cols] = jnp.where(f[4:5] > 0.5, c3_ref[:, cols] + (1.0 / 6.0) * s1, bulk)
    idx = idx_ref[...]
    at = stack_right(to_slots(r_ref, lane_hot(idx), idx))
    for m in range(4):
        b3_out[m] = b3_ref[m] + (1.0 / 6.0) * dot(pp_ref[32 * m:32 * m + 32, :], at)


def last_kernel(
    count_ref, int_ref, u_ref, fh_ref, xl_ref, xh_ref, yl_ref, yh_ref, idx_ref, b3_ref, w_ref,
    field_ref, out_ref, pad_ref, rate_ref,
):
    halo_add(int_ref, fh_ref, xl_ref, xh_ref, yl_ref, yh_ref, pad_ref, rate_ref)
    for r in range(ROWS):
        value = u_ref[0:27, block(r)] + (2.0 / 3.0) * rate_ref[0:27, block(r)]
        field_ref[pl.ds(r, 27, stride=32), :] = value
    idx = idx_ref[...]
    at = (2.0 / 3.0) * to_slots(rate_ref, lane_hot(idx), idx)
    live = lax.broadcasted_iota(jnp.int32, (1, SLOTS), 1) < count_ref[0, 0]
    for m in range(4):
        out_ref[m] = jnp.where(live, b3_ref[m, 0:27, :] + at[0:27], w_ref[m])


VMEM = pl.BlockSpec(memory_space=pltpu.VMEM)
SMEM = pl.BlockSpec(memory_space=pltpu.SMEM)
DENSE = jax.ShapeDtypeStruct((32, ZONES), F32)
FACES = [jax.ShapeDtypeStruct((72, 128), F32)] * 2 + [jax.ShapeDtypeStruct((36, 128), F32)] * 2
SLOT3 = jax.ShapeDtypeStruct((4, 32, SLOTS), F32)


def call(kernel, outs, args, scratch=(), smem=0, flops=0):
    specs = [SMEM] * smem + [VMEM] * (len(args) - smem)
    moved = 4 * sum(int(np.prod(a.shape)) for a in list(args) + list(outs))
    return pl.pallas_call(
        kernel,
        out_shape=outs,
        in_specs=specs,
        out_specs=[VMEM] * len(outs),
        scratch_shapes=list(scratch),
        compiler_params=pltpu.CompilerParams(vmem_limit_bytes=48 * 1024 * 1024),
        cost_estimate=pl.CostEstimate(flops=flops, bytes_accessed=moved, transcendentals=0),
    )(*args)


def exchange(faces):
    x_low, x_high, y_low, y_high = faces

    def neighbours(axis, low, high):
        up = [(i, i + 1) for i in range(lax.axis_size(axis) - 1)]
        down = [(j, i) for i, j in up]
        return lax.ppermute(high, axis, up), lax.ppermute(low, axis, down)

    return (*neighbours("gx", x_low, x_high), *neighbours("yz", y_low, y_high))


def on_device(
    state, mix_weights, mix_frac, mix_index, mix_count, vol_matrix, face_matrix, mat_matrix
):
    flat = state.reshape(27 * ROWS, CZ)
    weights = mix_weights.reshape(4, 27, SLOTS)
    frac = mix_frac.reshape(4, SLOTS)
    idx = mix_index.reshape(1, SLOTS)
    count = mix_count.reshape(1, 1)
    sel = jnp.asarray(selections(), BF16)
    g_space = pltpu.VMEM((224, ZONES), F32)
    pad = pltpu.VMEM((16, 3072), F32)

    v0, *faces = call(first_kernel, [DENSE] + FACES, [flat])
    halo = exchange(faces)
    bf = lambda rows, lanes: jax.ShapeDtypeStruct((rows, lanes), BF16)
    fm_shape = jax.ShapeDtypeStruct((8, ZONES), F32)
    inner, u, c2, c3, fm, wg, fh, pp, b3 = call(
        mixed_kernel,
        [DENSE, DENSE, DENSE, DENSE, fm_shape, bf(224, 128), bf(128, 64), bf(256, 128), SLOT3],
        [count, v0, weights, frac, idx, vol_matrix, face_matrix, mat_matrix, sel],
        [g_space, pltpu.VMEM((32, 128), F32), pltpu.VMEM((128, 128), F32),
         pltpu.VMEM((32, SLOTS), F32), pltpu.VMEM((112, SLOTS), F32)],
        smem=1, flops=4 * 10**9,
    )

    def step(part, inner, u, halo):
        def kernel(*refs):
            step_kernel(part, *refs)
        v, rate, *faces = call(kernel, [DENSE, DENSE] + FACES, [inner, u, fh, *halo], [pad])
        return v, rate, exchange(faces)

    v1, r0, halo = step(1.0, inner, u, halo)
    inner, u, c3, b3 = call(
        between_one, [DENSE, DENSE, DENSE, SLOT3],
        [v0, v1, r0, c2, c3, fm, idx, wg, pp, b3], [g_space], flops=2 * 10**9,
    )
    v2, r1, halo = step(0.25, inner, u, halo)
    inner, u, b3 = call(
        between_two, [DENSE, DENSE, SLOT3],
        [v0, v2, r1, c3, fm, idx, wg, pp, b3], [g_space], flops=2 * 10**9,
    )
    field, out = call(
        last_kernel,
        [jax.ShapeDtypeStruct((27 * ROWS, CZ), F32), jax.ShapeDtypeStruct((4, 27, SLOTS), F32)],
        [count, inner, u, fh, *halo, idx, b3, weights],
        [pad, pltpu.VMEM((32, ZONES), F32)], smem=1,
    )
    return field.reshape(state.shape), out.reshape(mix_weights.shape)


def solution(mesh):
    placed = (
        P(None, "gx", "yz", None),
        P("gx", "yz", None, None, None),
        P("gx", "yz", None, None),
        P("gx", "yz", None),
        P("gx", "yz"),
        P(),
        P(),
        P(),
    )
    return jax.shard_map(
        on_device,
        mesh=mesh,
        in_specs=placed,
        out_specs=(P(None, "gx", "yz", None), P("gx", "yz", None, None, None)),
        check_vma=False,
    )
```

time: 180 us -> 64 us (0.36)
  the two profiles are of different devices: /device:TPU:354 before, /device:TPU:199 now
where the time goes in v1:
time: 64 us; the launch traced here: 63.5 us
  starting transfers between devices  44.5 us (70%)
  Pallas kernels  13.5 us (21%)
  local copies, waits for them, and re-layouts  3.86 us (6%)
  between operations  1.55 us (2%)
    ppermute x12, starting transfers between devices, neighbours(): return (lax.ppermute(high, axis, up), lax.ppermute(low, axis, down))  44.5 us
    pallas_call x7, Pallas kernels, call(): pl.pallas_call(kernel, out_shape=outs, in_specs=specs, out_specs=[VMEM] *...  13.5 us
    unnamed x17, local copies, waits for them, and re-layouts  3.86 us
  transfers between devices with their start and end apart: 12, of which 0 were waited for; matrix products, arithmetic and copies ran while one was open for 2% of the time, Pallas kernels for 17%

profile of v1, /device:TPU:199, one launch (start us, length us, event | category | flops | bytes accessed | tf_op | source)
XLA Modules:
  0.0 63.5 jit_solution(17569247958055829863)
XLA Ops:
  0.6 0.0 copy-start
  0.6 1.0 %copy-done = f32[27,4,8,128]{3,2,1,0:T(8,128)S(1)} copy-done((f32[27,4,8,128]{3,2,1,0:T(8,128)S(1)}, f32[27,4,8,128]{3,2,1,0:T(8,128)}, u32[]{:S(2)}) %copy-start) | copy-done | bytes 442392
  1.6 0.0 copy-start.6
  1.6 0.3 shard_map.104
  1.9 5.8 %collective-permute-start.2 = (f32[36,128]{1,0:T(8,128)S(1)}, f32[36,128]{1,0:T(8,128)S(1)}, u32[]{:S(2)}, u32[]{:S(2)}) collective-permute-start(f32[36,128]{1,0:T(8,128)S(1)} %get-tuple-element.43), channel_id=1, source_target_pairs={{0,1},{1,2},{2,3},{3,4},{4,5},{5,6},{6,7},{7,8},{8,9},{9,10},{10,1... | collective-permute-start | bytes 55304 | tf_op jit(solution)/shard_map/ppermute | solution.py:326
  7.7 1.9 %collective-permute-start.3 = (f32[36,128]{1,0:T(8,128)S(1)}, f32[36,128]{1,0:T(8,128)S(1)}, u32[]{:S(2)}, u32[]{:S(2)}) collective-permute-start(f32[36,128]{1,0:T(8,128)S(1)} %get-tuple-element.44), channel_id=1, source_target_pairs={{1,0},{2,1},{3,2},{4,3},{5,4},{6,5},{7,6},{8,7},{9,8},{10,9},{11,1... | collective-permute-start | bytes 55304 | tf_op jit(solution)/shard_map/ppermute | solution.py:326
  9.6 3.2 %collective-permute-start = (f32[72,128]{1,0:T(8,128)S(1)}, f32[72,128]{1,0:T(8,128)S(1)}, u32[]{:S(2)}, u32[]{:S(2)}) collective-permute-start(f32[72,128]{1,0:T(8,128)S(1)} %get-tuple-element.41), channel_id=1, source_target_pairs={{0,16},{16,32},{32,48},{48,64},{64,80},{80,96},{96,112},{112,128},... | collective-permute-start | bytes 110600 | tf_op jit(solution)/shard_map/ppermute | solution.py:326
  12.8 4.2 %collective-permute-start.1 = (f32[72,128]{1,0:T(8,128)S(1)}, f32[72,128]{1,0:T(8,128)S(1)}, u32[]{:S(2)}, u32[]{:S(2)}) collective-permute-start(f32[72,128]{1,0:T(8,128)S(1)} %get-tuple-element.42), channel_id=1, source_target_pairs={{16,0},{32,16},{48,32},{64,48},{80,64},{96,80},{112,96},{128,112},... | collective-permute-start | bytes 110600 | tf_op jit(solution)/shard_map/ppermute | solution.py:326
  17.7 0.8 %copy.12.mat_ref = f32[4,27,27]{2,1,0:T(8,128)S(1)} copy(f32[4,27,27]{2,0,1:T(4,128)} %param.16) | data formatting | bytes 23328 | tf_op args[7]
  18.5 0.0 copy-done.6
  18.5 0.0 copy-start.2
  18.5 0.0 copy-start.3
  18.5 0.0 copy-start.4
  18.5 0.0 copy-start.5
  18.6 0.3 copy.15
  18.8 0.0 copy-start.1
  18.8 0.4 copy-done.2
  19.2 0.0 copy-done.3
  19.3 0.0 copy-done.4
  19.3 0.2 copy-done.5
  19.5 0.1 copy-done.1
  19.5 4.8 %shard_map.105 = (f32[32,4096]{1,0:T(8,128)S(1)}, f32[32,4096]{1,0:T(8,128)S(1)}, f32[32,4096]{1,0:T(8,128)S(1)}, f32[32,4096]{1,0:T(8,128)S(1)}, f32[8,4096]{1,...) custom-call(s32[1,1]{1,0:T(1,128)S(6)} %copy.16.count_ref, ...), custom_call_target="tpu_custom_call" | custom-call | flops 4000000000 | bytes 4333504 | tf_op jit(solution)/shard_map/pallas_call | solution.py:309
  24.3 0.0 collective-permute-done.2.refs_5_
  24.3 0.0 collective-permute-done.3.refs_6_
  24.3 0.0 collective-permute-done.refs_3_
  24.3 0.0 collective-permute-done.1.refs_4_
  24.4 0.3 shard_map.106
  24.6 5.4 %collective-permute-start.6 = (f32[36,128]{1,0:T(8,128)S(1)}, f32[36,128]{1,0:T(8,128)S(1)}, u32[]{:S(2)}, u32[]{:S(2)}) collective-permute-start(f32[36,128]{1,0:T(8,128)S(1)} %get-tuple-element.57), channel_id=1, source_target_pairs={{0,1},{1,2},{2,3},{3,4},{4,5},{5,6},{6,7},{7,8},{8,9},{9,10},{10,1... | collective-permute-start | bytes 55304 | tf_op jit(solution)/shard_map/ppermute | solution.py:326
  30.1 1.9 %collective-permute-start.7 = (f32[36,128]{1,0:T(8,128)S(1)}, f32[36,128]{1,0:T(8,128)S(1)}, u32[]{:S(2)}, u32[]{:S(2)}) collective-permute-start(f32[36,128]{1,0:T(8,128)S(1)} %get-tuple-element.58), channel_id=1, source_target_pairs={{1,0},{2,1},{3,2},{4,3},{5,4},{6,5},{7,6},{8,7},{9,8},{10,9},{11,1... | collective-permute-start | bytes 55304 | tf_op jit(solution)/shard_map/ppermute | solution.py:326
  32.0 1.9 %collective-permute-start.4 = (f32[72,128]{1,0:T(8,128)S(1)}, f32[72,128]{1,0:T(8,128)S(1)}, u32[]{:S(2)}, u32[]{:S(2)}) collective-permute-start(f32[72,128]{1,0:T(8,128)S(1)} %get-tuple-element.55), channel_id=1, source_target_pairs={{0,16},{16,32},{32,48},{48,64},{64,80},{80,96},{96,112},{112,128},... | collective-permute-start | bytes 110600 | tf_op jit(solution)/shard_map/ppermute | solution.py:326
  33.9 5.5 %collective-permute-start.5 = (f32[72,128]{1,0:T(8,128)S(1)}, f32[72,128]{1,0:T(8,128)S(1)}, u32[]{:S(2)}, u32[]{:S(2)}) collective-permute-start(f32[72,128]{1,0:T(8,128)S(1)} %get-tuple-element.56), channel_id=1, source_target_pairs={{16,0},{32,16},{48,32},{64,48},{80,64},{96,80},{112,96},{128,112},... | collective-permute-start | bytes 110600 | tf_op jit(solution)/shard_map/ppermute | solution.py:326
  39.4 3.0 %shard_map.107 = (f32[32,4096]{1,0:T(8,128)S(1)}, f32[32,4096]{1,0:T(8,128)S(1)}, f32[32,4096]{1,0:T(8,128)S(1)}, f32[4,32,1024]{2,1,0:T(8,128)S(1)}) custom-call(f32[32,4096]{1,0:T(8,128)S(1)} %get-tuple-element.37.v_ref.v0_ref, f32[32,4096]{1,0:T(8,128)S(1)} %get-tuple-element.45.v1_ref, f32[32,4096]{1,0:T(8,128)S(1)} %get-tuple-element.46.r_ref, ...), custom_call_target="tpu_custom_call" | custom-call | flops 2000000000 | bytes 5623808 | tf_op jit(solution)/shard_map/pallas_call | solution.py:309
  42.4 0.0 collective-permute-done.6.refs_5_
  42.4 0.0 collective-permute-done.7.refs_6_
  42.5 0.0 collective-permute-done.4.refs_3_
  42.5 0.0 collective-permute-done.5.refs_4_
  42.5 0.2 shard_map.108
  42.7 5.4 %collective-permute-start.10 = (f32[36,128]{1,0:T(8,128)S(1)}, f32[36,128]{1,0:T(8,128)S(1)}, u32[]{:S(2)}, u32[]{:S(2)}) collective-permute-start(f32[36,128]{1,0:T(8,128)S(1)} %get-tuple-element.67), channel_id=1, source_target_pairs={{0,1},{1,2},{2,3},{3,4},{4,5},{5,6},{6,7},{7,8},{8,9},{9,10},{10,1... | collective-permute-start | bytes 55304 | tf_op jit(solution)/shard_map/ppermute | solution.py:326
  48.2 1.9 %collective-permute-start.11 = (f32[36,128]{1,0:T(8,128)S(1)}, f32[36,128]{1,0:T(8,128)S(1)}, u32[]{:S(2)}, u32[]{:S(2)}) collective-permute-start(f32[36,128]{1,0:T(8,128)S(1)} %get-tuple-element.68), channel_id=1, source_target_pairs={{1,0},{2,1},{3,2},{4,3},{5,4},{6,5},{7,6},{8,7},{9,8},{10,9},{11,1... | collective-permute-start | bytes 55304 | tf_op jit(solution)/shard_map/ppermute | solution.py:326
  50.1 1.9 %collective-permute-start.8 = (f32[72,128]{1,0:T(8,128)S(1)}, f32[72,128]{1,0:T(8,128)S(1)}, u32[]{:S(2)}, u32[]{:S(2)}) collective-permute-start(f32[72,128]{1,0:T(8,128)S(1)} %get-tuple-element.65), channel_id=1, source_target_pairs={{0,16},{16,32},{32,48},{48,64},{64,80},{80,96},{96,112},{112,128},... | collective-permute-start | bytes 110600 | tf_op jit(solution)/shard_map/ppermute | solution.py:326
  52.0 5.5 %collective-permute-start.9 = (f32[72,128]{1,0:T(8,128)S(1)}, f32[72,128]{1,0:T(8,128)S(1)}, u32[]{:S(2)}, u32[]{:S(2)}) collective-permute-start(f32[72,128]{1,0:T(8,128)S(1)} %get-tuple-element.66), channel_id=1, source_target_pairs={{16,0},{32,16},{48,32},{64,48},{80,64},{96,80},{112,96},{128,112},... | collective-permute-start | bytes 110600 | tf_op jit(solution)/shard_map/ppermute | solution.py:326
  57.5 2.8 %shard_map.109 = (f32[32,4096]{1,0:T(8,128)S(1)}, f32[32,4096]{1,0:T(8,128)S(1)}, f32[4,32,1024]{2,1,0:T(8,128)S(1)}) custom-call(f32[32,4096]{1,0:T(8,128)S(1)} %get-tuple-element.37.v_ref.v0_ref, f32[32,4096]{1,0:T(8,128)S(1)} %get-tuple-element.59.v2_ref, f32[32,4096]{1,0:T(8,128)S(1)} %get-tuple-element.60.r_ref, ...), custom_call_target="tpu_custom_call" | custom-call | flops 2000000000 | bytes 4575232 | tf_op jit(solution)/shard_map/pallas_call | solution.py:309
  60.3 0.0 collective-permute-done.10.yl_ref
  60.3 0.0 collective-permute-done.11.yh_ref
  60.3 0.0 collective-permute-done.8.xl_ref
  60.3 0.0 collective-permute-done.9.xh_ref
  60.3 2.1 %shard_map.110 = (f32[864,128]{1,0:T(8,128)}, f32[4,27,1024]{2,1,0:T(8,128)S(1)}) custom-call(s32[1,1]{1,0:T(1,128)S(6)} %copy.16.count_ref, f32[32,4096]{1,0:T(8,128)S(1)} %get-tuple-element.63.int_ref, f32[32,4096]{1,0:T(8,128)S(1)} %get-tuple-element.64.u_ref, bf16[128,64]{1,0:T(8,128)(2,1)S(1)} %get-tuple-element.40.refs_2_.fh_ref, ...), custom_call_target="tpu_custom_call" | custom-call | bytes 3047428 | tf_op jit(solution)/shard_map/pallas_call | solution.py:309
  62.4 1.0 %copy.13 = f32[1,1,4,27,1024]{4,2,3,1,0:T(4,128)} copy(f32[1,1,4,27,1024]{4,3,2,1,0:T(8,128)S(1)} %bitcast.10) | data formatting | bytes 884736
Async XLA Ops:
  0.6 1.0 %copy-start = (f32[27,4,8,128]{3,2,1,0:T(8,128)S(1)}, f32[27,4,8,128]{3,2,1,0:T(8,128)}, u32[]{:S(2)}) copy-start(f32[27,4,8,128]{3,2,1,0:T(8,128)} %param.9) | copy-start | bytes 1327108
  1.6 16.9 %copy-start.6 = (f32[1,1,4,27,1024]{4,2,3,1,0:T(4,128)S(1)}, f32[1,1,4,27,1024]{4,2,3,1,0:T(4,128)}, u32[]{:S(2)}) copy-start(f32[1,1,4,27,1024]{4,2,3,1,0:T(4,128)} %param.10) | copy-start | bytes 1327108
  1.9 22.4 %collective-permute-start.2 = (f32[36,128]{1,0:T(8,128)S(1)}, f32[36,128]{1,0:T(8,128)S(1)}, u32[]{:S(2)}, u32[]{:S(2)}) collective-permute-start(f32[36,128]{1,0:T(8,128)S(1)} %get-tuple-element.43), channel_id=1, source_target_pairs={{0,1},{1,2},{2,3},{3,4},{4,5},{5,6},{6,7},{7,8},{8,9},{9,10},{10,1... | collective-permute-start | bytes 55304 | tf_op jit(solution)/shard_map/ppermute | solution.py:326
  7.7 16.6 %collective-permute-start.3 = (f32[36,128]{1,0:T(8,128)S(1)}, f32[36,128]{1,0:T(8,128)S(1)}, u32[]{:S(2)}, u32[]{:S(2)}) collective-permute-start(f32[36,128]{1,0:T(8,128)S(1)} %get-tuple-element.44), channel_id=1, source_target_pairs={{1,0},{2,1},{3,2},{4,3},{5,4},{6,5},{7,6},{8,7},{9,8},{10,9},{11,1... | collective-permute-start | bytes 55304 | tf_op jit(solution)/shard_map/ppermute | solution.py:326
  9.6 14.7 %collective-permute-start = (f32[72,128]{1,0:T(8,128)S(1)}, f32[72,128]{1,0:T(8,128)S(1)}, u32[]{:S(2)}, u32[]{:S(2)}) collective-permute-start(f32[72,128]{1,0:T(8,128)S(1)} %get-tuple-element.41), channel_id=1, source_target_pairs={{0,16},{16,32},{32,48},{48,64},{64,80},{80,96},{96,112},{112,128},... | collective-permute-start | bytes 110600 | tf_op jit(solution)/shard_map/ppermute | solution.py:326
  12.8 11.5 %collective-permute-start.1 = (f32[72,128]{1,0:T(8,128)S(1)}, f32[72,128]{1,0:T(8,128)S(1)}, u32[]{:S(2)}, u32[]{:S(2)}) collective-permute-start(f32[72,128]{1,0:T(8,128)S(1)} %get-tuple-element.42), channel_id=1, source_target_pairs={{16,0},{32,16},{48,32},{64,48},{80,64},{96,80},{112,96},{128,112},... | collective-permute-start | bytes 110600 | tf_op jit(solution)/shard_map/ppermute | solution.py:326
  18.5 0.7 %copy-start.2 = (f32[1,1,4,1024]{3,2,1,0:T(4,128)S(1)}, f32[1,1,4,1024]{3,2,1,0:T(4,128)}, u32[]{:S(2)}) copy-start(f32[1,1,4,1024]{3,2,1,0:T(4,128)} %param.11) | copy-start | bytes 49156
  18.5 0.7 %copy-start.3 = (f32[27,27]{1,0:T(8,128)S(1)}, f32[27,27]{1,0:T(8,128)}, u32[]{:S(2)}) copy-start(f32[27,27]{1,0:T(8,128)} %vol_ref.1) | copy-start | bytes 8752
  18.5 0.7 %copy-start.4 = (f32[27,54]{1,0:T(8,128)S(1)}, f32[27,54]{1,0:T(8,128)}, u32[]{:S(2)}) copy-start(f32[27,54]{1,0:T(8,128)} %face_ref.1) | copy-start | bytes 17500
  18.5 0.9 %copy-start.5 = (bf16[64,1152]{1,0:T(8,128)(2,1)S(1)}, bf16[64,1152]{1,0:T(8,128)(2,1)}, u32[]{:S(2)}) copy-start(bf16[64,1152]{1,0:T(8,128)(2,1)} %constant.2.clone.sel_ref) | copy-start | bytes 442372
  18.8 0.7 %copy-start.1 = (s32[1,1,1024]{2,1,0:T(1,128)S(1)}, s32[1,1,1024]{2,1,0:T(1,128)}, u32[]{:S(2)}) copy-start(s32[1,1,1024]{2,1,0:T(1,128)} %param.12) | copy-start | bytes 12292
  24.6 17.8 %collective-permute-start.6 = (f32[36,128]{1,0:T(8,128)S(1)}, f32[36,128]{1,0:T(8,128)S(1)}, u32[]{:S(2)}, u32[]{:S(2)}) collective-permute-start(f32[36,128]{1,0:T(8,128)S(1)} %get-tuple-element.57), channel_id=1, source_target_pairs={{0,1},{1,2},{2,3},{3,4},{4,5},{5,6},{6,7},{7,8},{8,9},{9,10},{10,1... | collective-permute-start | bytes 55304 | tf_op jit(solution)/shard_map/ppermute | solution.py:326
  30.1 12.4 %collective-permute-start.7 = (f32[36,128]{1,0:T(8,128)S(1)}, f32[36,128]{1,0:T(8,128)S(1)}, u32[]{:S(2)}, u32[]{:S(2)}) collective-permute-start(f32[36,128]{1,0:T(8,128)S(1)} %get-tuple-element.58), channel_id=1, source_target_pairs={{1,0},{2,1},{3,2},{4,3},{5,4},{6,5},{7,6},{8,7},{9,8},{10,9},{11,1... | collective-permute-start | bytes 55304 | tf_op jit(solution)/shard_map/ppermute | solution.py:326
  32.0 10.5 %collective-permute-start.4 = (f32[72,128]{1,0:T(8,128)S(1)}, f32[72,128]{1,0:T(8,128)S(1)}, u32[]{:S(2)}, u32[]{:S(2)}) collective-permute-start(f32[72,128]{1,0:T(8,128)S(1)} %get-tuple-element.55), channel_id=1, source_target_pairs={{0,16},{16,32},{32,48},{48,64},{64,80},{80,96},{96,112},{112,128},... | collective-permute-start | bytes 110600 | tf_op jit(solution)/shard_map/ppermute | solution.py:326
  33.9 8.6 %collective-permute-start.5 = (f32[72,128]{1,0:T(8,128)S(1)}, f32[72,128]{1,0:T(8,128)S(1)}, u32[]{:S(2)}, u32[]{:S(2)}) collective-permute-start(f32[72,128]{1,0:T(8,128)S(1)} %get-tuple-element.56), channel_id=1, source_target_pairs={{16,0},{32,16},{48,32},{64,48},{80,64},{96,80},{112,96},{128,112},... | collective-permute-start | bytes 110600 | tf_op jit(solution)/shard_map/ppermute | solution.py:326
  42.7 17.5 %collective-permute-start.10 = (f32[36,128]{1,0:T(8,128)S(1)}, f32[36,128]{1,0:T(8,128)S(1)}, u32[]{:S(2)}, u32[]{:S(2)}) collective-permute-start(f32[36,128]{1,0:T(8,128)S(1)} %get-tuple-element.67), channel_id=1, source_target_pairs={{0,1},{1,2},{2,3},{3,4},{4,5},{5,6},{6,7},{7,8},{8,9},{9,10},{10,1... | collective-permute-start | bytes 55304 | tf_op jit(solution)/shard_map/ppermute | solution.py:326
  48.2 12.1 %collective-permute-start.11 = (f32[36,128]{1,0:T(8,128)S(1)}, f32[36,128]{1,0:T(8,128)S(1)}, u32[]{:S(2)}, u32[]{:S(2)}) collective-permute-start(f32[36,128]{1,0:T(8,128)S(1)} %get-tuple-element.68), channel_id=1, source_target_pairs={{1,0},{2,1},{3,2},{4,3},{5,4},{6,5},{7,6},{8,7},{9,8},{10,9},{11,1... | collective-permute-start | bytes 55304 | tf_op jit(solution)/shard_map/ppermute | solution.py:326
  50.1 10.2 %collective-permute-start.8 = (f32[72,128]{1,0:T(8,128)S(1)}, f32[72,128]{1,0:T(8,128)S(1)}, u32[]{:S(2)}, u32[]{:S(2)}) collective-permute-start(f32[72,128]{1,0:T(8,128)S(1)} %get-tuple-element.65), channel_id=1, source_target_pairs={{0,16},{16,32},{32,48},{48,64},{64,80},{80,96},{96,112},{112,128},... | collective-permute-start | bytes 110600 | tf_op jit(solution)/shard_map/ppermute | solution.py:326
  52.0 8.3 %collective-permute-start.9 = (f32[72,128]{1,0:T(8,128)S(1)}, f32[72,128]{1,0:T(8,128)S(1)}, u32[]{:S(2)}, u32[]{:S(2)}) collective-permute-start(f32[72,128]{1,0:T(8,128)S(1)} %get-tuple-element.66), channel_id=1, source_target_pairs={{16,0},{32,16},{48,32},{64,48},{80,64},{96,80},{112,96},{128,112},... | collective-permute-start | bytes 110600 | tf_op jit(solution)/shard_map/ppermute | solution.py:326

commit v2 on v1

v2 whole, which is shorter than its diff:
```python
import numpy as np
import jax
import jax.numpy as jnp
from jax import lax
from jax.experimental import pallas as pl
from jax.experimental.pallas import tpu as pltpu
from jax.sharding import PartitionSpec as P

F32 = jnp.float32
BF16 = jnp.bfloat16
CX, CY, CZ = 4, 8, 128
ROWS = CX * CY
ZONES = ROWS * CZ
SLOTS = 1024
GROUP = 256
GROUPS = ZONES // GROUP
HIGHEST = lax.Precision.HIGHEST


def face_dofs(face, own):
    axis, high = divmod(face, 2)
    at = (2 if high else 0) if own else (0 if high else 2)
    dofs = []
    for p in range(3):
        for q in range(3):
            abc = [p, q]
            abc.insert(axis, at)
            dofs.append(abc[0] * 9 + abc[1] * 3 + abc[2])
    return dofs


def selections():
    sel = np.zeros((64, 7 * 128 + 4 * 64), np.float32)
    for face in range(6):
        for q in range(9):
            row = 9 * face + q
            for copy in range(4):
                sel[row, copy * 32 + face_dofs(face, True)[q]] -= 1.0
                sel[row, (face + 1) * 128 + copy * 32 + face_dofs(face, False)[q]] += 1.0
                if face < 4:
                    sel[row, 7 * 128 + face * 64 + copy * 16 + q] += 1.0
    return sel


def halves(x):
    hi = x.astype(BF16)
    lo = (x - hi.astype(F32)).astype(BF16)
    return hi, lo


def stack_right(x):
    hi, lo = halves(x)
    return jnp.concatenate([hi, lo, hi, lo], axis=0)


def stack_left(x, half):
    hi = x.astype(BF16).astype(F32)
    lane = lax.broadcasted_iota(jnp.int32, x.shape, 1)
    return jnp.where(lane < half, hi, x - hi).astype(BF16)


def dot(a, b):
    return jnp.dot(a, b, preferred_element_type=F32)


def block(r):
    return slice(r * CZ, (r + 1) * CZ)


def interior(v_ref, wg_ref, g_ref, out_ref):
    for x in range(CX):
        cols = slice(x * 1024, (x + 1) * 1024)
        g_ref[:, cols] = dot(wg_ref[...], stack_right(v_ref[:, cols]))
    lane = lax.broadcasted_iota(jnp.int32, (32, CZ), 1)
    for x in range(CX):
        for y in range(CY):
            r = x * CY + y
            total = g_ref[0:32, block(r)]
            if x > 0:
                total += g_ref[32:64, block(r - CY)]
            if x < CX - 1:
                total += g_ref[64:96, block(r + CY)]
            if y > 0:
                total += g_ref[96:128, block(r - 1)]
            if y < CY - 1:
                total += g_ref[128:160, block(r + 1)]
            below = pltpu.roll(g_ref[160:192, block(r)], 1, 1)
            above = pltpu.roll(g_ref[192:224, block(r)], CZ - 1, 1)
            total += jnp.where(lane == 0, 0.0, below)
            total += jnp.where(lane == CZ - 1, 0.0, above)
            out_ref[:, block(r)] = total


def lane_hot(idx):
    place = lax.broadcasted_iota(jnp.int32, (GROUP, SLOTS), 0)
    return jnp.where(place == (idx & (GROUP - 1)), 1.0, 0.0).astype(BF16)


def to_slots(r_ref, hot, idx):
    total = jnp.zeros((32, SLOTS), F32)
    group = lax.shift_right_logical(idx, 8)
    for g in range(GROUPS):
        hi, lo = halves(r_ref[:, g * GROUP:(g + 1) * GROUP])
        both = dot(jnp.concatenate([hi, lo], axis=0), hot)
        total = jnp.where(group == g, both[0:32] + both[32:64], total)
    return total


def first_kernel(*refs):
    count = 8
    sources, (v_ref, ylo_ref, yhi_ref), rest = refs[:count], refs[count:count + 3], refs[count + 3:]
    targets, (state_ref, sems) = rest[:count - 1], rest[count - 1:]
    copies = [
        pltpu.make_async_copy(source, target, sems.at[k])
        for k, (source, target) in enumerate(zip(sources, (state_ref,) + targets))
    ]
    for copy in copies:
        copy.start()
    v_ref[24:32, :] = jnp.zeros((8, ZONES), F32)
    copies[0].wait()
    for q in range(9):
        low, high = face_dofs(2, True)[q], face_dofs(3, True)[q]
        ylo_ref[q * 4:q * 4 + 4, :] = state_ref[pl.ds(low * 32, 4, stride=8), :]
        yhi_ref[q * 4:q * 4 + 4, :] = state_ref[pl.ds(high * 32 + 7, 4, stride=8), :]
    for r in range(ROWS):
        v_ref[0:27, block(r)] = state_ref[pl.ds(r, 27, stride=32), :]
    for copy in copies[1:]:
        copy.wait()


def mixed_kernel(
    count_ref, v_ref, w_ref, frac_ref, idx_ref, vol_ref, face_ref, mat_ref, sel_ref,
    int_ref, u_ref, fm_ref, wg_ref, fh_ref, pp_ref, b3_ref, c_ref,
    g_ref, small_ref, diag_ref, wpad_ref,
):
    small_ref[...] = jnp.zeros((32, 128), F32)
    small_ref[0:27, 0:54] = face_ref[...]
    f_hi, f_lo = halves(small_ref[:, 0:64])
    laid = dot(f_hi, sel_ref[...]) + dot(f_lo, sel_ref[...])
    small_ref[...] = jnp.zeros((32, 128), F32)
    small_ref[0:27, 0:27] = vol_ref[...]
    vol = small_ref[...]
    vol4 = vol + pltpu.roll(vol, 32, 1)
    vol4 = vol4 + pltpu.roll(vol4, 64, 1)
    wg_ref[0:32, :] = stack_left(laid[:, 0:128] + vol4, 64)
    for k in range(1, 7):
        wg_ref[32 * k:32 * k + 32, :] = stack_left(laid[:, 128 * k:128 * k + 128], 64)
    for k in range(4):
        first = 7 * 128 + 64 * k
        fh_ref[32 * k:32 * k + 32, :] = stack_left(laid[:, first:first + 64], 32)
    interior(v_ref, wg_ref, g_ref, int_ref)

    for m in range(4):
        small_ref[0:27, 0:27] = mat_ref[:, m, :]
        small = small_ref[...]
        diag_ref[32 * m:32 * m + 32, :] = pltpu.roll(small, 32 * m, 1) if m else small
    m1 = diag_ref[...]
    row = lax.broadcasted_iota(jnp.int32, (128, 128), 0)
    column = lax.broadcasted_iota(jnp.int32, (128, 128), 1)
    eye = jnp.where(row == column, 1.0, 0.0)
    m2 = jnp.dot(m1, m1, precision=HIGHEST)
    p1 = eye + m1 + m2 + jnp.dot(m1 + m2, m2, precision=HIGHEST)
    p2 = jnp.dot(p1, p1, precision=HIGHEST)
    p3 = jnp.dot(p2, p1, precision=HIGHEST)
    q2 = 0.75 * eye + 0.25 * p2
    q3 = (1.0 / 3.0) * eye + 0.5 * p1 + (1.0 / 6.0) * p3

    def stacked(matrix, m):
        rows = matrix[32 * m:32 * m + 32, :]
        for shift in (32, 64):
            rows = rows + pltpu.roll(rows, shift, 1)
        return stack_left(rows, 64)

    for m in range(4):
        pp_ref[32 * m:32 * m + 32, :] = stacked(p1, m)
        pp_ref[128 + 32 * m:128 + 32 * m + 32, :] = stacked(p2, m)

    idx = idx_ref[...]
    slot = lax.broadcasted_iota(jnp.int32, (1, SLOTS), 1)
    live = slot < count_ref[0, 0]
    frac = frac_ref[...]
    wpad_ref[...] = jnp.zeros((32, SLOTS), F32)
    sums = [0.0, 0.0, 0.0]
    for m in range(4):
        wpad_ref[0:27, :] = w_ref[:, m, :]
        left = jnp.concatenate([stacked(p1, m), stacked(q2, m), stacked(q3, m)], axis=0)
        values = dot(left, stack_right(wpad_ref[...]))
        for k in range(3):
            sums[k] = sums[k] + frac[m:m + 1, :] * values[32 * k:32 * k + 32]
        b3_ref[m] = values[64:96]
    first = jnp.where(live, sums[0], 0.0)
    first = jnp.concatenate([first[0:27], jnp.where(live, frac, 0.0), first[31:32]], axis=0)
    for k in range(2):
        c_ref[32 * k:32 * k + 32, :] = jnp.where(live, sums[k + 1], 0.0)

    hot = lane_hot(idx)
    for g in range(GROUPS):
        cols = slice(g * GROUP, (g + 1) * GROUP)
        dense = to_zones(stack_pair(first), hot, idx, g)
        u_ref[:, cols] = jnp.where(dense[27:28] > 0.0, dense, v_ref[:, cols])
        fm_ref[:, cols] = dense[24:32]


def stack_pair(x):
    return jnp.concatenate(halves(x), axis=0)


def to_zones(both, hot, idx, g):
    here = jnp.where(lax.shift_right_logical(idx, 8) == g, 1.0, 0.0).astype(BF16)
    dense = lax.dot_general(
        both * here, hot, (((1,), (1,)), ((), ())), preferred_element_type=F32
    )
    rows = both.shape[0] // 2
    return dense[0:rows] + dense[rows:]


def zones_kernel(after_ref, c_ref, idx_ref, c2_ref, c3_ref):
    idx = idx_ref[...]
    hot = lane_hot(idx)
    both = stack_pair(c_ref[...])
    for g in range(GROUPS):
        cols = slice(g * GROUP, (g + 1) * GROUP)
        dense = to_zones(both, hot, idx, g)
        c2_ref[:, cols] = dense[0:32]
        c3_ref[:, cols] = dense[32:64]


def inside(axis):
    at = lax.axis_index(axis)
    return at > 0, at < lax.axis_size(axis) - 1


def halo_x(xlo_ref, xhi_ref, pad_ref, first=0):
    for y in range(CY):
        pad_ref[0:9, block(y)] = xlo_ref[pl.ds(first + y, 9, stride=8), :]
        pad_ref[0:9, block(CY + y)] = xhi_ref[pl.ds(first + y, 9, stride=8), :]


def halo_y(ylo_ref, yhi_ref, pad_ref):
    low, high = inside("yz")
    for x in range(CX):
        pad_ref[0:9, block(16 + x)] = jnp.where(low, ylo_ref[pl.ds(x, 9, stride=4), :], 0.0)
        pad_ref[0:9, block(20 + x)] = jnp.where(high, yhi_ref[pl.ds(x, 9, stride=4), :], 0.0)


def terms(fh_ref, pad_ref, face):
    first, last = ((0, 1024), (1024, 2048), (2048, 2560), (2560, 3072))[face]
    return dot(fh_ref[32 * face:32 * face + 32, :], stack_right(pad_ref[:, first:last]))


def halo_add(int_ref, fh_ref, pad_ref, rate_ref, along_x, along_y):
    x_low, x_high = [terms(fh_ref, pad_ref, face) for face in (0, 1)] if along_x else (None, None)
    y_low, y_high = [terms(fh_ref, pad_ref, face) for face in (2, 3)] if along_y else (None, None)
    for x in range(CX):
        for y in range(CY):
            r = x * CY + y
            total = int_ref[:, block(r)]
            if along_x and x == 0:
                total += x_low[:, block(y)]
            if along_x and x == CX - 1:
                total += x_high[:, block(y)]
            if along_y and y == 0:
                total += y_low[:, block(x)]
            if along_y and y == CY - 1:
                total += y_high[:, block(x)]
            rate_ref[:, block(r)] = total


def x_faces(v_ref, xlo_ref, xhi_ref, first=0):
    for y in range(CY):
        xlo_ref[pl.ds(first + y, 9, stride=8), :] = v_ref[0:9, block(y)]
        xhi_ref[pl.ds(first + y, 9, stride=8), :] = v_ref[18:27, block(24 + y)]


def y_faces(v_ref, ylo_ref, yhi_ref):
    for x in range(CX):
        for a in range(3):
            ylo_ref[pl.ds(12 * a + x, 3, stride=4), :] = v_ref[9 * a:9 * a + 3, block(8 * x)]
            yhi_ref[pl.ds(12 * a + x, 3, stride=4), :] = v_ref[9 * a + 6:9 * a + 9, block(8 * x + 7)]


def y_first_kernel(
    int_ref, u_ref, v_ref, fh_ref, yl_ref, yh_ref, rate_ref, xlo_ref, xhi_ref, pad_ref,
):
    pad_ref[...] = jnp.zeros((16, 3072), F32)
    halo_y(yl_ref, yh_ref, pad_ref)
    halo_add(int_ref, fh_ref, pad_ref, rate_ref, False, True)
    x_faces(v_ref, xlo_ref, xhi_ref)
    for y in range(CY):
        xlo_ref[pl.ds(72 + y, 9, stride=8), :] = u_ref[0:9, block(y)] + rate_ref[0:9, block(y)]
        xhi_ref[pl.ds(72 + y, 9, stride=8), :] = (
            u_ref[18:27, block(24 + y)] + rate_ref[18:27, block(24 + y)]
        )


def x_first_kernel(
    int_ref, u_ref, v_ref, fh_ref, xl_ref, xh_ref,
    next_ref, rate_ref, beside_ref, ylo_ref, yhi_ref, pad_ref, own_ref,
):
    pad_ref[...] = jnp.zeros((16, 3072), F32)
    halo_x(xl_ref, xh_ref, pad_ref)
    halo_add(int_ref, fh_ref, pad_ref, rate_ref, True, False)
    next_ref[...] = u_ref[...] + rate_ref[...]
    y_faces(next_ref, ylo_ref, yhi_ref)
    own_ref[...] = jnp.zeros((16, 2048), F32)
    own_ref[0:9, 0:1024] = v_ref[0:9, 0:1024]
    own_ref[0:9, 1024:2048] = v_ref[18:27, 3072:4096]
    to_low = dot(fh_ref[32:64, :], stack_right(own_ref[:, 0:1024]))
    to_high = dot(fh_ref[0:32, :], stack_right(own_ref[:, 1024:2048]))
    low, high = inside("gx")
    halo_x(xl_ref, xh_ref, pad_ref, 72)
    beside_ref[...] = jnp.zeros((16, 2048), F32)
    beside_ref[0:9, 0:1024] = pad_ref[0:9, 0:1024] + jnp.where(low, to_low[18:27], 0.0)
    beside_ref[0:9, 1024:2048] = pad_ref[0:9, 1024:2048] + jnp.where(high, to_high[0:9], 0.0)


def second_kernel(
    int_ref, u_ref, fh_ref, yl_ref, yh_ref,
    v_ref, rate_ref, xlo_ref, xhi_ref, ylo_ref, yhi_ref, pad_ref,
):
    pad_ref[...] = jnp.zeros((16, 3072), F32)
    halo_y(yl_ref, yh_ref, pad_ref)
    halo_add(int_ref, fh_ref, pad_ref, rate_ref, False, True)
    v_ref[...] = u_ref[...] + 0.25 * rate_ref[...]
    x_faces(v_ref, xlo_ref, xhi_ref)
    y_faces(v_ref, ylo_ref, yhi_ref)


def between_one(
    v0_ref, v1_ref, r_ref, beside_ref, c2_ref, c3_ref, fm_ref, idx_ref, wg_ref, fh_ref, pp_ref, b3_ref,
    int_ref, u_ref, c3_out, b3_out, g_ref,
):
    interior(v1_ref, wg_ref, g_ref, int_ref)
    int_ref[:, 0:1024] += terms(fh_ref, beside_ref, 0)
    int_ref[:, 3072:4096] += terms(fh_ref, beside_ref, 1)
    for x in range(CX):
        cols = slice(x * 1024, (x + 1) * 1024)
        q = dot(pp_ref[...], stack_right(r_ref[:, cols]))
        f = fm_ref[:, cols]
        s1 = sum(f[m + 3:m + 4] * q[32 * m:32 * m + 32] for m in range(4))
        s2 = sum(f[m + 3:m + 4] * q[128 + 32 * m:160 + 32 * m] for m in range(4))
        bulk = 0.75 * v0_ref[:, cols] + 0.25 * v1_ref[:, cols]
        u_ref[:, cols] = jnp.where(f[3:4] > 0.0, c2_ref[:, cols] + 0.25 * s1, bulk)
        c3_out[:, cols] = c3_ref[:, cols] + (1.0 / 6.0) * s2
    idx = idx_ref[...]
    at = stack_right(to_slots(r_ref, lane_hot(idx), idx))
    for m in range(4):
        b3_out[m] = b3_ref[m] + (1.0 / 6.0) * dot(pp_ref[128 + 32 * m:160 + 32 * m, :], at)


def between_two(
    v0_ref, v2_ref, r_ref, c3_ref, fm_ref, idx_ref, wg_ref, pp_ref, b3_ref,
    int_ref, u_ref, b3_out, g_ref,
):
    interior(v2_ref, wg_ref, g_ref, int_ref)
    for x in range(CX):
        cols = slice(x * 1024, (x + 1) * 1024)
        q = dot(pp_ref[0:128, :], stack_right(r_ref[:, cols]))
        f = fm_ref[:, cols]
        s1 = sum(f[m + 3:m + 4] * q[32 * m:32 * m + 32] for m in range(4))
        bulk = (1.0 / 3.0) * v0_ref[:, cols] + (2.0 / 3.0) * v2_ref[:, cols]
        u_ref[:, cols] = jnp.where(f[3:4] > 0.0, c3_ref[:, cols] + (1.0 / 6.0) * s1, bulk)
    idx = idx_ref[...]
    at = stack_right(to_slots(r_ref, lane_hot(idx), idx))
    for m in range(4):
        b3_out[m] = b3_ref[m] + (1.0 / 6.0) * dot(pp_ref[32 * m:32 * m + 32, :], at)


def last_kernel(
    count_ref, int_ref, u_ref, fh_ref, xl_ref, xh_ref, yl_ref, yh_ref, idx_ref, b3_ref, w_ref,
    field_hbm, out_hbm, pad_ref, rate_ref, field_ref, out_ref, sems,
):
    pad_ref[...] = jnp.zeros((16, 3072), F32)
    halo_x(xl_ref, xh_ref, pad_ref)
    halo_y(yl_ref, yh_ref, pad_ref)
    halo_add(int_ref, fh_ref, pad_ref, rate_ref, True, True)
    for r in range(ROWS):
        value = u_ref[0:27, block(r)] + (2.0 / 3.0) * rate_ref[0:27, block(r)]
        field_ref[pl.ds(r, 27, stride=32), :] = value
    field_copy = pltpu.make_async_copy(field_ref, field_hbm, sems.at[0])
    field_copy.start()
    idx = idx_ref[...]
    at = (2.0 / 3.0) * to_slots(rate_ref, lane_hot(idx), idx)
    live = lax.broadcasted_iota(jnp.int32, (1, SLOTS), 1) < count_ref[0, 0]
    for m in range(4):
        out_ref[:, m, :] = jnp.where(live, b3_ref[m, 0:27, :] + at[0:27], w_ref[:, m, :])
    out_copy = pltpu.make_async_copy(out_ref, out_hbm, sems.at[1])
    out_copy.start()
    field_copy.wait()
    out_copy.wait()


VMEM = pl.BlockSpec(memory_space=pltpu.VMEM)
SMEM = pl.BlockSpec(memory_space=pltpu.SMEM)
ANY = pl.BlockSpec(memory_space=pl.ANY)
DENSE = jax.ShapeDtypeStruct((32, ZONES), F32)
X_FACES = [jax.ShapeDtypeStruct((72, 128), F32)] * 2
X_TWICE = [jax.ShapeDtypeStruct((144, 128), F32)] * 2
Y_FACES = [jax.ShapeDtypeStruct((36, 128), F32)] * 2
SLOT3 = jax.ShapeDtypeStruct((4, 32, SLOTS), F32)


def call(kernel, outs, args, scratch=(), smem=0, flops=0, in_spec=VMEM, out_spec=VMEM):
    specs = [SMEM] * smem + [in_spec] * (len(args) - smem)
    moved = 4 * sum(int(np.prod(a.shape)) for a in list(args) + list(outs))
    return pl.pallas_call(
        kernel,
        out_shape=outs,
        in_specs=specs,
        out_specs=[out_spec] * len(outs),
        scratch_shapes=list(scratch),
        compiler_params=pltpu.CompilerParams(vmem_limit_bytes=48 * 1024 * 1024),
        cost_estimate=pl.CostEstimate(flops=flops, bytes_accessed=moved, transcendentals=0),
    )(*args)


def exchange_x(low, high):
    n = lax.axis_size("gx")
    below = lax.ppermute(high, "gx", [(i, i + 1) for i in range(n - 1)])
    above = lax.ppermute(low, "gx", [(i + 1, i) for i in range(n - 1)])
    return below, above


def exchange_y(low, high):
    n = lax.axis_size("yz")
    below = lax.ppermute(high, "yz", [(i, (i + 1) % n) for i in range(n)])
    above = lax.ppermute(low, "yz", [(i, (i - 1) % n) for i in range(n)])
    return below, above


def on_device(
    state, mix_weights, mix_frac, mix_index, mix_count, vol_matrix, face_matrix, mat_matrix
):
    flat = state.reshape(27 * ROWS, CZ)
    small = [
        mix_weights.reshape(4, 27, SLOTS).transpose(1, 0, 2),
        mix_frac.reshape(4, SLOTS),
        mix_index.reshape(1, SLOTS),
        vol_matrix,
        face_matrix,
        mat_matrix.transpose(1, 0, 2),
        jnp.asarray(selections(), BF16),
    ]
    count = mix_count.reshape(1, 1)
    g_space = pltpu.VMEM((224, ZONES), F32)
    pad = pltpu.VMEM((16, 3072), F32)
    bf = lambda rows, lanes: jax.ShapeDtypeStruct((rows, lanes), BF16)
    f32 = lambda rows, lanes: jax.ShapeDtypeStruct((rows, lanes), F32)

    v0, *out = call(
        first_kernel,
        [DENSE] + Y_FACES + [jax.ShapeDtypeStruct(a.shape, a.dtype) for a in small],
        [flat] + small,
        [pltpu.VMEM((27 * ROWS, CZ), F32), pltpu.SemaphoreType.DMA((8,))],
        in_spec=ANY,
    )
    halo = exchange_y(*out[:2])
    small = out[2:]
    weights, idx = small[0], small[2]
    inner, u, fm, wg, fh, pp, b3, rest = call(
        mixed_kernel,
        [DENSE, DENSE, f32(8, ZONES), bf(224, 128), bf(128, 64), bf(256, 128), SLOT3, f32(64, SLOTS)],
        [count, v0] + small,
        [g_space, pltpu.VMEM((32, 128), F32), pltpu.VMEM((128, 128), F32),
         pltpu.VMEM((32, SLOTS), F32)],
        smem=1, flops=3 * 10**9,
    )
    inner, *faces = call(
        y_first_kernel, [DENSE] + X_TWICE, [inner, u, v0, fh, *halo], [pad]
    )
    halo = exchange_x(*faces)
    c2, c3 = call(zones_kernel, [DENSE, DENSE], [faces[0], rest, idx], flops=2 * 10**9)
    v1, r0, beside, *faces = call(
        x_first_kernel, [DENSE, DENSE, f32(16, 2048)] + Y_FACES, [inner, u, v0, fh, *halo],
        [pad, pltpu.VMEM((16, 2048), F32)],
    )
    halo = exchange_y(*faces)
    inner, u, c3, b3 = call(
        between_one, [DENSE, DENSE, DENSE, SLOT3],
        [v0, v1, r0, beside, c2, c3, fm, idx, wg, fh, pp, b3], [g_space], flops=2 * 10**9,
    )
    v2, r1, *faces = call(
        second_kernel, [DENSE, DENSE] + X_FACES + Y_FACES, [inner, u, fh, *halo], [pad]
    )
    y_halo = exchange_y(*faces[2:])
    x_halo = exchange_x(*faces[:2])
    inner, u, b3 = call(
        between_two, [DENSE, DENSE, SLOT3],
        [v0, v2, r1, c3, fm, idx, wg, pp, b3], [g_space], flops=2 * 10**9,
    )
    field, out = call(
        last_kernel,
        [jax.ShapeDtypeStruct((27 * ROWS, CZ), F32), jax.ShapeDtypeStruct((27, 4, SLOTS), F32)],
        [count, inner, u, fh, *x_halo, *y_halo, idx, b3, weights],
        [pad, pltpu.VMEM((32, ZONES), F32), pltpu.VMEM((27 * ROWS, CZ), F32),
         pltpu.VMEM((27, 4, SLOTS), F32), pltpu.SemaphoreType.DMA((2,))],
        smem=1, out_spec=ANY,
    )
    return field.reshape(state.shape), out.transpose(1, 0, 2).reshape(mix_weights.shape)


def solution(mesh):
    placed = (
        P(None, "gx", "yz", None),
        P("gx", "yz", None, None, None),
        P("gx", "yz", None, None),
        P("gx", "yz", None),
        P("gx", "yz"),
        P(),
        P(),
        P(),
    )
    return jax.shard_map(
        on_device,
        mesh=mesh,
        in_specs=placed,
        out_specs=(P(None, "gx", "yz", None), P("gx", "yz", None, None, None)),
        check_vma=False,
    )
```

time: 64 us -> 57.2 us (0.89)
  the two profiles are of different devices: /device:TPU:199 before, /device:TPU:6 now
where the time goes in v2:
time: 57.2 us; the launch traced here: 56.6 us
  starting transfers between devices  30.3 us (53%)
  Pallas kernels  18.2 us (32%)
  local copies, waits for them, and re-layouts  6.58 us (12%)
  between operations  1.48 us (3%)
    pallas_call x9, Pallas kernels, call(): pl.pallas_call(kernel, out_shape=outs, in_specs=specs, out_specs=[out_spe...  18.2 us
    ppermute x3, starting transfers between devices, exchange_y(): above = lax.ppermute(low, 'yz', [(i, (i - 1) % n) for i in range(n)])  14.4 us
    ppermute x2, starting transfers between devices, exchange_x(): above = lax.ppermute(low, 'gx', [(i + 1, i) for i in range(n - 1)])  9.97 us
    unnamed x16, local copies, waits for them, and re-layouts  6.58 us
    ppermute x2, starting transfers between devices, exchange_x(): below = lax.ppermute(high, 'gx', [(i, i + 1) for i in range(n - 1)])  5.92 us
  transfers between devices with their start and end apart: 10, of which 0 were waited for; matrix products, arithmetic and copies ran while one was open for 0% of the time, Pallas kernels for 24%

profile of v2, /device:TPU:6, one launch (start us, length us, event | category | flops | bytes accessed | tf_op | source)
XLA Modules:
  0.0 56.6 jit_solution(14229046151675684398)
XLA Ops:
  0.6 0.0 copy-start.7
  0.6 0.7 %copy-done.7 = s32[1,1,1024]{2,1,0:T(1,128)S(1)} copy-done((s32[1,1,1024]{2,1,0:T(1,128)S(1)}, s32[1,1,1024]{2,1,0:T(1,128)}, u32[]{:S(2)}) %copy-start.7) | copy-done | bytes 4120
  1.3 0.0 copy-start
  1.3 1.0 %copy-done = f32[27,4,8,128]{3,2,1,0:T(8,128)S(1)} copy-done((f32[27,4,8,128]{3,2,1,0:T(8,128)S(1)}, f32[27,4,8,128]{3,2,1,0:T(8,128)}, u32[]{:S(2)}) %copy-start) | copy-done | bytes 442392
  2.3 0.0 copy-start.1
  2.3 1.0 %copy-done.1 = f32[1,1,4,27,1024]{4,2,3,1,0:T(4,128)S(1)} copy-done((f32[1,1,4,27,1024]{4,2,3,1,0:T(4,128)S(1)}, f32[1,1,4,27,1024]{4,2,3,1,0:T(4,128)}, u32[]{:S(2)}) %copy-start.1) | copy-done | bytes 442392
  3.3 0.0 copy-start.2
  3.3 0.9 %copy-done.2 = bf16[64,1152]{1,0:T(8,128)(2,1)S(1)} copy-done((bf16[64,1152]{1,0:T(8,128)(2,1)S(1)}, bf16[64,1152]{1,0:T(8,128)(2,1)}, u32[]{:S(2)}) %copy-start.2) | copy-done | bytes 147480
  4.3 0.0 copy-start.3
  4.3 0.8 %copy-done.3 = f32[4,27,27]{2,0,1:T(4,128)S(1)} copy-done((f32[4,27,27]{2,0,1:T(4,128)S(1)}, f32[4,27,27]{2,0,1:T(4,128)}, u32[]{:S(2)}) %copy-start.3) | copy-done | bytes 11688
  5.1 0.0 copy-start.4
  5.1 0.7 %copy-done.4 = f32[1,1,4,1024]{3,2,1,0:T(4,128)S(1)} copy-done((f32[1,1,4,1024]{3,2,1,0:T(4,128)S(1)}, f32[1,1,4,1024]{3,2,1,0:T(4,128)}, u32[]{:S(2)}) %copy-start.4) | copy-done | bytes 16408
  5.8 0.0 copy-start.5
  5.8 0.7 %copy-done.5 = f32[27,27]{1,0:T(8,128)S(1)} copy-done((f32[27,27]{1,0:T(8,128)S(1)}, f32[27,27]{1,0:T(8,128)}, u32[]{:S(2)}) %copy-start.5) | copy-done | bytes 2940
  6.5 0.0 copy-start.6
  6.5 0.7 %copy-done.6 = f32[27,54]{1,0:T(8,128)S(1)} copy-done((f32[27,54]{1,0:T(8,128)S(1)}, f32[27,54]{1,0:T(8,128)}, u32[]{:S(2)}) %copy-start.6) | copy-done | bytes 5856
  7.2 1.3 %shard_map.104 = (f32[32,4096]{1,0:T(8,128)S(1)}, f32[36,128]{1,0:T(8,128)S(1)}, f32[36,128]{1,0:T(8,128)S(1)}, f32[27,4,1024]{2,1,0:T(4,128)S(1)}, f32[4,1024]{...) custom-call(f32[864,128]{1,0:T(8,128)S(1)} %bitcast.11, ...), custom_call_target="tpu_custom_call" | custom-call | bytes 2559864 | tf_op jit(solution)/shard_map/pallas_call | solution.py:406
  8.5 0.0 collective-permute-start
  8.5 8.5 %collective-permute-start.1 = (f32[36,128]{1,0:T(8,128)S(1)}, f32[36,128]{1,0:T(8,128)S(1)}, u32[]{:S(2)}, u32[]{:S(2)}) collective-permute-start(f32[36,128]{1,0:T(8,128)S(1)} %get-tuple-element.57), channel_id=1, source_target_pairs={{0,15},{1,0},{2,1},{3,2},{4,3},{5,4},{6,5},{7,6},{8,7},{9,8},{10,9... | collective-permute-start | bytes 55304 | tf_op jit(solution)/shard_map/ppermute | solution.py:427
  17.7 4.8 %shard_map.105 = (f32[32,4096]{1,0:T(8,128)S(1)}, f32[32,4096]{1,0:T(8,128)S(1)}, f32[8,4096]{1,0:T(8,128)S(1)}, bf16[224,128]{1,0:T(8,128)(2,1)S(1)}, bf16[128,...) custom-call(s32[1,1]{1,0:T(1,128)S(6)} %copy.11.count_ref, ...), custom_call_target="tpu_custom_call" | custom-call | flops 3000000000 | bytes 3547072 | tf_op jit(solution)/shard_map/pallas_call | solution.py:406
  22.4 0.0 collective-permute-done.yl_ref
  22.5 0.0 collective-permute-done.1.yh_ref
  22.5 0.2 shard_map.106
  22.6 3.5 %collective-permute-start.2 = (f32[144,128]{1,0:T(8,128)S(1)}, f32[144,128]{1,0:T(8,128)S(1)}, u32[]{:S(2)}, u32[]{:S(2)}) collective-permute-start(f32[144,128]{1,0:T(8,128)S(1)} %get-tuple-element.59), channel_id=1, source_target_pairs={{0,16},{16,32},{32,48},{48,64},{64,80},{80,96},{96,112},{112,128},... | collective-permute-start | bytes 221192 | tf_op jit(solution)/shard_map/ppermute | solution.py:419
  26.1 4.5 %collective-permute-start.3 = (f32[144,128]{1,0:T(8,128)S(1)}, f32[144,128]{1,0:T(8,128)S(1)}, u32[]{:S(2)}, u32[]{:S(2)}) collective-permute-start(f32[144,128]{1,0:T(8,128)S(1)} %get-tuple-element.60.after_ref), channel_id=1, source_target_pairs={{16,0},{32,16},{48,32},{64,48},{80,64},{96,80},{112,96},{128,112},... | collective-permute-start | bytes 221192 | tf_op jit(solution)/shard_map/ppermute | solution.py:420
  30.6 2.8 %shard_map.108 = (f32[32,4096]{1,0:T(8,128)S(1)}, f32[32,4096]{1,0:T(8,128)S(1)}) custom-call(f32[144,128]{1,0:T(8,128)S(1)} %get-tuple-element.60.after_ref, f32[64,1024]{1,0:T(8,128)S(1)} %get-tuple-element.64.c_ref, s32[1,1024]{1,0:T(1,128)S(1)} %get-tuple-element.48.idx_ref), custom_call_target="tpu_custom_call" | custom-call | flops 2000000000 | bytes 1388544 | tf_op jit(solution)/shard_map/pallas_call | solution.py:406
  33.4 0.0 collective-permute-done.2.xl_ref
  33.4 0.0 collective-permute-done.3.xh_ref
  33.4 0.2 shard_map.107
  33.7 0.0 collective-permute-start.4
  33.7 2.9 %collective-permute-start.5 = (f32[36,128]{1,0:T(8,128)S(1)}, f32[36,128]{1,0:T(8,128)S(1)}, u32[]{:S(2)}, u32[]{:S(2)}) collective-permute-start(f32[36,128]{1,0:T(8,128)S(1)} %get-tuple-element.74), channel_id=1, source_target_pairs={{0,15},{1,0},{2,1},{3,2},{4,3},{5,4},{6,5},{7,6},{8,7},{9,8},{10,9... | collective-permute-start | bytes 55304 | tf_op jit(solution)/shard_map/ppermute | solution.py:427
  36.6 3.1 %shard_map.109 = (f32[32,4096]{1,0:T(8,128)S(1)}, f32[32,4096]{1,0:T(8,128)S(1)}, f32[32,4096]{1,0:T(8,128)S(1)}, f32[4,32,1024]{2,1,0:T(8,128)S(1)}) custom-call(f32[32,4096]{1,0:T(8,128)S(1)} %get-tuple-element.45.v_ref.v0_ref, f32[32,4096]{1,0:T(8,128)S(1)} %get-tuple-element.61.v1_ref, f32[32,4096]{1,0:T(8,128)S(1)} %get-tuple-element.62.r_ref, ...), custom_call_target="tpu_custom_call" | custom-call | flops 2000000000 | bytes 5787648 | tf_op jit(solution)/shard_map/pallas_call | solution.py:406
  39.7 0.0 collective-permute-done.4.yl_ref
  39.7 0.0 collective-permute-done.5.yh_ref
  39.8 0.2 shard_map.110
  40.0 0.0 collective-permute-start.8
  40.0 2.9 %collective-permute-start.9 = (f32[36,128]{1,0:T(8,128)S(1)}, f32[36,128]{1,0:T(8,128)S(1)}, u32[]{:S(2)}, u32[]{:S(2)}) collective-permute-start(f32[36,128]{1,0:T(8,128)S(1)} %get-tuple-element.84), channel_id=1, source_target_pairs={{0,15},{1,0},{2,1},{3,2},{4,3},{5,4},{6,5},{7,6},{8,7},{9,8},{10,9... | collective-permute-start | bytes 55304 | tf_op jit(solution)/shard_map/ppermute | solution.py:427
  42.9 2.4 %collective-permute-start.6 = (f32[72,128]{1,0:T(8,128)S(1)}, f32[72,128]{1,0:T(8,128)S(1)}, u32[]{:S(2)}, u32[]{:S(2)}) collective-permute-start(f32[72,128]{1,0:T(8,128)S(1)} %get-tuple-element.81), channel_id=1, source_target_pairs={{0,16},{16,32},{32,48},{48,64},{64,80},{80,96},{96,112},{112,128},... | collective-permute-start | bytes 110600 | tf_op jit(solution)/shard_map/ppermute | solution.py:419
  45.4 5.5 %collective-permute-start.7 = (f32[72,128]{1,0:T(8,128)S(1)}, f32[72,128]{1,0:T(8,128)S(1)}, u32[]{:S(2)}, u32[]{:S(2)}) collective-permute-start(f32[72,128]{1,0:T(8,128)S(1)} %get-tuple-element.82), channel_id=1, source_target_pairs={{16,0},{32,16},{48,32},{64,48},{80,64},{96,80},{112,96},{128,112},... | collective-permute-start | bytes 110600 | tf_op jit(solution)/shard_map/ppermute | solution.py:420
  50.9 2.8 %shard_map.111 = (f32[32,4096]{1,0:T(8,128)S(1)}, f32[32,4096]{1,0:T(8,128)S(1)}, f32[4,32,1024]{2,1,0:T(8,128)S(1)}) custom-call(f32[32,4096]{1,0:T(8,128)S(1)} %get-tuple-element.45.v_ref.v0_ref, f32[32,4096]{1,0:T(8,128)S(1)} %get-tuple-element.75.v2_ref, f32[32,4096]{1,0:T(8,128)S(1)} %get-tuple-element.76.r_ref, ...), custom_call_target="tpu_custom_call" | custom-call | flops 2000000000 | bytes 4575232 | tf_op jit(solution)/shard_map/pallas_call | solution.py:406
  53.7 0.0 collective-permute-done.8.yl_ref
  53.7 0.0 collective-permute-done.9.yh_ref
  53.7 0.0 collective-permute-done.6.xl_ref
  53.7 0.0 collective-permute-done.7.xh_ref
  53.7 2.9 %shard_map.112 = (f32[864,128]{1,0:T(8,128)}, f32[27,4,1024]{2,1,0:T(4,128)}) custom-call(s32[1,1]{1,0:T(1,128)S(6)} %copy.11.count_ref, f32[32,4096]{1,0:T(8,128)S(1)} %get-tuple-element.79.int_ref, f32[32,4096]{1,0:T(8,128)S(1)} %get-tuple-element.80.u_ref, bf16[128,64]{1,0:T(8,128)(2,1)S(1)} %get-tuple-element.55.fh_ref, ...), custom_call_target="tpu_custom_call" | custom-call | bytes 3047428 | tf_op jit(solution)/shard_map/pallas_call | solution.py:406
Async XLA Ops:
  0.6 0.7 %copy-start.7 = (s32[1,1,1024]{2,1,0:T(1,128)S(1)}, s32[1,1,1024]{2,1,0:T(1,128)}, u32[]{:S(2)}) copy-start(s32[1,1,1024]{2,1,0:T(1,128)} %param.12) | copy-start | bytes 12292
  1.3 1.0 %copy-start = (f32[27,4,8,128]{3,2,1,0:T(8,128)S(1)}, f32[27,4,8,128]{3,2,1,0:T(8,128)}, u32[]{:S(2)}) copy-start(f32[27,4,8,128]{3,2,1,0:T(8,128)} %param.9) | copy-start | bytes 1327108
  2.3 1.0 %copy-start.1 = (f32[1,1,4,27,1024]{4,2,3,1,0:T(4,128)S(1)}, f32[1,1,4,27,1024]{4,2,3,1,0:T(4,128)}, u32[]{:S(2)}) copy-start(f32[1,1,4,27,1024]{4,2,3,1,0:T(4,128)} %param.10) | copy-start | bytes 1327108
  3.3 0.9 %copy-start.2 = (bf16[64,1152]{1,0:T(8,128)(2,1)S(1)}, bf16[64,1152]{1,0:T(8,128)(2,1)}, u32[]{:S(2)}) copy-start(bf16[64,1152]{1,0:T(8,128)(2,1)} %constant.2.clone.refs_7_) | copy-start | bytes 442372
  4.3 0.8 %copy-start.3 = (f32[4,27,27]{2,0,1:T(4,128)S(1)}, f32[4,27,27]{2,0,1:T(4,128)}, u32[]{:S(2)}) copy-start(f32[4,27,27]{2,0,1:T(4,128)} %param.16) | copy-start | bytes 34996
  5.1 0.7 %copy-start.4 = (f32[1,1,4,1024]{3,2,1,0:T(4,128)S(1)}, f32[1,1,4,1024]{3,2,1,0:T(4,128)}, u32[]{:S(2)}) copy-start(f32[1,1,4,1024]{3,2,1,0:T(4,128)} %param.11) | copy-start | bytes 49156
  5.8 0.7 %copy-start.5 = (f32[27,27]{1,0:T(8,128)S(1)}, f32[27,27]{1,0:T(8,128)}, u32[]{:S(2)}) copy-start(f32[27,27]{1,0:T(8,128)} %refs_4_.1) | copy-start | bytes 8752
  6.5 0.7 %copy-start.6 = (f32[27,54]{1,0:T(8,128)S(1)}, f32[27,54]{1,0:T(8,128)}, u32[]{:S(2)}) copy-start(f32[27,54]{1,0:T(8,128)} %refs_5_.1) | copy-start | bytes 17500
  8.5 13.9 %collective-permute-start = (f32[36,128]{1,0:T(8,128)S(1)}, f32[36,128]{1,0:T(8,128)S(1)}, u32[]{:S(2)}, u32[]{:S(2)}) collective-permute-start(f32[36,128]{1,0:T(8,128)S(1)} %get-tuple-element.56), channel_id=1, source_target_pairs={{0,1},{1,2},{2,3},{3,4},{4,5},{5,6},{6,7},{7,8},{8,9},{9,10},{10,1... | collective-permute-start | bytes 55304 | tf_op jit(solution)/shard_map/ppermute | solution.py:426
  8.5 13.9 %collective-permute-start.1 = (f32[36,128]{1,0:T(8,128)S(1)}, f32[36,128]{1,0:T(8,128)S(1)}, u32[]{:S(2)}, u32[]{:S(2)}) collective-permute-start(f32[36,128]{1,0:T(8,128)S(1)} %get-tuple-element.57), channel_id=1, source_target_pairs={{0,15},{1,0},{2,1},{3,2},{4,3},{5,4},{6,5},{7,6},{8,7},{9,8},{10,9... | collective-permute-start | bytes 55304 | tf_op jit(solution)/shard_map/ppermute | solution.py:427
  22.6 10.8 %collective-permute-start.2 = (f32[144,128]{1,0:T(8,128)S(1)}, f32[144,128]{1,0:T(8,128)S(1)}, u32[]{:S(2)}, u32[]{:S(2)}) collective-permute-start(f32[144,128]{1,0:T(8,128)S(1)} %get-tuple-element.59), channel_id=1, source_target_pairs={{0,16},{16,32},{32,48},{48,64},{64,80},{80,96},{96,112},{112,128},... | collective-permute-start | bytes 221192 | tf_op jit(solution)/shard_map/ppermute | solution.py:419
  26.1 7.3 %collective-permute-start.3 = (f32[144,128]{1,0:T(8,128)S(1)}, f32[144,128]{1,0:T(8,128)S(1)}, u32[]{:S(2)}, u32[]{:S(2)}) collective-permute-start(f32[144,128]{1,0:T(8,128)S(1)} %get-tuple-element.60.after_ref), channel_id=1, source_target_pairs={{16,0},{32,16},{48,32},{64,48},{80,64},{96,80},{112,96},{128,112},... | collective-permute-start | bytes 221192 | tf_op jit(solution)/shard_map/ppermute | solution.py:420
  33.7 6.1 %collective-permute-start.4 = (f32[36,128]{1,0:T(8,128)S(1)}, f32[36,128]{1,0:T(8,128)S(1)}, u32[]{:S(2)}, u32[]{:S(2)}) collective-permute-start(f32[36,128]{1,0:T(8,128)S(1)} %get-tuple-element.73), channel_id=1, source_target_pairs={{0,1},{1,2},{2,3},{3,4},{4,5},{5,6},{6,7},{7,8},{8,9},{9,10},{10,1... | collective-permute-start | bytes 55304 | tf_op jit(solution)/shard_map/ppermute | solution.py:426
  33.7 6.1 %collective-permute-start.5 = (f32[36,128]{1,0:T(8,128)S(1)}, f32[36,128]{1,0:T(8,128)S(1)}, u32[]{:S(2)}, u32[]{:S(2)}) collective-permute-start(f32[36,128]{1,0:T(8,128)S(1)} %get-tuple-element.74), channel_id=1, source_target_pairs={{0,15},{1,0},{2,1},{3,2},{4,3},{5,4},{6,5},{7,6},{8,7},{9,8},{10,9... | collective-permute-start | bytes 55304 | tf_op jit(solution)/shard_map/ppermute | solution.py:427
  40.0 13.7 %collective-permute-start.8 = (f32[36,128]{1,0:T(8,128)S(1)}, f32[36,128]{1,0:T(8,128)S(1)}, u32[]{:S(2)}, u32[]{:S(2)}) collective-permute-start(f32[36,128]{1,0:T(8,128)S(1)} %get-tuple-element.83), channel_id=1, source_target_pairs={{0,1},{1,2},{2,3},{3,4},{4,5},{5,6},{6,7},{7,8},{8,9},{9,10},{10,1... | collective-permute-start | bytes 55304 | tf_op jit(solution)/shard_map/ppermute | solution.py:426
  40.0 13.7 %collective-permute-start.9 = (f32[36,128]{1,0:T(8,128)S(1)}, f32[36,128]{1,0:T(8,128)S(1)}, u32[]{:S(2)}, u32[]{:S(2)}) collective-permute-start(f32[36,128]{1,0:T(8,128)S(1)} %get-tuple-element.84), channel_id=1, source_target_pairs={{0,15},{1,0},{2,1},{3,2},{4,3},{5,4},{6,5},{7,6},{8,7},{9,8},{10,9... | collective-permute-start | bytes 55304 | tf_op jit(solution)/shard_map/ppermute | solution.py:427
  42.9 10.8 %collective-permute-start.6 = (f32[72,128]{1,0:T(8,128)S(1)}, f32[72,128]{1,0:T(8,128)S(1)}, u32[]{:S(2)}, u32[]{:S(2)}) collective-permute-start(f32[72,128]{1,0:T(8,128)S(1)} %get-tuple-element.81), channel_id=1, source_target_pairs={{0,16},{16,32},{32,48},{48,64},{64,80},{80,96},{96,112},{112,128},... | collective-permute-start | bytes 110600 | tf_op jit(solution)/shard_map/ppermute | solution.py:419
  45.4 8.3 %collective-permute-start.7 = (f32[72,128]{1,0:T(8,128)S(1)}, f32[72,128]{1,0:T(8,128)S(1)}, u32[]{:S(2)}, u32[]{:S(2)}) collective-permute-start(f32[72,128]{1,0:T(8,128)S(1)} %get-tuple-element.82), channel_id=1, source_target_pairs={{16,0},{32,16},{48,32},{64,48},{80,64},{96,80},{112,96},{128,112},... | collective-permute-start | bytes 110600 | tf_op jit(solution)/shard_map/ppermute | solution.py:420

commit v3 on v2

--- a/solution.py
+++ b/solution.py
@@ -14,7 +14,6 @@
 SLOTS = 1024
 GROUP = 256
 GROUPS = ZONES // GROUP
-HIGHEST = lax.Precision.HIGHEST
 
 
 def face_dofs(face, own):
@@ -61,6 +60,13 @@
 
 def dot(a, b):
     return jnp.dot(a, b, preferred_element_type=F32)
+
+
+def product(a, b):
+    a_hi, a_lo = halves(a)
+    b_hi, b_lo = halves(b)
+    left = jnp.concatenate([a_hi, a_lo], axis=1)
+    return dot(left, jnp.concatenate([b_hi, b_hi], axis=0)) + dot(a_hi, b_lo)
 
 
 def block(r):
@@ -97,12 +103,15 @@
 
 
 def to_slots(r_ref, hot, idx):
+    group = lax.shift_right_logical(idx, 8)
+    parts = []
+    for g in range(GROUPS):
+        parts += halves(r_ref[:, g * GROUP:(g + 1) * GROUP])
+    taken = dot(jnp.concatenate(parts, axis=0), hot)
     total = jnp.zeros((32, SLOTS), F32)
-    group = lax.shift_right_logical(idx, 8)
     for g in range(GROUPS):
-        hi, lo = halves(r_ref[:, g * GROUP:(g + 1) * GROUP])
-        both = dot(jnp.concatenate([hi, lo], axis=0), hot)
-        total = jnp.where(group == g, both[0:32] + both[32:64], total)
+        both = taken[64 * g:64 * g + 32] + taken[64 * g + 32:64 * g + 64]
+        total = jnp.where(group == g, both, total)
     return total
 
 
@@ -136,7 +145,8 @@
     small_ref[...] = jnp.zeros((32, 128), F32)
     small_ref[0:27, 0:54] = face_ref[...]
     f_hi, f_lo = halves(small_ref[:, 0:64])
-    laid = dot(f_hi, sel_ref[...]) + dot(f_lo, sel_ref[...])
+    sel = sel_ref[...].astype(BF16)
+    laid = dot(f_hi, sel) + dot(f_lo, sel)
     small_ref[...] = jnp.zeros((32, 128), F32)
     small_ref[0:27, 0:27] = vol_ref[...]
     vol = small_ref[...]
@@ -158,10 +168,10 @@
     row = lax.broadcasted_iota(jnp.int32, (128, 128), 0)
     column = lax.broadcasted_iota(jnp.int32, (128, 128), 1)
     eye = jnp.where(row == column, 1.0, 0.0)
-    m2 = jnp.dot(m1, m1, precision=HIGHEST)
-    p1 = eye + m1 + m2 + jnp.dot(m1 + m2, m2, precision=HIGHEST)
-    p2 = jnp.dot(p1, p1, precision=HIGHEST)
-    p3 = jnp.dot(p2, p1, precision=HIGHEST)
+    m2 = product(m1, m1)
+    p1 = eye + m1 + m2 + product(m1 + m2, m2)
+    p2 = product(p1, p1)
+    p3 = product(p2, p1)
     q2 = 0.75 * eye + 0.25 * p2
     q3 = (1.0 / 3.0) * eye + 0.5 * p1 + (1.0 / 6.0) * p3
 
@@ -194,35 +204,35 @@
         c_ref[32 * k:32 * k + 32, :] = jnp.where(live, sums[k + 1], 0.0)
 
     hot = lane_hot(idx)
+    dense = to_zones(first, hot, idx)
     for g in range(GROUPS):
         cols = slice(g * GROUP, (g + 1) * GROUP)
-        dense = to_zones(stack_pair(first), hot, idx, g)
-        u_ref[:, cols] = jnp.where(dense[27:28] > 0.0, dense, v_ref[:, cols])
-        fm_ref[:, cols] = dense[24:32]
-
-
-def stack_pair(x):
-    return jnp.concatenate(halves(x), axis=0)
-
-
-def to_zones(both, hot, idx, g):
-    here = jnp.where(lax.shift_right_logical(idx, 8) == g, 1.0, 0.0).astype(BF16)
+        here = dense[g]
+        u_ref[:, cols] = jnp.where(here[27:28] > 0.0, here, v_ref[:, cols])
+        fm_ref[:, cols] = here[24:32]
+
+
+def to_zones(values, hot, idx):
+    both = jnp.concatenate(halves(values), axis=0)
+    group = lax.shift_right_logical(idx, 8)
+    parts = [both * jnp.where(group == g, 1.0, 0.0).astype(BF16) for g in range(GROUPS)]
     dense = lax.dot_general(
-        both * here, hot, (((1,), (1,)), ((), ())), preferred_element_type=F32
-    )
-    rows = both.shape[0] // 2
-    return dense[0:rows] + dense[rows:]
+        jnp.concatenate(parts, axis=0), hot, (((1,), (1,)), ((), ())), preferred_element_type=F32
+    )
+    rows = values.shape[0]
+    return [
+        dense[2 * rows * g:2 * rows * g + rows] + dense[2 * rows * g + rows:2 * rows * (g + 1)]
+        for g in range(GROUPS)
+    ]
 
 
 def zones_kernel(after_ref, c_ref, idx_ref, c2_ref, c3_ref):
     idx = idx_ref[...]
-    hot = lane_hot(idx)
-    both = stack_pair(c_ref[...])
+    dense = to_zones(c_ref[...], lane_hot(idx), idx)
     for g in range(GROUPS):
         cols = slice(g * GROUP, (g + 1) * GROUP)
-        dense = to_zones(both, hot, idx, g)
-        c2_ref[:, cols] = dense[0:32]
-        c3_ref[:, cols] = dense[32:64]
+        c2_ref[:, cols] = dense[g][0:32]
+        c3_ref[:, cols] = dense[g][32:64]
 
 
 def inside(axis):
@@ -393,6 +403,7 @@
 VMEM = pl.BlockSpec(memory_space=pltpu.VMEM)
 SMEM = pl.BlockSpec(memory_space=pltpu.SMEM)
 ANY = pl.BlockSpec(memory_space=pl.ANY)
+HBM = pl.BlockSpec(memory_space=pltpu.HBM)
 DENSE = jax.ShapeDtypeStruct((32, ZONES), F32)
 X_FACES = [jax.ShapeDtypeStruct((72, 128), F32)] * 2
 X_TWICE = [jax.ShapeDtypeStruct((144, 128), F32)] * 2
@@ -400,7 +411,7 @@
 SLOT3 = jax.ShapeDtypeStruct((4, 32, SLOTS), F32)
 
 
-def call(kernel, outs, args, scratch=(), smem=0, flops=0, in_spec=VMEM, out_spec=VMEM):
+def call(kernel, outs, args, scratch=(), smem=0, flops=0, in_spec=VMEM, out_spec=VMEM, vmem=48):
     specs = [SMEM] * smem + [in_spec] * (len(args) - smem)
     moved = 4 * sum(int(np.prod(a.shape)) for a in list(args) + list(outs))
     return pl.pallas_call(
@@ -409,7 +420,7 @@
         in_specs=specs,
         out_specs=[out_spec] * len(outs),
         scratch_shapes=list(scratch),
-        compiler_params=pltpu.CompilerParams(vmem_limit_bytes=48 * 1024 * 1024),
+        compiler_params=pltpu.CompilerParams(vmem_limit_bytes=vmem * 1024 * 1024),
         cost_estimate=pl.CostEstimate(flops=flops, bytes_accessed=moved, transcendentals=0),
     )(*args)
 
@@ -439,7 +450,7 @@
         vol_matrix,
         face_matrix,
         mat_matrix.transpose(1, 0, 2),
-        jnp.asarray(selections(), BF16),
+        jnp.asarray(selections()),
     ]
     count = mix_count.reshape(1, 1)
     g_space = pltpu.VMEM((224, ZONES), F32)
@@ -450,9 +461,9 @@
     v0, *out = call(
         first_kernel,
         [DENSE] + Y_FACES + [jax.ShapeDtypeStruct(a.shape, a.dtype) for a in small],
-        [flat] + small,
+        [pltpu.with_memory_space_constraint(a, pltpu.HBM) for a in [flat] + small],
         [pltpu.VMEM((27 * ROWS, CZ), F32), pltpu.SemaphoreType.DMA((8,))],
-        in_spec=ANY,
+        in_spec=HBM,
     )
     halo = exchange_y(*out[:2])
     small = out[2:]

time: 57.2 us -> 46.5 us (0.81)
  the two profiles are of different devices: /device:TPU:6 before, /device:TPU:18 now
where the time goes in v3:
time: 46.5 us; the launch traced here: 46.2 us
  starting transfers between devices  27.3 us (59%)
  Pallas kernels  12.1 us (26%)
  waiting for transfers between devices  5.36 us (12%)
  between operations  1.45 us (3%)
    ppermute x3, starting transfers between devices, exchange_y(): above = lax.ppermute(low, 'yz', [(i, (i - 1) % n) for i in range(n)])  14.4 us
    pallas_call x9, Pallas kernels, call(): pl.pallas_call(kernel, out_shape=outs, in_specs=specs, out_specs=[out_spe...  12.1 us
    ppermute x2, starting transfers between devices, exchange_x(): below = lax.ppermute(high, 'gx', [(i, i + 1) for i in range(n - 1)])  8.6 us
    ppermute x2, waiting for transfers between devices, exchange_x(): above = lax.ppermute(low, 'gx', [(i + 1, i) for i in range(n - 1)])  5.34 us
    ppermute x2, starting transfers between devices, exchange_x(): above = lax.ppermute(low, 'gx', [(i + 1, i) for i in range(n - 1)])  4.28 us
  transfers between devices with their start and end apart: 10, of which 2 were waited for; matrix products, arithmetic and copies ran while one was open for 0% of the time, Pallas kernels for 17%

profile of v3, /device:TPU:18, one launch (start us, length us, event | category | flops | bytes accessed | tf_op | source)
XLA Modules:
  0.0 46.2 jit_solution(7053454424064473628)
XLA Ops:
  0.6 1.4 %shard_map.104 = (f32[32,4096]{1,0:T(8,128)S(1)}, f32[36,128]{1,0:T(8,128)S(1)}, f32[36,128]{1,0:T(8,128)S(1)}, f32[27,4,1024]{2,1,0:T(4,128)S(1)}, f32[4,1024]{...) custom-call(f32[864,128]{1,0:T(8,128)} %bitcast.11, ...), custom_call_target="tpu_custom_call" | custom-call | bytes 2559864 | tf_op jit(solution)/shard_map/pallas_call | solution.py:417
  2.0 0.0 collective-permute-start
  2.1 8.5 %collective-permute-start.1 = (f32[36,128]{1,0:T(8,128)S(1)}, f32[36,128]{1,0:T(8,128)S(1)}, u32[]{:S(2)}, u32[]{:S(2)}) collective-permute-start(f32[36,128]{1,0:T(8,128)S(1)} %get-tuple-element.57), channel_id=1, source_target_pairs={{0,15},{1,0},{2,1},{3,2},{4,3},{5,4},{6,5},{7,6},{8,7},{9,8},{10,9... | collective-permute-start | bytes 55304 | tf_op jit(solution)/shard_map/ppermute | solution.py:438
  11.2 2.7 %shard_map.105 = (f32[32,4096]{1,0:T(8,128)S(1)}, f32[32,4096]{1,0:T(8,128)S(1)}, f32[8,4096]{1,0:T(8,128)S(1)}, bf16[224,128]{1,0:T(8,128)(2,1)S(1)}, bf16[128,...) custom-call(s32[1,1]{1,0:T(1,128)S(6)} %copy.11.count_ref, ...), custom_call_target="tpu_custom_call" | custom-call | flops 3000000000 | bytes 3547072 | tf_op jit(solution)/shard_map/pallas_call | solution.py:417
  13.9 0.0 collective-permute-done.yl_ref
  13.9 0.0 collective-permute-done.1.yh_ref
  13.9 0.2 shard_map.106
  14.1 3.5 %collective-permute-start.2 = (f32[144,128]{1,0:T(8,128)S(1)}, f32[144,128]{1,0:T(8,128)S(1)}, u32[]{:S(2)}, u32[]{:S(2)}) collective-permute-start(f32[144,128]{1,0:T(8,128)S(1)} %get-tuple-element.59), channel_id=1, source_target_pairs={{0,16},{16,32},{32,48},{48,64},{64,80},{80,96},{96,112},{112,128},... | collective-permute-start | bytes 221192 | tf_op jit(solution)/shard_map/ppermute | solution.py:430
  17.6 2.4 %collective-permute-start.3 = (f32[144,128]{1,0:T(8,128)S(1)}, f32[144,128]{1,0:T(8,128)S(1)}, u32[]{:S(2)}, u32[]{:S(2)}) collective-permute-start(f32[144,128]{1,0:T(8,128)S(1)} %get-tuple-element.60.after_ref), channel_id=1, source_target_pairs={{16,0},{32,16},{48,32},{64,48},{80,64},{96,80},{112,96},{128,112},... | collective-permute-start | bytes 221192 | tf_op jit(solution)/shard_map/ppermute | solution.py:431
  19.9 1.3 %shard_map.108 = (f32[32,4096]{1,0:T(8,128)S(1)}, f32[32,4096]{1,0:T(8,128)S(1)}) custom-call(f32[144,128]{1,0:T(8,128)S(1)} %get-tuple-element.60.after_ref, f32[64,1024]{1,0:T(8,128)S(1)} %get-tuple-element.64.c_ref, s32[1,1024]{1,0:T(1,128)S(1)} %get-tuple-element.48.idx_ref), custom_call_target="tpu_custom_call" | custom-call | flops 2000000000 | bytes 1388544 | tf_op jit(solution)/shard_map/pallas_call | solution.py:417
  21.2 0.0 collective-permute-done.2.xl_ref
  21.2 3.4 %collective-permute-done.3.xh_ref = f32[144,128]{1,0:T(8,128)S(1)} collective-permute-done((f32[144,128]{1,0:T(8,128)S(1)}, f32[144,128]{1,0:T(8,128)S(1)}, u32[]{:S(2)}, u32[]{:S(2)}) %collective-permute-start.3) | collective-permute-done | bytes 73760 | tf_op jit(solution)/shard_map/ppermute | solution.py:431
  24.6 0.2 shard_map.107
  24.8 0.0 collective-permute-start.4
  24.9 2.9 %collective-permute-start.5 = (f32[36,128]{1,0:T(8,128)S(1)}, f32[36,128]{1,0:T(8,128)S(1)}, u32[]{:S(2)}, u32[]{:S(2)}) collective-permute-start(f32[36,128]{1,0:T(8,128)S(1)} %get-tuple-element.74), channel_id=1, source_target_pairs={{0,15},{1,0},{2,1},{3,2},{4,3},{5,4},{6,5},{7,6},{8,7},{9,8},{10,9... | collective-permute-start | bytes 55304 | tf_op jit(solution)/shard_map/ppermute | solution.py:438
  27.8 2.2 %shard_map.109 = (f32[32,4096]{1,0:T(8,128)S(1)}, f32[32,4096]{1,0:T(8,128)S(1)}, f32[32,4096]{1,0:T(8,128)S(1)}, f32[4,32,1024]{2,1,0:T(8,128)S(1)}) custom-call(f32[32,4096]{1,0:T(8,128)S(1)} %get-tuple-element.45.v_ref.v0_ref, f32[32,4096]{1,0:T(8,128)S(1)} %get-tuple-element.61.v1_ref, f32[32,4096]{1,0:T(8,128)S(1)} %get-tuple-element.62.r_ref, ...), custom_call_target="tpu_custom_call" | custom-call | flops 2000000000 | bytes 5787648 | tf_op jit(solution)/shard_map/pallas_call | solution.py:417
  30.0 0.0 collective-permute-done.4.yl_ref
  30.0 0.0 collective-permute-done.5.yh_ref
  30.0 0.2 shard_map.110
  30.2 0.0 collective-permute-start.8
  30.3 2.9 %collective-permute-start.9 = (f32[36,128]{1,0:T(8,128)S(1)}, f32[36,128]{1,0:T(8,128)S(1)}, u32[]{:S(2)}, u32[]{:S(2)}) collective-permute-start(f32[36,128]{1,0:T(8,128)S(1)} %get-tuple-element.84), channel_id=1, source_target_pairs={{0,15},{1,0},{2,1},{3,2},{4,3},{5,4},{6,5},{7,6},{8,7},{9,8},{10,9... | collective-permute-start | bytes 55304 | tf_op jit(solution)/shard_map/ppermute | solution.py:438
  33.2 5.1 %collective-permute-start.6 = (f32[72,128]{1,0:T(8,128)S(1)}, f32[72,128]{1,0:T(8,128)S(1)}, u32[]{:S(2)}, u32[]{:S(2)}) collective-permute-start(f32[72,128]{1,0:T(8,128)S(1)} %get-tuple-element.81), channel_id=1, source_target_pairs={{0,16},{16,32},{32,48},{48,64},{64,80},{80,96},{96,112},{112,128},... | collective-permute-start | bytes 110600 | tf_op jit(solution)/shard_map/ppermute | solution.py:430
  38.3 1.9 %collective-permute-start.7 = (f32[72,128]{1,0:T(8,128)S(1)}, f32[72,128]{1,0:T(8,128)S(1)}, u32[]{:S(2)}, u32[]{:S(2)}) collective-permute-start(f32[72,128]{1,0:T(8,128)S(1)} %get-tuple-element.82), channel_id=1, source_target_pairs={{16,0},{32,16},{48,32},{64,48},{80,64},{96,80},{112,96},{128,112},... | collective-permute-start | bytes 110600 | tf_op jit(solution)/shard_map/ppermute | solution.py:431
  40.3 1.9 %shard_map.111 = (f32[32,4096]{1,0:T(8,128)S(1)}, f32[32,4096]{1,0:T(8,128)S(1)}, f32[4,32,1024]{2,1,0:T(8,128)S(1)}) custom-call(f32[32,4096]{1,0:T(8,128)S(1)} %get-tuple-element.45.v_ref.v0_ref, f32[32,4096]{1,0:T(8,128)S(1)} %get-tuple-element.75.v2_ref, f32[32,4096]{1,0:T(8,128)S(1)} %get-tuple-element.76.r_ref, ...), custom_call_target="tpu_custom_call" | custom-call | flops 2000000000 | bytes 4575232 | tf_op jit(solution)/shard_map/pallas_call | solution.py:417
  42.2 0.0 collective-permute-done.8.yl_ref
  42.2 0.0 collective-permute-done.9.yh_ref
  42.2 0.0 collective-permute-done.6.xl_ref
  42.2 2.0 %collective-permute-done.7.xh_ref = f32[72,128]{1,0:T(8,128)S(1)} collective-permute-done((f32[72,128]{1,0:T(8,128)S(1)}, f32[72,128]{1,0:T(8,128)S(1)}, u32[]{:S(2)}, u32[]{:S(2)}) %collective-permute-start.7) | collective-permute-done | bytes 36896 | tf_op jit(solution)/shard_map/ppermute | solution.py:431
  44.2 2.1 %shard_map.112 = (f32[864,128]{1,0:T(8,128)}, f32[27,4,1024]{2,1,0:T(4,128)}) custom-call(s32[1,1]{1,0:T(1,128)S(6)} %copy.11.count_ref, f32[32,4096]{1,0:T(8,128)S(1)} %get-tuple-element.79.int_ref, f32[32,4096]{1,0:T(8,128)S(1)} %get-tuple-element.80.u_ref, bf16[128,64]{1,0:T(8,128)(2,1)S(1)} %get-tuple-element.55.fh_ref, ...), custom_call_target="tpu_custom_call" | custom-call | bytes 3047428 | tf_op jit(solution)/shard_map/pallas_call | solution.py:417
Async XLA Ops:
  2.0 11.8 %collective-permute-start = (f32[36,128]{1,0:T(8,128)S(1)}, f32[36,128]{1,0:T(8,128)S(1)}, u32[]{:S(2)}, u32[]{:S(2)}) collective-permute-start(f32[36,128]{1,0:T(8,128)S(1)} %get-tuple-element.56), channel_id=1, source_target_pairs={{0,1},{1,2},{2,3},{3,4},{4,5},{5,6},{6,7},{7,8},{8,9},{9,10},{10,1... | collective-permute-start | bytes 55304 | tf_op jit(solution)/shard_map/ppermute | solution.py:437
  2.1 11.8 %collective-permute-start.1 = (f32[36,128]{1,0:T(8,128)S(1)}, f32[36,128]{1,0:T(8,128)S(1)}, u32[]{:S(2)}, u32[]{:S(2)}) collective-permute-start(f32[36,128]{1,0:T(8,128)S(1)} %get-tuple-element.57), channel_id=1, source_target_pairs={{0,15},{1,0},{2,1},{3,2},{4,3},{5,4},{6,5},{7,6},{8,7},{9,8},{10,9... | collective-permute-start | bytes 55304 | tf_op jit(solution)/shard_map/ppermute | solution.py:438
  14.1 7.2 %collective-permute-start.2 = (f32[144,128]{1,0:T(8,128)S(1)}, f32[144,128]{1,0:T(8,128)S(1)}, u32[]{:S(2)}, u32[]{:S(2)}) collective-permute-start(f32[144,128]{1,0:T(8,128)S(1)} %get-tuple-element.59), channel_id=1, source_target_pairs={{0,16},{16,32},{32,48},{48,64},{64,80},{80,96},{96,112},{112,128},... | collective-permute-start | bytes 221192 | tf_op jit(solution)/shard_map/ppermute | solution.py:430
  17.6 7.0 %collective-permute-start.3 = (f32[144,128]{1,0:T(8,128)S(1)}, f32[144,128]{1,0:T(8,128)S(1)}, u32[]{:S(2)}, u32[]{:S(2)}) collective-permute-start(f32[144,128]{1,0:T(8,128)S(1)} %get-tuple-element.60.after_ref), channel_id=1, source_target_pairs={{16,0},{32,16},{48,32},{64,48},{80,64},{96,80},{112,96},{128,112},... | collective-permute-start | bytes 221192 | tf_op jit(solution)/shard_map/ppermute | solution.py:431
  24.8 5.2 %collective-permute-start.4 = (f32[36,128]{1,0:T(8,128)S(1)}, f32[36,128]{1,0:T(8,128)S(1)}, u32[]{:S(2)}, u32[]{:S(2)}) collective-permute-start(f32[36,128]{1,0:T(8,128)S(1)} %get-tuple-element.73), channel_id=1, source_target_pairs={{0,1},{1,2},{2,3},{3,4},{4,5},{5,6},{6,7},{7,8},{8,9},{9,10},{10,1... | collective-permute-start | bytes 55304 | tf_op jit(solution)/shard_map/ppermute | solution.py:437
  24.9 5.2 %collective-permute-start.5 = (f32[36,128]{1,0:T(8,128)S(1)}, f32[36,128]{1,0:T(8,128)S(1)}, u32[]{:S(2)}, u32[]{:S(2)}) collective-permute-start(f32[36,128]{1,0:T(8,128)S(1)} %get-tuple-element.74), channel_id=1, source_target_pairs={{0,15},{1,0},{2,1},{3,2},{4,3},{5,4},{6,5},{7,6},{8,7},{9,8},{10,9... | collective-permute-start | bytes 55304 | tf_op jit(solution)/shard_map/ppermute | solution.py:438
  30.2 11.9 %collective-permute-start.8 = (f32[36,128]{1,0:T(8,128)S(1)}, f32[36,128]{1,0:T(8,128)S(1)}, u32[]{:S(2)}, u32[]{:S(2)}) collective-permute-start(f32[36,128]{1,0:T(8,128)S(1)} %get-tuple-element.83), channel_id=1, source_target_pairs={{0,1},{1,2},{2,3},{3,4},{4,5},{5,6},{6,7},{7,8},{8,9},{9,10},{10,1... | collective-permute-start | bytes 55304 | tf_op jit(solution)/shard_map/ppermute | solution.py:437
  30.3 11.9 %collective-permute-start.9 = (f32[36,128]{1,0:T(8,128)S(1)}, f32[36,128]{1,0:T(8,128)S(1)}, u32[]{:S(2)}, u32[]{:S(2)}) collective-permute-start(f32[36,128]{1,0:T(8,128)S(1)} %get-tuple-element.84), channel_id=1, source_target_pairs={{0,15},{1,0},{2,1},{3,2},{4,3},{5,4},{6,5},{7,6},{8,7},{9,8},{10,9... | collective-permute-start | bytes 55304 | tf_op jit(solution)/shard_map/ppermute | solution.py:438
  33.2 9.0 %collective-permute-start.6 = (f32[72,128]{1,0:T(8,128)S(1)}, f32[72,128]{1,0:T(8,128)S(1)}, u32[]{:S(2)}, u32[]{:S(2)}) collective-permute-start(f32[72,128]{1,0:T(8,128)S(1)} %get-tuple-element.81), channel_id=1, source_target_pairs={{0,16},{16,32},{32,48},{48,64},{64,80},{80,96},{96,112},{112,128},... | collective-permute-start | bytes 110600 | tf_op jit(solution)/shard_map/ppermute | solution.py:430
  38.3 5.9 %collective-permute-start.7 = (f32[72,128]{1,0:T(8,128)S(1)}, f32[72,128]{1,0:T(8,128)S(1)}, u32[]{:S(2)}, u32[]{:S(2)}) collective-permute-start(f32[72,128]{1,0:T(8,128)S(1)} %get-tuple-element.82), channel_id=1, source_target_pairs={{16,0},{32,16},{48,32},{64,48},{80,64},{96,80},{112,96},{128,112},... | collective-permute-start | bytes 110600 | tf_op jit(solution)/shard_map/ppermute | solution.py:431

commit v4 on v3

--- a/solution.py
+++ b/solution.py
@@ -29,7 +29,7 @@
 
 
 def selections():
-    sel = np.zeros((64, 7 * 128 + 4 * 64), np.float32)
+    sel = np.zeros((64, 7 * 128 + 2 * 256), np.float32)
     for face in range(6):
         for q in range(9):
             row = 9 * face + q
@@ -38,6 +38,7 @@
                 sel[row, (face + 1) * 128 + copy * 32 + face_dofs(face, False)[q]] += 1.0
                 if face < 4:
                     sel[row, 7 * 128 + face * 64 + copy * 16 + q] += 1.0
+                    sel[row, 9 * 128 + copy * 64 + face * 16 + q] += 1.0
     return sel
 
 
@@ -139,7 +140,7 @@
 
 def mixed_kernel(
     count_ref, v_ref, w_ref, frac_ref, idx_ref, vol_ref, face_ref, mat_ref, sel_ref,
-    int_ref, u_ref, fm_ref, wg_ref, fh_ref, pp_ref, b3_ref, c_ref,
+    int_ref, u_ref, fm_ref, wg_ref, fh_ref, fs_ref, power_ref,
     g_ref, small_ref, diag_ref, wpad_ref,
 ):
     small_ref[...] = jnp.zeros((32, 128), F32)
@@ -158,6 +159,7 @@
     for k in range(4):
         first = 7 * 128 + 64 * k
         fh_ref[32 * k:32 * k + 32, :] = stack_left(laid[:, first:first + 64], 32)
+    fs_ref[...] = stack_left(laid[:, 9 * 128:11 * 128], 128)
     interior(v_ref, wg_ref, g_ref, int_ref)
 
     for m in range(4):
@@ -165,51 +167,45 @@
         small = small_ref[...]
         diag_ref[32 * m:32 * m + 32, :] = pltpu.roll(small, 32 * m, 1) if m else small
     m1 = diag_ref[...]
-    row = lax.broadcasted_iota(jnp.int32, (128, 128), 0)
-    column = lax.broadcasted_iota(jnp.int32, (128, 128), 1)
-    eye = jnp.where(row == column, 1.0, 0.0)
     m2 = product(m1, m1)
-    p1 = eye + m1 + m2 + product(m1 + m2, m2)
-    p2 = product(p1, p1)
-    p3 = product(p2, p1)
-    q2 = 0.75 * eye + 0.25 * p2
-    q3 = (1.0 / 3.0) * eye + 0.5 * p1 + (1.0 / 6.0) * p3
-
-    def stacked(matrix, m):
-        rows = matrix[32 * m:32 * m + 32, :]
-        for shift in (32, 64):
-            rows = rows + pltpu.roll(rows, shift, 1)
-        return stack_left(rows, 64)
-
-    for m in range(4):
-        pp_ref[32 * m:32 * m + 32, :] = stacked(p1, m)
-        pp_ref[128 + 32 * m:128 + 32 * m + 32, :] = stacked(p2, m)
+    p1 = identity() + m1 + m2 + product(m1 + m2, m2)
+    power_ref[...] = p1
 
     idx = idx_ref[...]
-    slot = lax.broadcasted_iota(jnp.int32, (1, SLOTS), 1)
-    live = slot < count_ref[0, 0]
     frac = frac_ref[...]
     wpad_ref[...] = jnp.zeros((32, SLOTS), F32)
-    sums = [0.0, 0.0, 0.0]
+    first = 0.0
     for m in range(4):
         wpad_ref[0:27, :] = w_ref[:, m, :]
-        left = jnp.concatenate([stacked(p1, m), stacked(q2, m), stacked(q3, m)], axis=0)
-        values = dot(left, stack_right(wpad_ref[...]))
-        for k in range(3):
-            sums[k] = sums[k] + frac[m:m + 1, :] * values[32 * k:32 * k + 32]
-        b3_ref[m] = values[64:96]
-    first = jnp.where(live, sums[0], 0.0)
+        values = dot(stacked(p1, m), stack_right(wpad_ref[...]))
+        first = first + frac[m:m + 1, :] * values
+    live = slots_live(count_ref)
+    first = jnp.where(live, first, 0.0)
     first = jnp.concatenate([first[0:27], jnp.where(live, frac, 0.0), first[31:32]], axis=0)
-    for k in range(2):
-        c_ref[32 * k:32 * k + 32, :] = jnp.where(live, sums[k + 1], 0.0)
-
-    hot = lane_hot(idx)
-    dense = to_zones(first, hot, idx)
+
+    dense = to_zones(first, lane_hot(idx), idx)
     for g in range(GROUPS):
         cols = slice(g * GROUP, (g + 1) * GROUP)
         here = dense[g]
         u_ref[:, cols] = jnp.where(here[27:28] > 0.0, here, v_ref[:, cols])
         fm_ref[:, cols] = here[24:32]
+
+
+def identity():
+    row = lax.broadcasted_iota(jnp.int32, (128, 128), 0)
+    column = lax.broadcasted_iota(jnp.int32, (128, 128), 1)
+    return jnp.where(row == column, 1.0, 0.0)
+
+
+def slots_live(count_ref):
+    return lax.broadcasted_iota(jnp.int32, (1, SLOTS), 1) < count_ref[0, 0]
+
+
+def stacked(matrix, m):
+    rows = matrix[32 * m:32 * m + 32, :]
+    for shift in (32, 64):
+        rows = rows + pltpu.roll(rows, shift, 1)
+    return stack_left(rows, 64)
 
 
 def to_zones(values, hot, idx):
@@ -226,9 +222,28 @@
     ]
 
 
-def zones_kernel(after_ref, c_ref, idx_ref, c2_ref, c3_ref):
+def later_kernel(
+    count_ref, after_ref, power_ref, w_ref, frac_ref, idx_ref,
+    c2_ref, c3_ref, pp_ref, b3_ref, wpad_ref,
+):
+    eye = identity()
+    p1 = power_ref[...]
+    p2 = product(p1, p1)
+    q2 = 0.75 * eye + 0.25 * p2
+    q3 = (1.0 / 3.0) * eye + 0.5 * p1 + (1.0 / 6.0) * product(p2, p1)
+    frac = frac_ref[...]
+    wpad_ref[...] = jnp.zeros((32, SLOTS), F32)
+    total = 0.0
+    for m in range(4):
+        pp_ref[32 * m:32 * m + 32, :] = stacked(p1, m)
+        pp_ref[128 + 32 * m:160 + 32 * m, :] = stacked(p2, m)
+        wpad_ref[0:27, :] = w_ref[:, m, :]
+        left = jnp.concatenate([stacked(q2, m), stacked(q3, m)], axis=0)
+        values = dot(left, stack_right(wpad_ref[...]))
+        b3_ref[m] = values[32:64]
+        total = total + frac[m:m + 1, :] * values
     idx = idx_ref[...]
-    dense = to_zones(c_ref[...], lane_hot(idx), idx)
+    dense = to_zones(jnp.where(slots_live(count_ref), total, 0.0), lane_hot(idx), idx)
     for g in range(GROUPS):
         cols = slice(g * GROUP, (g + 1) * GROUP)
         c2_ref[:, cols] = dense[g][0:32]
@@ -360,7 +375,7 @@
 
 def between_two(
     v0_ref, v2_ref, r_ref, c3_ref, fm_ref, idx_ref, wg_ref, pp_ref, b3_ref,
-    int_ref, u_ref, b3_out, g_ref,
+    u_ref, b3_out, g_ref, int_ref,
 ):
     interior(v2_ref, wg_ref, g_ref, int_ref)
     for x in range(CX):
@@ -369,31 +384,53 @@
         f = fm_ref[:, cols]
         s1 = sum(f[m + 3:m + 4] * q[32 * m:32 * m + 32] for m in range(4))
         bulk = (1.0 / 3.0) * v0_ref[:, cols] + (2.0 / 3.0) * v2_ref[:, cols]
-        u_ref[:, cols] = jnp.where(f[3:4] > 0.0, c3_ref[:, cols] + (1.0 / 6.0) * s1, bulk)
+        old = jnp.where(f[3:4] > 0.0, c3_ref[:, cols] + (1.0 / 6.0) * s1, bulk)
+        u_ref[:, cols] = old + (2.0 / 3.0) * int_ref[:, cols]
     idx = idx_ref[...]
-    at = stack_right(to_slots(r_ref, lane_hot(idx), idx))
+    hot = lane_hot(idx)
+    at = stack_right(to_slots(r_ref, hot, idx))
+    inner = (2.0 / 3.0) * to_slots(int_ref, hot, idx)
     for m in range(4):
-        b3_out[m] = b3_ref[m] + (1.0 / 6.0) * dot(pp_ref[32 * m:32 * m + 32, :], at)
+        b3_out[m] = b3_ref[m] + inner + (1.0 / 6.0) * dot(pp_ref[32 * m:32 * m + 32, :], at)
+
+
+def faces_to_slots(pad_ref, idx):
+    parts = []
+    for g in range(8):
+        parts += halves(pad_ref[:, g * GROUP:(g + 1) * GROUP])
+    for x in range(CX):
+        low, high = pad_ref[:, block(16 + x)], pad_ref[:, block(20 + x)]
+        parts += halves(jnp.concatenate([low, high], axis=1))
+    taken = dot(jnp.concatenate(parts, axis=0), lane_hot(idx))
+    taken = [taken[32 * k:32 * k + 16] + taken[32 * k + 16:32 * k + 32] for k in range(12)]
+    group = lax.shift_right_logical(idx, 8)
+    x, y = lax.shift_right_logical(idx, 10), lax.shift_right_logical(idx, 7) & 7
+    x_low = x_high = beside = jnp.zeros((16, SLOTS), F32)
+    for k in range(4):
+        x_low = jnp.where(group == k, taken[k], x_low)
+        x_high = jnp.where(group == 12 + k, taken[4 + k], x_high)
+        beside = jnp.where(x == k, taken[8 + k], beside)
+    y_low, y_high = jnp.where(y == 0, beside, 0.0), jnp.where(y == CY - 1, beside, 0.0)
+    return jnp.concatenate([x_low, x_high, y_low, y_high], axis=0)
 
 
 def last_kernel(
-    count_ref, int_ref, u_ref, fh_ref, xl_ref, xh_ref, yl_ref, yh_ref, idx_ref, b3_ref, w_ref,
-    field_hbm, out_hbm, pad_ref, rate_ref, field_ref, out_ref, sems,
+    count_ref, u_ref, fh_ref, fs_ref, yl_ref, yh_ref, xl_ref, xh_ref, idx_ref, b3_ref, w_ref,
+    field_hbm, out_hbm, pad_ref, whole_ref, field_ref, out_ref, sems,
 ):
     pad_ref[...] = jnp.zeros((16, 3072), F32)
     halo_x(xl_ref, xh_ref, pad_ref)
     halo_y(yl_ref, yh_ref, pad_ref)
-    halo_add(int_ref, fh_ref, pad_ref, rate_ref, True, True)
+    pad_ref[...] = (2.0 / 3.0) * pad_ref[...]
+    halo_add(u_ref, fh_ref, pad_ref, whole_ref, True, True)
     for r in range(ROWS):
-        value = u_ref[0:27, block(r)] + (2.0 / 3.0) * rate_ref[0:27, block(r)]
-        field_ref[pl.ds(r, 27, stride=32), :] = value
+        field_ref[pl.ds(r, 27, stride=32), :] = whole_ref[0:27, block(r)]
     field_copy = pltpu.make_async_copy(field_ref, field_hbm, sems.at[0])
     field_copy.start()
-    idx = idx_ref[...]
-    at = (2.0 / 3.0) * to_slots(rate_ref, lane_hot(idx), idx)
-    live = lax.broadcasted_iota(jnp.int32, (1, SLOTS), 1) < count_ref[0, 0]
+    added = dot(fs_ref[...], stack_right(faces_to_slots(pad_ref, idx_ref[...])))
+    live = slots_live(count_ref)
     for m in range(4):
-        out_ref[:, m, :] = jnp.where(live, b3_ref[m, 0:27, :] + at[0:27], w_ref[:, m, :])
+        out_ref[:, m, :] = jnp.where(live, b3_ref[m, 0:27, :] + added[0:27], w_ref[:, m, :])
     out_copy = pltpu.make_async_copy(out_ref, out_hbm, sems.at[1])
     out_copy.start()
     field_copy.wait()
@@ -411,16 +448,15 @@
 SLOT3 = jax.ShapeDtypeStruct((4, 32, SLOTS), F32)
 
 
-def call(kernel, outs, args, scratch=(), smem=0, flops=0, in_spec=VMEM, out_spec=VMEM, vmem=48):
-    specs = [SMEM] * smem + [in_spec] * (len(args) - smem)
+def call(kernel, outs, args, scratch=(), smem=0, flops=0, in_spec=VMEM, out_spec=VMEM):
     moved = 4 * sum(int(np.prod(a.shape)) for a in list(args) + list(outs))
     return pl.pallas_call(
         kernel,
         out_shape=outs,
-        in_specs=specs,
+        in_specs=[SMEM] * smem + [in_spec] * (len(args) - smem),
         out_specs=[out_spec] * len(outs),
         scratch_shapes=list(scratch),
-        compiler_params=pltpu.CompilerParams(vmem_limit_bytes=vmem * 1024 * 1024),
+        compiler_params=pltpu.CompilerParams(vmem_limit_bytes=48 * 1024 * 1024),
         cost_estimate=pl.CostEstimate(flops=flops, bytes_accessed=moved, transcendentals=0),
     )(*args)
 
@@ -466,11 +502,10 @@
         in_spec=HBM,
     )
     halo = exchange_y(*out[:2])
-    small = out[2:]
-    weights, idx = small[0], small[2]
-    inner, u, fm, wg, fh, pp, b3, rest = call(
+    weights, frac, idx, *_ = small = out[2:]
+    inner, u, fm, wg, fh, fs, power = call(
         mixed_kernel,
-        [DENSE, DENSE, f32(8, ZONES), bf(224, 128), bf(128, 64), bf(256, 128), SLOT3, f32(64, SLOTS)],
+        [DENSE, DENSE, f32(8, ZONES), bf(224, 128), bf(128, 64), bf(32, 256), f32(128, 128)],
         [count, v0] + small,
         [g_space, pltpu.VMEM((32, 128), F32), pltpu.VMEM((128, 128), F32),
          pltpu.VMEM((32, SLOTS), F32)],
@@ -480,7 +515,11 @@
         y_first_kernel, [DENSE] + X_TWICE, [inner, u, v0, fh, *halo], [pad]
     )
     halo = exchange_x(*faces)
-    c2, c3 = call(zones_kernel, [DENSE, DENSE], [faces[0], rest, idx], flops=2 * 10**9)
+    c2, c3, pp, b3 = call(
+        later_kernel, [DENSE, DENSE, bf(256, 128), SLOT3],
+        [count, faces[0], power, weights, frac, idx], [pltpu.VMEM((32, SLOTS), F32)],
+        smem=1, flops=2 * 10**9,
+    )
     v1, r0, beside, *faces = call(
         x_first_kernel, [DENSE, DENSE, f32(16, 2048)] + Y_FACES, [inner, u, v0, fh, *halo],
         [pad, pltpu.VMEM((16, 2048), F32)],
@@ -493,16 +532,17 @@
     v2, r1, *faces = call(
         second_kernel, [DENSE, DENSE] + X_FACES + Y_FACES, [inner, u, fh, *halo], [pad]
     )
+    x_halo = exchange_x(*faces[:2])
     y_halo = exchange_y(*faces[2:])
-    x_halo = exchange_x(*faces[:2])
-    inner, u, b3 = call(
-        between_two, [DENSE, DENSE, SLOT3],
-        [v0, v2, r1, c3, fm, idx, wg, pp, b3], [g_space], flops=2 * 10**9,
+    u, b3 = call(
+        between_two, [DENSE, SLOT3],
+        [v0, v2, r1, c3, fm, idx, wg, pp, b3], [g_space, pltpu.VMEM((32, ZONES), F32)],
+        flops=2 * 10**9,
     )
     field, out = call(
         last_kernel,
         [jax.ShapeDtypeStruct((27 * ROWS, CZ), F32), jax.ShapeDtypeStruct((27, 4, SLOTS), F32)],
-        [count, inner, u, fh, *x_halo, *y_halo, idx, b3, weights],
+        [count, u, fh, fs, *y_halo, *x_halo, idx, b3, weights],
         [pad, pltpu.VMEM((32, ZONES), F32), pltpu.VMEM((27 * ROWS, CZ), F32),
          pltpu.VMEM((27, 4, SLOTS), F32), pltpu.SemaphoreType.DMA((2,))],
         smem=1, out_spec=ANY,

time: 46.5 us -> 45.8 us (0.985)
  the two profiles are of different devices: /device:TPU:18 before, /device:TPU:6 now
where the time goes in v4:
time: 45.8 us; the launch traced here: 44.9 us
  starting transfers between devices  30.6 us (67%)
  Pallas kernels  12.7 us (28%)
  between operations  1.46 us (3%)
    ppermute x3, starting transfers between devices, exchange_y(): above = lax.ppermute(low, 'yz', [(i, (i - 1) % n) for i in range(n)])  14.4 us
    pallas_call x9, Pallas kernels, call(): pl.pallas_call(kernel, out_shape=outs, in_specs=[SMEM] * smem + [in_spec]...  12.7 us
    ppermute x2, starting transfers between devices, exchange_x(): above = lax.ppermute(low, 'gx', [(i + 1, i) for i in range(n - 1)])  9.5 us
    ppermute x2, starting transfers between devices, exchange_x(): below = lax.ppermute(high, 'gx', [(i, i + 1) for i in range(n - 1)])  6.69 us
  transfers between devices with their start and end apart: 10, of which 0 were waited for; matrix products, arithmetic and copies ran while one was open for 0% of the time, Pallas kernels for 20%

profile of v4, /device:TPU:6, one launch (start us, length us, event | category | flops | bytes accessed | tf_op | source)
XLA Modules:
  0.0 44.9 jit_solution(12345203402868643345)
XLA Ops:
  0.6 1.4 %shard_map.104 = (f32[32,4096]{1,0:T(8,128)S(1)}, f32[36,128]{1,0:T(8,128)S(1)}, f32[36,128]{1,0:T(8,128)S(1)}, f32[27,4,1024]{2,1,0:T(4,128)S(1)}, f32[4,1024]{...) custom-call(f32[864,128]{1,0:T(8,128)} %bitcast.11, ...), custom_call_target="tpu_custom_call" | custom-call | bytes 2690936 | tf_op jit(solution)/shard_map/pallas_call | solution.py:453
  2.0 0.0 collective-permute-start
  2.1 8.5 %collective-permute-start.1 = (f32[36,128]{1,0:T(8,128)S(1)}, f32[36,128]{1,0:T(8,128)S(1)}, u32[]{:S(2)}, u32[]{:S(2)}) collective-permute-start(f32[36,128]{1,0:T(8,128)S(1)} %get-tuple-element.57), channel_id=1, source_target_pairs={{0,15},{1,0},{2,1},{3,2},{4,3},{5,4},{6,5},{7,6},{8,7},{9,8},{10,9... | collective-permute-start | bytes 55304 | tf_op jit(solution)/shard_map/ppermute | solution.py:474
  11.2 2.1 %shard_map.105 = (f32[32,4096]{1,0:T(8,128)S(1)}, f32[32,4096]{1,0:T(8,128)S(1)}, f32[8,4096]{1,0:T(8,128)S(1)}, bf16[224,128]{1,0:T(8,128)(2,1)S(1)}, bf16[128,...) custom-call(s32[1,1]{1,0:T(1,128)S(6)} %copy.11.count_ref, ...), custom_call_target="tpu_custom_call" | custom-call | flops 3000000000 | bytes 2793408 | tf_op jit(solution)/shard_map/pallas_call | solution.py:453
  13.4 0.0 collective-permute-done.yl_ref
  13.4 0.0 collective-permute-done.1.yh_ref
  13.4 0.2 shard_map.106
  13.6 3.5 %collective-permute-start.2 = (f32[144,128]{1,0:T(8,128)S(1)}, f32[144,128]{1,0:T(8,128)S(1)}, u32[]{:S(2)}, u32[]{:S(2)}) collective-permute-start(f32[144,128]{1,0:T(8,128)S(1)} %get-tuple-element.59), channel_id=1, source_target_pairs={{0,16},{16,32},{32,48},{48,64},{64,80},{80,96},{96,112},{112,128},... | collective-permute-start | bytes 221192 | tf_op jit(solution)/shard_map/ppermute | solution.py:466
  17.1 4.5 %collective-permute-start.3 = (f32[144,128]{1,0:T(8,128)S(1)}, f32[144,128]{1,0:T(8,128)S(1)}, u32[]{:S(2)}, u32[]{:S(2)}) collective-permute-start(f32[144,128]{1,0:T(8,128)S(1)} %get-tuple-element.60.after_ref), channel_id=1, source_target_pairs={{16,0},{32,16},{48,32},{64,48},{80,64},{96,80},{112,96},{128,112},... | collective-permute-start | bytes 221192 | tf_op jit(solution)/shard_map/ppermute | solution.py:467
  21.5 2.0 %shard_map.108 = (f32[32,4096]{1,0:T(8,128)S(1)}, f32[32,4096]{1,0:T(8,128)S(1)}, bf16[256,128]{1,0:T(8,128)(2,1)S(1)}, f32[4,32,1024]{2,1,0:T(8,128)S(1)}) custom-call(s32[1,1]{1,0:T(1,128)S(6)} %copy.11.count_ref, f32[144,128]{1,0:T(8,128)S(1)} %get-tuple-element.60.after_ref, f32[128,128]{1,0:T(8,128)S(1)} %get-tuple-element.64.power_ref, ...), custom_call_target="tpu_custom_call" | custom-call | flops 2000000000 | bytes 2306052 | tf_op jit(solution)/shard_map/pallas_call | solution.py:453
  23.5 0.0 collective-permute-done.2.xl_ref
  23.5 0.0 collective-permute-done.3.xh_ref
  23.6 0.2 shard_map.107
  23.8 0.0 collective-permute-start.4
  23.8 2.9 %collective-permute-start.5 = (f32[36,128]{1,0:T(8,128)S(1)}, f32[36,128]{1,0:T(8,128)S(1)}, u32[]{:S(2)}, u32[]{:S(2)}) collective-permute-start(f32[36,128]{1,0:T(8,128)S(1)} %get-tuple-element.74), channel_id=1, source_target_pairs={{0,15},{1,0},{2,1},{3,2},{4,3},{5,4},{6,5},{7,6},{8,7},{9,8},{10,9... | collective-permute-start | bytes 55304 | tf_op jit(solution)/shard_map/ppermute | solution.py:474
  26.8 2.2 %shard_map.109 = (f32[32,4096]{1,0:T(8,128)S(1)}, f32[32,4096]{1,0:T(8,128)S(1)}, f32[32,4096]{1,0:T(8,128)S(1)}, f32[4,32,1024]{2,1,0:T(8,128)S(1)}) custom-call(f32[32,4096]{1,0:T(8,128)S(1)} %get-tuple-element.45.v_ref.v0_ref, f32[32,4096]{1,0:T(8,128)S(1)} %get-tuple-element.61.v1_ref, f32[32,4096]{1,0:T(8,128)S(1)} %get-tuple-element.62.r_ref, ...), custom_call_target="tpu_custom_call" | custom-call | flops 2000000000 | bytes 5787648 | tf_op jit(solution)/shard_map/pallas_call | solution.py:453
  29.0 0.0 collective-permute-done.4.yl_ref
  29.0 0.0 collective-permute-done.5.yh_ref
  29.0 0.2 shard_map.110
  29.2 0.0 collective-permute-start.6
  29.2 2.9 %collective-permute-start.7 = (f32[36,128]{1,0:T(8,128)S(1)}, f32[36,128]{1,0:T(8,128)S(1)}, u32[]{:S(2)}, u32[]{:S(2)}) collective-permute-start(f32[36,128]{1,0:T(8,128)S(1)} %get-tuple-element.82), channel_id=1, source_target_pairs={{0,15},{1,0},{2,1},{3,2},{4,3},{5,4},{6,5},{7,6},{8,7},{9,8},{10,9... | collective-permute-start | bytes 55304 | tf_op jit(solution)/shard_map/ppermute | solution.py:474
  32.1 3.2 %collective-permute-start.8 = (f32[72,128]{1,0:T(8,128)S(1)}, f32[72,128]{1,0:T(8,128)S(1)}, u32[]{:S(2)}, u32[]{:S(2)}) collective-permute-start(f32[72,128]{1,0:T(8,128)S(1)} %get-tuple-element.83), channel_id=1, source_target_pairs={{0,16},{16,32},{32,48},{48,64},{64,80},{80,96},{96,112},{112,128},... | collective-permute-start | bytes 110600 | tf_op jit(solution)/shard_map/ppermute | solution.py:466
  35.4 5.0 %collective-permute-start.9 = (f32[72,128]{1,0:T(8,128)S(1)}, f32[72,128]{1,0:T(8,128)S(1)}, u32[]{:S(2)}, u32[]{:S(2)}) collective-permute-start(f32[72,128]{1,0:T(8,128)S(1)} %get-tuple-element.84), channel_id=1, source_target_pairs={{16,0},{32,16},{48,32},{64,48},{80,64},{96,80},{112,96},{128,112},... | collective-permute-start | bytes 110600 | tf_op jit(solution)/shard_map/ppermute | solution.py:467
  40.4 2.5 %shard_map.111 = (f32[32,4096]{1,0:T(8,128)S(1)}, f32[4,32,1024]{2,1,0:T(8,128)S(1)}) custom-call(f32[32,4096]{1,0:T(8,128)S(1)} %get-tuple-element.45.v_ref.v0_ref, f32[32,4096]{1,0:T(8,128)S(1)} %get-tuple-element.75.v2_ref, f32[32,4096]{1,0:T(8,128)S(1)} %get-tuple-element.76.r_ref, f32[32,4096]{1,0:T(8,128)S(1)} %get-tuple-element.77.c3_ref, ...), custom_call_target="tpu_custom_call" | custom-call | flops 2000000000 | bytes 4050944 | tf_op jit(solution)/shard_map/pallas_call | solution.py:453
  42.9 0.0 collective-permute-done.6.yl_ref
  42.9 0.0 collective-permute-done.7.yh_ref
  42.9 0.0 collective-permute-done.8.xl_ref
  42.9 0.0 collective-permute-done.9.xh_ref
  42.9 1.9 %shard_map.112 = (f32[864,128]{1,0:T(8,128)}, f32[27,4,1024]{2,1,0:T(4,128)}) custom-call(s32[1,1]{1,0:T(1,128)S(6)} %copy.11.count_ref, f32[32,4096]{1,0:T(8,128)S(1)} %get-tuple-element.79.u_ref, bf16[128,64]{1,0:T(8,128)(2,1)S(1)} %get-tuple-element.55.fh_ref, bf16[32,256]{1,0:T(8,128)(2,1)S(1)} %get-tuple-element.80.fs_ref, ...), custom_call_target="tpu_custom_call" | custom-call | bytes 2555908 | tf_op jit(solution)/shard_map/pallas_call | solution.py:453
Async XLA Ops:
  2.0 11.3 %collective-permute-start = (f32[36,128]{1,0:T(8,128)S(1)}, f32[36,128]{1,0:T(8,128)S(1)}, u32[]{:S(2)}, u32[]{:S(2)}) collective-permute-start(f32[36,128]{1,0:T(8,128)S(1)} %get-tuple-element.56), channel_id=1, source_target_pairs={{0,1},{1,2},{2,3},{3,4},{4,5},{5,6},{6,7},{7,8},{8,9},{9,10},{10,1... | collective-permute-start | bytes 55304 | tf_op jit(solution)/shard_map/ppermute | solution.py:473
  2.1 11.3 %collective-permute-start.1 = (f32[36,128]{1,0:T(8,128)S(1)}, f32[36,128]{1,0:T(8,128)S(1)}, u32[]{:S(2)}, u32[]{:S(2)}) collective-permute-start(f32[36,128]{1,0:T(8,128)S(1)} %get-tuple-element.57), channel_id=1, source_target_pairs={{0,15},{1,0},{2,1},{3,2},{4,3},{5,4},{6,5},{7,6},{8,7},{9,8},{10,9... | collective-permute-start | bytes 55304 | tf_op jit(solution)/shard_map/ppermute | solution.py:474
  13.6 10.0 %collective-permute-start.2 = (f32[144,128]{1,0:T(8,128)S(1)}, f32[144,128]{1,0:T(8,128)S(1)}, u32[]{:S(2)}, u32[]{:S(2)}) collective-permute-start(f32[144,128]{1,0:T(8,128)S(1)} %get-tuple-element.59), channel_id=1, source_target_pairs={{0,16},{16,32},{32,48},{48,64},{64,80},{80,96},{96,112},{112,128},... | collective-permute-start | bytes 221192 | tf_op jit(solution)/shard_map/ppermute | solution.py:466
  17.1 6.5 %collective-permute-start.3 = (f32[144,128]{1,0:T(8,128)S(1)}, f32[144,128]{1,0:T(8,128)S(1)}, u32[]{:S(2)}, u32[]{:S(2)}) collective-permute-start(f32[144,128]{1,0:T(8,128)S(1)} %get-tuple-element.60.after_ref), channel_id=1, source_target_pairs={{16,0},{32,16},{48,32},{64,48},{80,64},{96,80},{112,96},{128,112},... | collective-permute-start | bytes 221192 | tf_op jit(solution)/shard_map/ppermute | solution.py:467
  23.8 5.2 %collective-permute-start.4 = (f32[36,128]{1,0:T(8,128)S(1)}, f32[36,128]{1,0:T(8,128)S(1)}, u32[]{:S(2)}, u32[]{:S(2)}) collective-permute-start(f32[36,128]{1,0:T(8,128)S(1)} %get-tuple-element.73), channel_id=1, source_target_pairs={{0,1},{1,2},{2,3},{3,4},{4,5},{5,6},{6,7},{7,8},{8,9},{9,10},{10,1... | collective-permute-start | bytes 55304 | tf_op jit(solution)/shard_map/ppermute | solution.py:473
  23.8 5.1 %collective-permute-start.5 = (f32[36,128]{1,0:T(8,128)S(1)}, f32[36,128]{1,0:T(8,128)S(1)}, u32[]{:S(2)}, u32[]{:S(2)}) collective-permute-start(f32[36,128]{1,0:T(8,128)S(1)} %get-tuple-element.74), channel_id=1, source_target_pairs={{0,15},{1,0},{2,1},{3,2},{4,3},{5,4},{6,5},{7,6},{8,7},{9,8},{10,9... | collective-permute-start | bytes 55304 | tf_op jit(solution)/shard_map/ppermute | solution.py:474
  29.2 13.7 %collective-permute-start.6 = (f32[36,128]{1,0:T(8,128)S(1)}, f32[36,128]{1,0:T(8,128)S(1)}, u32[]{:S(2)}, u32[]{:S(2)}) collective-permute-start(f32[36,128]{1,0:T(8,128)S(1)} %get-tuple-element.81), channel_id=1, source_target_pairs={{0,1},{1,2},{2,3},{3,4},{4,5},{5,6},{6,7},{7,8},{8,9},{9,10},{10,1... | collective-permute-start | bytes 55304 | tf_op jit(solution)/shard_map/ppermute | solution.py:473
  29.2 13.7 %collective-permute-start.7 = (f32[36,128]{1,0:T(8,128)S(1)}, f32[36,128]{1,0:T(8,128)S(1)}, u32[]{:S(2)}, u32[]{:S(2)}) collective-permute-start(f32[36,128]{1,0:T(8,128)S(1)} %get-tuple-element.82), channel_id=1, source_target_pairs={{0,15},{1,0},{2,1},{3,2},{4,3},{5,4},{6,5},{7,6},{8,7},{9,8},{10,9... | collective-permute-start | bytes 55304 | tf_op jit(solution)/shard_map/ppermute | solution.py:474
  32.1 10.8 %collective-permute-start.8 = (f32[72,128]{1,0:T(8,128)S(1)}, f32[72,128]{1,0:T(8,128)S(1)}, u32[]{:S(2)}, u32[]{:S(2)}) collective-permute-start(f32[72,128]{1,0:T(8,128)S(1)} %get-tuple-element.83), channel_id=1, source_target_pairs={{0,16},{16,32},{32,48},{48,64},{64,80},{80,96},{96,112},{112,128},... | collective-permute-start | bytes 110600 | tf_op jit(solution)/shard_map/ppermute | solution.py:466
  35.4 7.6 %collective-permute-start.9 = (f32[72,128]{1,0:T(8,128)S(1)}, f32[72,128]{1,0:T(8,128)S(1)}, u32[]{:S(2)}, u32[]{:S(2)}) collective-permute-start(f32[72,128]{1,0:T(8,128)S(1)} %get-tuple-element.84), channel_id=1, source_target_pairs={{16,0},{32,16},{48,32},{64,48},{80,64},{96,80},{112,96},{128,112},... | collective-permute-start | bytes 110600 | tf_op jit(solution)/shard_map/ppermute | solution.py:467

commit v5 on v4

--- a/solution.py
+++ b/solution.py
@@ -139,7 +139,7 @@
 
 
 def mixed_kernel(
-    count_ref, v_ref, w_ref, frac_ref, idx_ref, vol_ref, face_ref, mat_ref, sel_ref,
+    live_ref, v_ref, w_ref, frac_ref, idx_ref, vol_ref, face_ref, mat_ref, sel_ref,
     int_ref, u_ref, fm_ref, wg_ref, fh_ref, fs_ref, power_ref,
     g_ref, small_ref, diag_ref, wpad_ref,
 ):
@@ -179,7 +179,7 @@
         wpad_ref[0:27, :] = w_ref[:, m, :]
         values = dot(stacked(p1, m), stack_right(wpad_ref[...]))
         first = first + frac[m:m + 1, :] * values
-    live = slots_live(count_ref)
+    live = live_ref[...] > 0.0
     first = jnp.where(live, first, 0.0)
     first = jnp.concatenate([first[0:27], jnp.where(live, frac, 0.0), first[31:32]], axis=0)
 
@@ -197,10 +197,6 @@
     return jnp.where(row == column, 1.0, 0.0)
 
 
-def slots_live(count_ref):
-    return lax.broadcasted_iota(jnp.int32, (1, SLOTS), 1) < count_ref[0, 0]
-
-
 def stacked(matrix, m):
     rows = matrix[32 * m:32 * m + 32, :]
     for shift in (32, 64):
@@ -223,7 +219,7 @@
 
 
 def later_kernel(
-    count_ref, after_ref, power_ref, w_ref, frac_ref, idx_ref,
+    live_ref, after_ref, power_ref, w_ref, frac_ref, idx_ref,
     c2_ref, c3_ref, pp_ref, b3_ref, wpad_ref,
 ):
     eye = identity()
@@ -235,15 +231,15 @@
     wpad_ref[...] = jnp.zeros((32, SLOTS), F32)
     total = 0.0
     for m in range(4):
-        pp_ref[32 * m:32 * m + 32, :] = stacked(p1, m)
-        pp_ref[128 + 32 * m:160 + 32 * m, :] = stacked(p2, m)
+        pp_ref[32 * m:32 * m + 32, 0:128] = stacked(p1, m)
+        pp_ref[32 * m:32 * m + 32, 128:256] = stacked(p2, m)
         wpad_ref[0:27, :] = w_ref[:, m, :]
         left = jnp.concatenate([stacked(q2, m), stacked(q3, m)], axis=0)
         values = dot(left, stack_right(wpad_ref[...]))
         b3_ref[m] = values[32:64]
         total = total + frac[m:m + 1, :] * values
     idx = idx_ref[...]
-    dense = to_zones(jnp.where(slots_live(count_ref), total, 0.0), lane_hot(idx), idx)
+    dense = to_zones(jnp.where(live_ref[...] > 0.0, total, 0.0), lane_hot(idx), idx)
     for g in range(GROUPS):
         cols = slice(g * GROUP, (g + 1) * GROUP)
         c2_ref[:, cols] = dense[g][0:32]
@@ -351,47 +347,48 @@
     y_faces(v_ref, ylo_ref, yhi_ref)
 
 
+def weighted(f, q):
+    return sum(f[m + 3:m + 4] * q[32 * m:32 * m + 32] for m in range(4))
+
+
 def between_one(
-    v0_ref, v1_ref, r_ref, beside_ref, c2_ref, c3_ref, fm_ref, idx_ref, wg_ref, fh_ref, pp_ref, b3_ref,
-    int_ref, u_ref, c3_out, b3_out, g_ref,
+    v0_ref, v1_ref, r_ref, beside_ref, c2_ref, fm_ref, wg_ref, fh_ref, pp_ref,
+    int_ref, u_ref, g_ref,
 ):
     interior(v1_ref, wg_ref, g_ref, int_ref)
     int_ref[:, 0:1024] += terms(fh_ref, beside_ref, 0)
     int_ref[:, 3072:4096] += terms(fh_ref, beside_ref, 1)
     for x in range(CX):
         cols = slice(x * 1024, (x + 1) * 1024)
-        q = dot(pp_ref[...], stack_right(r_ref[:, cols]))
         f = fm_ref[:, cols]
-        s1 = sum(f[m + 3:m + 4] * q[32 * m:32 * m + 32] for m in range(4))
-        s2 = sum(f[m + 3:m + 4] * q[128 + 32 * m:160 + 32 * m] for m in range(4))
+        s1 = weighted(f, dot(pp_ref[:, 0:128], stack_right(r_ref[:, cols])))
         bulk = 0.75 * v0_ref[:, cols] + 0.25 * v1_ref[:, cols]
         u_ref[:, cols] = jnp.where(f[3:4] > 0.0, c2_ref[:, cols] + 0.25 * s1, bulk)
-        c3_out[:, cols] = c3_ref[:, cols] + (1.0 / 6.0) * s2
-    idx = idx_ref[...]
-    at = stack_right(to_slots(r_ref, lane_hot(idx), idx))
-    for m in range(4):
-        b3_out[m] = b3_ref[m] + (1.0 / 6.0) * dot(pp_ref[128 + 32 * m:160 + 32 * m, :], at)
 
 
 def between_two(
-    v0_ref, v2_ref, r_ref, c3_ref, fm_ref, idx_ref, wg_ref, pp_ref, b3_ref,
-    u_ref, b3_out, g_ref, int_ref,
+    v0_ref, v2_ref, r0_ref, r1_ref, c3_ref, fm_ref, live_ref, idx_ref, wg_ref, pp_ref, b3_ref, w_ref,
+    u_ref, slots_ref, g_ref, int_ref,
 ):
     interior(v2_ref, wg_ref, g_ref, int_ref)
     for x in range(CX):
         cols = slice(x * 1024, (x + 1) * 1024)
-        q = dot(pp_ref[0:128, :], stack_right(r_ref[:, cols]))
+        both = jnp.concatenate([stack_right(r1_ref[:, cols]), stack_right(r0_ref[:, cols])], axis=0)
         f = fm_ref[:, cols]
-        s1 = sum(f[m + 3:m + 4] * q[32 * m:32 * m + 32] for m in range(4))
+        s1 = weighted(f, dot(pp_ref[...], both))
         bulk = (1.0 / 3.0) * v0_ref[:, cols] + (2.0 / 3.0) * v2_ref[:, cols]
         old = jnp.where(f[3:4] > 0.0, c3_ref[:, cols] + (1.0 / 6.0) * s1, bulk)
         u_ref[:, cols] = old + (2.0 / 3.0) * int_ref[:, cols]
     idx = idx_ref[...]
     hot = lane_hot(idx)
-    at = stack_right(to_slots(r_ref, hot, idx))
+    both = jnp.concatenate(
+        [stack_right(to_slots(r1_ref, hot, idx)), stack_right(to_slots(r0_ref, hot, idx))], axis=0
+    )
     inner = (2.0 / 3.0) * to_slots(int_ref, hot, idx)
+    live = live_ref[...] > 0.0
     for m in range(4):
-        b3_out[m] = b3_ref[m] + inner + (1.0 / 6.0) * dot(pp_ref[32 * m:32 * m + 32, :], at)
+        value = b3_ref[m] + inner + (1.0 / 6.0) * dot(pp_ref[32 * m:32 * m + 32, :], both)
+        slots_ref[:, m, :] = jnp.where(live, value[0:27], w_ref[:, m, :])
 
 
 def faces_to_slots(pad_ref, idx):
@@ -415,7 +412,7 @@
 
 
 def last_kernel(
-    count_ref, u_ref, fh_ref, fs_ref, yl_ref, yh_ref, xl_ref, xh_ref, idx_ref, b3_ref, w_ref,
+    live_ref, u_ref, fh_ref, fs_ref, yl_ref, yh_ref, xl_ref, xh_ref, idx_ref, slots_ref,
     field_hbm, out_hbm, pad_ref, whole_ref, field_ref, out_ref, sems,
 ):
     pad_ref[...] = jnp.zeros((16, 3072), F32)
@@ -428,9 +425,9 @@
     field_copy = pltpu.make_async_copy(field_ref, field_hbm, sems.at[0])
     field_copy.start()
     added = dot(fs_ref[...], stack_right(faces_to_slots(pad_ref, idx_ref[...])))
-    live = slots_live(count_ref)
-    for m in range(4):
-        out_ref[:, m, :] = jnp.where(live, b3_ref[m, 0:27, :] + added[0:27], w_ref[:, m, :])
+    added = jnp.where(live_ref[...] > 0.0, added, 0.0)
+    for d in range(27):
+        out_ref[d] = slots_ref[d] + added[d:d + 1]
     out_copy = pltpu.make_async_copy(out_ref, out_hbm, sems.at[1])
     out_copy.start()
     field_copy.wait()
@@ -438,7 +435,6 @@
 
 
 VMEM = pl.BlockSpec(memory_space=pltpu.VMEM)
-SMEM = pl.BlockSpec(memory_space=pltpu.SMEM)
 ANY = pl.BlockSpec(memory_space=pl.ANY)
 HBM = pl.BlockSpec(memory_space=pltpu.HBM)
 DENSE = jax.ShapeDtypeStruct((32, ZONES), F32)
@@ -448,12 +444,12 @@
 SLOT3 = jax.ShapeDtypeStruct((4, 32, SLOTS), F32)
 
 
-def call(kernel, outs, args, scratch=(), smem=0, flops=0, in_spec=VMEM, out_spec=VMEM):
+def call(kernel, outs, args, scratch=(), flops=0, in_spec=VMEM, out_spec=VMEM):
     moved = 4 * sum(int(np.prod(a.shape)) for a in list(args) + list(outs))
     return pl.pallas_call(
         kernel,
         out_shape=outs,
-        in_specs=[SMEM] * smem + [in_spec] * (len(args) - smem),
+        in_specs=[in_spec] * len(args),
         out_specs=[out_spec] * len(outs),
         scratch_shapes=list(scratch),
         compiler_params=pltpu.CompilerParams(vmem_limit_bytes=48 * 1024 * 1024),
@@ -488,7 +484,8 @@
         mat_matrix.transpose(1, 0, 2),
         jnp.asarray(selections()),
     ]
-    count = mix_count.reshape(1, 1)
+    slot = lax.broadcasted_iota(jnp.int32, (1, SLOTS), 1)
+    live = jnp.where(slot < mix_count.reshape(1, 1), 1.0, 0.0)
     g_space = pltpu.VMEM((224, ZONES), F32)
     pad = pltpu.VMEM((16, 3072), F32)
     bf = lambda rows, lanes: jax.ShapeDtypeStruct((rows, lanes), BF16)
@@ -506,46 +503,46 @@
     inner, u, fm, wg, fh, fs, power = call(
         mixed_kernel,
         [DENSE, DENSE, f32(8, ZONES), bf(224, 128), bf(128, 64), bf(32, 256), f32(128, 128)],
-        [count, v0] + small,
+        [live, v0] + small,
         [g_space, pltpu.VMEM((32, 128), F32), pltpu.VMEM((128, 128), F32),
          pltpu.VMEM((32, SLOTS), F32)],
-        smem=1, flops=3 * 10**9,
+        flops=3 * 10**9,
     )
     inner, *faces = call(
         y_first_kernel, [DENSE] + X_TWICE, [inner, u, v0, fh, *halo], [pad]
     )
     halo = exchange_x(*faces)
     c2, c3, pp, b3 = call(
-        later_kernel, [DENSE, DENSE, bf(256, 128), SLOT3],
-        [count, faces[0], power, weights, frac, idx], [pltpu.VMEM((32, SLOTS), F32)],
-        smem=1, flops=2 * 10**9,
+        later_kernel, [DENSE, DENSE, bf(128, 256), SLOT3],
+        [live, faces[0], power, weights, frac, idx], [pltpu.VMEM((32, SLOTS), F32)],
+        flops=2 * 10**9,
     )
     v1, r0, beside, *faces = call(
         x_first_kernel, [DENSE, DENSE, f32(16, 2048)] + Y_FACES, [inner, u, v0, fh, *halo],
         [pad, pltpu.VMEM((16, 2048), F32)],
     )
     halo = exchange_y(*faces)
-    inner, u, c3, b3 = call(
-        between_one, [DENSE, DENSE, DENSE, SLOT3],
-        [v0, v1, r0, beside, c2, c3, fm, idx, wg, fh, pp, b3], [g_space], flops=2 * 10**9,
+    inner, u = call(
+        between_one, [DENSE, DENSE],
+        [v0, v1, r0, beside, c2, fm, wg, fh, pp], [g_space], flops=2 * 10**9,
     )
     v2, r1, *faces = call(
         second_kernel, [DENSE, DENSE] + X_FACES + Y_FACES, [inner, u, fh, *halo], [pad]
     )
     x_halo = exchange_x(*faces[:2])
     y_halo = exchange_y(*faces[2:])
-    u, b3 = call(
-        between_two, [DENSE, SLOT3],
-        [v0, v2, r1, c3, fm, idx, wg, pp, b3], [g_space, pltpu.VMEM((32, ZONES), F32)],
+    u, slots = call(
+        between_two, [DENSE, jax.ShapeDtypeStruct((27, 4, SLOTS), F32)],
+        [v0, v2, r0, r1, c3, fm, live, idx, wg, pp, b3, weights], [g_space, pltpu.VMEM((32, ZONES), F32)],
         flops=2 * 10**9,
     )
     field, out = call(
         last_kernel,
         [jax.ShapeDtypeStruct((27 * ROWS, CZ), F32), jax.ShapeDtypeStruct((27, 4, SLOTS), F32)],
-        [count, u, fh, fs, *y_halo, *x_halo, idx, b3, weights],
+        [live, u, fh, fs, *y_halo, *x_halo, idx, slots],
         [pad, pltpu.VMEM((32, ZONES), F32), pltpu.VMEM((27 * ROWS, CZ), F32),
          pltpu.VMEM((27, 4, SLOTS), F32), pltpu.SemaphoreType.DMA((2,))],
-        smem=1, out_spec=ANY,
+        out_spec=ANY,
     )
     return field.reshape(state.shape), out.transpose(1, 0, 2).reshape(mix_weights.shape)
 

time: 45.8 us -> 45.1 us (0.985); the launches traced: 44.9 us -> 44.9 us
  waiting for transfers between devices: 0.03 us -> 0.49 us
  transfers between devices with their start and end apart: 10 -> 10, of which waited for: 0 -> 1; matrix products, arithmetic and copies ran while one was open for 0% -> 0% of each run, Pallas kernels for 20% -> 19%
where the time goes in v5:
time: 45.1 us; the launch traced here: 44.9 us
  starting transfers between devices  30.6 us (68%)
  Pallas kernels  12.3 us (27%)
  between operations  1.46 us (3%)
  waiting for transfers between devices  0.49 us (1%)
    ppermute x3, starting transfers between devices, exchange_y(): above = lax.ppermute(low, 'yz', [(i, (i - 1) % n) for i in range(n)])  14.4 us
    pallas_call x9, Pallas kernels, call(): pl.pallas_call(kernel, out_shape=outs, in_specs=[in_spec] * len(args), ou...  12.3 us
    ppermute x2, starting transfers between devices, exchange_x(): above = lax.ppermute(low, 'gx', [(i + 1, i) for i in range(n - 1)])  9.49 us
    ppermute x2, starting transfers between devices, exchange_x(): below = lax.ppermute(high, 'gx', [(i, i + 1) for i in range(n - 1)])  6.7 us
  transfers between devices with their start and end apart: 10, of which 1 were waited for; matrix products, arithmetic and copies ran while one was open for 0% of the time, Pallas kernels for 19%

profile of v5, /device:TPU:6, one launch (start us, length us, event | category | flops | bytes accessed | tf_op | source)
XLA Modules:
  0.0 44.9 jit_solution(10769785145749292450)
XLA Ops:
  0.6 1.4 %shard_map.104 = (f32[32,4096]{1,0:T(8,128)S(1)}, f32[36,128]{1,0:T(8,128)S(1)}, f32[36,128]{1,0:T(8,128)S(1)}, f32[27,4,1024]{2,1,0:T(4,128)S(1)}, f32[4,1024]{...) custom-call(f32[864,128]{1,0:T(8,128)} %bitcast.13, ...), custom_call_target="tpu_custom_call" | custom-call | bytes 2690936 | tf_op jit(solution)/shard_map/pallas_call | solution.py:449
  2.0 0.0 collective-permute-start
  2.1 8.5 %collective-permute-start.1 = (f32[36,128]{1,0:T(8,128)S(1)}, f32[36,128]{1,0:T(8,128)S(1)}, u32[]{:S(2)}, u32[]{:S(2)}) collective-permute-start(f32[36,128]{1,0:T(8,128)S(1)} %get-tuple-element.55), channel_id=1, source_target_pairs={{0,15},{1,0},{2,1},{3,2},{4,3},{5,4},{6,5},{7,6},{8,7},{9,8},{10,9... | collective-permute-start | bytes 55304 | tf_op jit(solution)/shard_map/ppermute | solution.py:470
  11.2 2.1 %shard_map.105 = (f32[32,4096]{1,0:T(8,128)S(1)}, f32[32,4096]{1,0:T(8,128)S(1)}, f32[8,4096]{1,0:T(8,128)S(1)}, bf16[224,128]{1,0:T(8,128)(2,1)S(1)}, bf16[128,...) custom-call(f32[1,1024]{1,0:T(1,128)S(1)} %compare_select_fusion.live_ref, ...), custom_call_target="tpu_custom_call" | custom-call | flops 3000000000 | bytes 2797500 | tf_op jit(solution)/shard_map/pallas_call | solution.py:449
  13.4 0.0 collective-permute-done.yl_ref
  13.4 0.0 collective-permute-done.1.yh_ref
  13.4 0.2 shard_map.106
  13.6 3.5 %collective-permute-start.2 = (f32[144,128]{1,0:T(8,128)S(1)}, f32[144,128]{1,0:T(8,128)S(1)}, u32[]{:S(2)}, u32[]{:S(2)}) collective-permute-start(f32[144,128]{1,0:T(8,128)S(1)} %get-tuple-element.57), channel_id=1, source_target_pairs={{0,16},{16,32},{32,48},{48,64},{64,80},{80,96},{96,112},{112,128},... | collective-permute-start | bytes 221192 | tf_op jit(solution)/shard_map/ppermute | solution.py:462
  17.1 4.5 %collective-permute-start.3 = (f32[144,128]{1,0:T(8,128)S(1)}, f32[144,128]{1,0:T(8,128)S(1)}, u32[]{:S(2)}, u32[]{:S(2)}) collective-permute-start(f32[144,128]{1,0:T(8,128)S(1)} %get-tuple-element.58.after_ref), channel_id=1, source_target_pairs={{16,0},{32,16},{48,32},{64,48},{80,64},{96,80},{112,96},{128,112},... | collective-permute-start | bytes 221192 | tf_op jit(solution)/shard_map/ppermute | solution.py:463
  21.5 2.0 %shard_map.108 = (f32[32,4096]{1,0:T(8,128)S(1)}, f32[32,4096]{1,0:T(8,128)S(1)}, bf16[128,256]{1,0:T(8,128)(2,1)S(1)}, f32[4,32,1024]{2,1,0:T(8,128)S(1)}) custom-call(f32[1,1024]{1,0:T(1,128)S(1)} %compare_select_fusion.live_ref, f32[144,128]{1,0:T(8,128)S(1)} %get-tuple-element.58.after_ref, f32[128,128]{1,0:T(8,128)S(1)} %get-tuple-element.62.power_ref, ...), custom_call_target="tpu_custom_call" | custom-call | flops 2000000000 | bytes 2310144 | tf_op jit(solution)/shard_map/pallas_call | solution.py:449
  23.5 0.0 collective-permute-done.2.xl_ref
  23.6 0.0 collective-permute-done.3.xh_ref
  23.6 0.2 shard_map.107
  23.8 0.0 collective-permute-start.4
  23.8 2.9 %collective-permute-start.5 = (f32[36,128]{1,0:T(8,128)S(1)}, f32[36,128]{1,0:T(8,128)S(1)}, u32[]{:S(2)}, u32[]{:S(2)}) collective-permute-start(f32[36,128]{1,0:T(8,128)S(1)} %get-tuple-element.70), channel_id=1, source_target_pairs={{0,15},{1,0},{2,1},{3,2},{4,3},{5,4},{6,5},{7,6},{8,7},{9,8},{10,9... | collective-permute-start | bytes 55304 | tf_op jit(solution)/shard_map/ppermute | solution.py:470
  26.8 1.0 %shard_map.109 = (f32[32,4096]{1,0:T(8,128)S(1)}, f32[32,4096]{1,0:T(8,128)S(1)}) custom-call(f32[32,4096]{1,0:T(8,128)S(1)} %get-tuple-element.43.v_ref.v0_ref, f32[32,4096]{1,0:T(8,128)S(1)} %get-tuple-element.59.v1_ref, f32[32,4096]{1,0:T(8,128)S(1)} %get-tuple-element.60.r_ref.r0_ref, f32[16,2048]{1,0:T(8,128)S(1)} %get-tuple-element.61.beside_ref, ...), custom_call_target="tpu_custom_call" | custom-call | flops 2000000000 | bytes 3686400 | tf_op jit(solution)/shard_map/pallas_call | solution.py:449
  27.8 0.5 %collective-permute-done.4.yl_ref = f32[36,128]{1,0:T(8,128)S(1)} collective-permute-done((f32[36,128]{1,0:T(8,128)S(1)}, f32[36,128]{1,0:T(8,128)S(1)}, u32[]{:S(2)}, u32[]{:S(2)}) %collective-permute-start.4) | collective-permute-done | bytes 18464 | tf_op jit(solution)/shard_map/ppermute | solution.py:469
  28.2 0.0 collective-permute-done.5.yh_ref
  28.3 0.2 shard_map.110
  28.5 0.0 collective-permute-start.6
  28.5 2.9 %collective-permute-start.7 = (f32[36,128]{1,0:T(8,128)S(1)}, f32[36,128]{1,0:T(8,128)S(1)}, u32[]{:S(2)}, u32[]{:S(2)}) collective-permute-start(f32[36,128]{1,0:T(8,128)S(1)} %get-tuple-element.78), channel_id=1, source_target_pairs={{0,15},{1,0},{2,1},{3,2},{4,3},{5,4},{6,5},{7,6},{8,7},{9,8},{10,9... | collective-permute-start | bytes 55304 | tf_op jit(solution)/shard_map/ppermute | solution.py:470
  31.4 3.2 %collective-permute-start.8 = (f32[72,128]{1,0:T(8,128)S(1)}, f32[72,128]{1,0:T(8,128)S(1)}, u32[]{:S(2)}, u32[]{:S(2)}) collective-permute-start(f32[72,128]{1,0:T(8,128)S(1)} %get-tuple-element.79), channel_id=1, source_target_pairs={{0,16},{16,32},{32,48},{48,64},{64,80},{80,96},{96,112},{112,128},... | collective-permute-start | bytes 110600 | tf_op jit(solution)/shard_map/ppermute | solution.py:462
  34.7 5.0 %collective-permute-start.9 = (f32[72,128]{1,0:T(8,128)S(1)}, f32[72,128]{1,0:T(8,128)S(1)}, u32[]{:S(2)}, u32[]{:S(2)}) collective-permute-start(f32[72,128]{1,0:T(8,128)S(1)} %get-tuple-element.80), channel_id=1, source_target_pairs={{16,0},{32,16},{48,32},{64,48},{80,64},{96,80},{112,96},{128,112},... | collective-permute-start | bytes 110600 | tf_op jit(solution)/shard_map/ppermute | solution.py:463
  39.7 3.3 %shard_map.111 = (f32[32,4096]{1,0:T(8,128)S(1)}, f32[27,4,1024]{2,1,0:T(4,128)S(1)}) custom-call(f32[32,4096]{1,0:T(8,128)S(1)} %get-tuple-element.43.v_ref.v0_ref, f32[32,4096]{1,0:T(8,128)S(1)} %get-tuple-element.71.v2_ref, f32[32,4096]{1,0:T(8,128)S(1)} %get-tuple-element.60.r_ref.r0_ref, f32[32,4096]{1,0:T(8,128)S(1)} %get-tuple-element.72.r1_ref, ...), custom_call_target="tpu_custom_call" | custom-call | flops 2000000000 | bytes 4939776 | tf_op jit(solution)/shard_map/pallas_call | solution.py:449
  43.0 0.0 collective-permute-done.6.yl_ref
  43.0 0.0 collective-permute-done.7.yh_ref
  43.0 0.0 collective-permute-done.8.xl_ref
  43.1 0.0 collective-permute-done.9.xh_ref
  43.1 1.8 %shard_map.112 = (f32[864,128]{1,0:T(8,128)}, f32[27,4,1024]{2,1,0:T(4,128)}) custom-call(f32[1,1024]{1,0:T(1,128)S(1)} %compare_select_fusion.live_ref, f32[32,4096]{1,0:T(8,128)S(1)} %get-tuple-element.75.u_ref, bf16[128,64]{1,0:T(8,128)(2,1)S(1)} %get-tuple-element.53.fh_ref, bf16[32,256]{1,0:T(8,128)(2,1)S(1)} %get-tuple-element.76.fs_ref, ...), custom_call_target="tpu_custom_call" | custom-call | bytes 2035712 | tf_op jit(solution)/shard_map/pallas_call | solution.py:449
  (1 shorter events, 0.0 us)
Async XLA Ops:
  2.0 11.3 %collective-permute-start = (f32[36,128]{1,0:T(8,128)S(1)}, f32[36,128]{1,0:T(8,128)S(1)}, u32[]{:S(2)}, u32[]{:S(2)}) collective-permute-start(f32[36,128]{1,0:T(8,128)S(1)} %get-tuple-element.54), channel_id=1, source_target_pairs={{0,1},{1,2},{2,3},{3,4},{4,5},{5,6},{6,7},{7,8},{8,9},{9,10},{10,1... | collective-permute-start | bytes 55304 | tf_op jit(solution)/shard_map/ppermute | solution.py:469
  2.1 11.3 %collective-permute-start.1 = (f32[36,128]{1,0:T(8,128)S(1)}, f32[36,128]{1,0:T(8,128)S(1)}, u32[]{:S(2)}, u32[]{:S(2)}) collective-permute-start(f32[36,128]{1,0:T(8,128)S(1)} %get-tuple-element.55), channel_id=1, source_target_pairs={{0,15},{1,0},{2,1},{3,2},{4,3},{5,4},{6,5},{7,6},{8,7},{9,8},{10,9... | collective-permute-start | bytes 55304 | tf_op jit(solution)/shard_map/ppermute | solution.py:470
  13.6 10.0 %collective-permute-start.2 = (f32[144,128]{1,0:T(8,128)S(1)}, f32[144,128]{1,0:T(8,128)S(1)}, u32[]{:S(2)}, u32[]{:S(2)}) collective-permute-start(f32[144,128]{1,0:T(8,128)S(1)} %get-tuple-element.57), channel_id=1, source_target_pairs={{0,16},{16,32},{32,48},{48,64},{64,80},{80,96},{96,112},{112,128},... | collective-permute-start | bytes 221192 | tf_op jit(solution)/shard_map/ppermute | solution.py:462
  17.1 6.5 %collective-permute-start.3 = (f32[144,128]{1,0:T(8,128)S(1)}, f32[144,128]{1,0:T(8,128)S(1)}, u32[]{:S(2)}, u32[]{:S(2)}) collective-permute-start(f32[144,128]{1,0:T(8,128)S(1)} %get-tuple-element.58.after_ref), channel_id=1, source_target_pairs={{16,0},{32,16},{48,32},{64,48},{80,64},{96,80},{112,96},{128,112},... | collective-permute-start | bytes 221192 | tf_op jit(solution)/shard_map/ppermute | solution.py:463
  23.8 4.4 %collective-permute-start.4 = (f32[36,128]{1,0:T(8,128)S(1)}, f32[36,128]{1,0:T(8,128)S(1)}, u32[]{:S(2)}, u32[]{:S(2)}) collective-permute-start(f32[36,128]{1,0:T(8,128)S(1)} %get-tuple-element.69), channel_id=1, source_target_pairs={{0,1},{1,2},{2,3},{3,4},{4,5},{5,6},{6,7},{7,8},{8,9},{9,10},{10,1... | collective-permute-start | bytes 55304 | tf_op jit(solution)/shard_map/ppermute | solution.py:469
  23.8 4.4 %collective-permute-start.5 = (f32[36,128]{1,0:T(8,128)S(1)}, f32[36,128]{1,0:T(8,128)S(1)}, u32[]{:S(2)}, u32[]{:S(2)}) collective-permute-start(f32[36,128]{1,0:T(8,128)S(1)} %get-tuple-element.70), channel_id=1, source_target_pairs={{0,15},{1,0},{2,1},{3,2},{4,3},{5,4},{6,5},{7,6},{8,7},{9,8},{10,9... | collective-permute-start | bytes 55304 | tf_op jit(solution)/shard_map/ppermute | solution.py:470
  28.5 14.6 %collective-permute-start.6 = (f32[36,128]{1,0:T(8,128)S(1)}, f32[36,128]{1,0:T(8,128)S(1)}, u32[]{:S(2)}, u32[]{:S(2)}) collective-permute-start(f32[36,128]{1,0:T(8,128)S(1)} %get-tuple-element.77), channel_id=1, source_target_pairs={{0,1},{1,2},{2,3},{3,4},{4,5},{5,6},{6,7},{7,8},{8,9},{9,10},{10,1... | collective-permute-start | bytes 55304 | tf_op jit(solution)/shard_map/ppermute | solution.py:469
  28.5 14.5 %collective-permute-start.7 = (f32[36,128]{1,0:T(8,128)S(1)}, f32[36,128]{1,0:T(8,128)S(1)}, u32[]{:S(2)}, u32[]{:S(2)}) collective-permute-start(f32[36,128]{1,0:T(8,128)S(1)} %get-tuple-element.78), channel_id=1, source_target_pairs={{0,15},{1,0},{2,1},{3,2},{4,3},{5,4},{6,5},{7,6},{8,7},{9,8},{10,9... | collective-permute-start | bytes 55304 | tf_op jit(solution)/shard_map/ppermute | solution.py:470
  31.4 11.6 %collective-permute-start.8 = (f32[72,128]{1,0:T(8,128)S(1)}, f32[72,128]{1,0:T(8,128)S(1)}, u32[]{:S(2)}, u32[]{:S(2)}) collective-permute-start(f32[72,128]{1,0:T(8,128)S(1)} %get-tuple-element.79), channel_id=1, source_target_pairs={{0,16},{16,32},{32,48},{48,64},{64,80},{80,96},{96,112},{112,128},... | collective-permute-start | bytes 110600 | tf_op jit(solution)/shard_map/ppermute | solution.py:462
  34.7 8.4 %collective-permute-start.9 = (f32[72,128]{1,0:T(8,128)S(1)}, f32[72,128]{1,0:T(8,128)S(1)}, u32[]{:S(2)}, u32[]{:S(2)}) collective-permute-start(f32[72,128]{1,0:T(8,128)S(1)} %get-tuple-element.80), channel_id=1, source_target_pairs={{16,0},{32,16},{48,32},{64,48},{80,64},{96,80},{112,96},{128,112},... | collective-permute-start | bytes 110600 | tf_op jit(solution)/shard_map/ppermute | solution.py:463

commit v6 on v5

--- a/solution.py
+++ b/solution.py
@@ -74,12 +74,19 @@
     return slice(r * CZ, (r + 1) * CZ)
 
 
-def interior(v_ref, wg_ref, g_ref, out_ref):
+def interior(v_ref, wg_ref, g_ref, out_ref, planes=tuple(range(CX)), shift=0):
     for x in range(CX):
         cols = slice(x * 1024, (x + 1) * 1024)
-        g_ref[:, cols] = dot(wg_ref[...], stack_right(v_ref[:, cols]))
+        right = stack_right(v_ref[:, cols])
+        if x in planes:
+            g_ref[:, cols] = dot(wg_ref[...], right)
+        else:
+            if x + 1 in planes:
+                g_ref[32:64, cols] = dot(wg_ref[32:64, :], right)
+            if x - 1 in planes:
+                g_ref[64:96, cols] = dot(wg_ref[64:96, :], right)
     lane = lax.broadcasted_iota(jnp.int32, (32, CZ), 1)
-    for x in range(CX):
+    for x in planes:
         for y in range(CY):
             r = x * CY + y
             total = g_ref[0:32, block(r)]
@@ -95,7 +102,7 @@
             above = pltpu.roll(g_ref[192:224, block(r)], CZ - 1, 1)
             total += jnp.where(lane == 0, 0.0, below)
             total += jnp.where(lane == CZ - 1, 0.0, above)
-            out_ref[:, block(r)] = total
+            out_ref[:, block(r - shift)] = total
 
 
 def lane_hot(idx):
@@ -140,7 +147,7 @@
 
 def mixed_kernel(
     live_ref, v_ref, w_ref, frac_ref, idx_ref, vol_ref, face_ref, mat_ref, sel_ref,
-    int_ref, u_ref, fm_ref, wg_ref, fh_ref, fs_ref, power_ref,
+    int_ref, u_ref, fm_ref, wg_ref, fh_ref, fs_ref, power_ref, first_ref,
     g_ref, small_ref, diag_ref, wpad_ref,
 ):
     small_ref[...] = jnp.zeros((32, 128), F32)
@@ -160,7 +167,8 @@
         first = 7 * 128 + 64 * k
         fh_ref[32 * k:32 * k + 32, :] = stack_left(laid[:, first:first + 64], 32)
     fs_ref[...] = stack_left(laid[:, 9 * 128:11 * 128], 128)
-    interior(v_ref, wg_ref, g_ref, int_ref)
+    int_ref[:, 1024:3072] = jnp.zeros((32, 2048), F32)
+    interior(v_ref, wg_ref, g_ref, int_ref, (0, 3))
 
     for m in range(4):
         small_ref[0:27, 0:27] = mat_ref[:, m, :]
@@ -183,10 +191,10 @@
     first = jnp.where(live, first, 0.0)
     first = jnp.concatenate([first[0:27], jnp.where(live, frac, 0.0), first[31:32]], axis=0)
 
-    dense = to_zones(first, lane_hot(idx), idx)
-    for g in range(GROUPS):
+    first_ref[...] = first
+    groups = (0, 1, 2, 3, 12, 13, 14, 15)
+    for g, here in zip(groups, to_zones(first, lane_hot(idx), idx, groups)):
         cols = slice(g * GROUP, (g + 1) * GROUP)
-        here = dense[g]
         u_ref[:, cols] = jnp.where(here[27:28] > 0.0, here, v_ref[:, cols])
         fm_ref[:, cols] = here[24:32]
 
@@ -204,24 +212,25 @@
     return stack_left(rows, 64)
 
 
-def to_zones(values, hot, idx):
+def to_zones(values, hot, idx, groups=tuple(range(GROUPS))):
     both = jnp.concatenate(halves(values), axis=0)
     group = lax.shift_right_logical(idx, 8)
-    parts = [both * jnp.where(group == g, 1.0, 0.0).astype(BF16) for g in range(GROUPS)]
+    parts = [both * jnp.where(group == g, 1.0, 0.0).astype(BF16) for g in groups]
     dense = lax.dot_general(
         jnp.concatenate(parts, axis=0), hot, (((1,), (1,)), ((), ())), preferred_element_type=F32
     )
     rows = values.shape[0]
     return [
         dense[2 * rows * g:2 * rows * g + rows] + dense[2 * rows * g + rows:2 * rows * (g + 1)]
-        for g in range(GROUPS)
+        for g in range(len(groups))
     ]
 
 
 def later_kernel(
-    live_ref, after_ref, power_ref, w_ref, frac_ref, idx_ref,
-    c2_ref, c3_ref, pp_ref, b3_ref, wpad_ref,
-):
+    live_ref, after_ref, power_ref, w_ref, frac_ref, idx_ref, v_ref, wg_ref, first_ref,
+    c2_ref, c3_ref, pp_ref, b3_ref, mid_ref, u_mid_ref, fm_mid_ref, wpad_ref, g_ref,
+):
+    interior(v_ref, wg_ref, g_ref, mid_ref, (1, 2), CY)
     eye = identity()
     p1 = power_ref[...]
     p2 = product(p1, p1)
@@ -239,7 +248,14 @@
         b3_ref[m] = values[32:64]
         total = total + frac[m:m + 1, :] * values
     idx = idx_ref[...]
-    dense = to_zones(jnp.where(live_ref[...] > 0.0, total, 0.0), lane_hot(idx), idx)
+    hot = lane_hot(idx)
+    groups = tuple(range(4, 12))
+    for g, here in zip(groups, to_zones(first_ref[...], hot, idx, groups)):
+        cols = slice((g - 4) * GROUP, (g - 3) * GROUP)
+        old = v_ref[:, g * GROUP:(g + 1) * GROUP]
+        u_mid_ref[:, cols] = jnp.where(here[27:28] > 0.0, here, old)
+        fm_mid_ref[:, cols] = here[24:32]
+    dense = to_zones(jnp.where(live_ref[...] > 0.0, total, 0.0), hot, idx)
     for g in range(GROUPS):
         cols = slice(g * GROUP, (g + 1) * GROUP)
         c2_ref[:, cols] = dense[g][0:32]
@@ -315,13 +331,19 @@
 
 
 def x_first_kernel(
-    int_ref, u_ref, v_ref, fh_ref, xl_ref, xh_ref,
-    next_ref, rate_ref, beside_ref, ylo_ref, yhi_ref, pad_ref, own_ref,
+    int_ref, mid_ref, u_ref, u_mid_ref, fm_ref, fm_mid_ref, v_ref, fh_ref, xl_ref, xh_ref,
+    next_ref, rate_ref, beside_ref, f_ref, ylo_ref, yhi_ref, pad_ref, own_ref,
 ):
     pad_ref[...] = jnp.zeros((16, 3072), F32)
     halo_x(xl_ref, xh_ref, pad_ref)
     halo_add(int_ref, fh_ref, pad_ref, rate_ref, True, False)
-    next_ref[...] = u_ref[...] + rate_ref[...]
+    rate_ref[:, 1024:3072] += mid_ref[...]
+    for x in range(CX):
+        cols = slice(x * 1024, (x + 1) * 1024)
+        inner = slice((x - 1) * 1024, x * 1024)
+        u = u_mid_ref[:, inner] if x in (1, 2) else u_ref[:, cols]
+        next_ref[:, cols] = u + rate_ref[:, cols]
+        f_ref[:, cols] = fm_mid_ref[:, inner] if x in (1, 2) else fm_ref[:, cols]
     y_faces(next_ref, ylo_ref, yhi_ref)
     own_ref[...] = jnp.zeros((16, 2048), F32)
     own_ref[0:9, 0:1024] = v_ref[0:9, 0:1024]
@@ -500,9 +522,10 @@
     )
     halo = exchange_y(*out[:2])
     weights, frac, idx, *_ = small = out[2:]
-    inner, u, fm, wg, fh, fs, power = call(
+    inner, u, fm, wg, fh, fs, power, first = call(
         mixed_kernel,
-        [DENSE, DENSE, f32(8, ZONES), bf(224, 128), bf(128, 64), bf(32, 256), f32(128, 128)],
+        [DENSE, DENSE, f32(8, ZONES), bf(224, 128), bf(128, 64), bf(32, 256), f32(128, 128),
+         f32(32, SLOTS)],
         [live, v0] + small,
         [g_space, pltpu.VMEM((32, 128), F32), pltpu.VMEM((128, 128), F32),
          pltpu.VMEM((32, SLOTS), F32)],
@@ -512,13 +535,16 @@
         y_first_kernel, [DENSE] + X_TWICE, [inner, u, v0, fh, *halo], [pad]
     )
     halo = exchange_x(*faces)
-    c2, c3, pp, b3 = call(
-        later_kernel, [DENSE, DENSE, bf(128, 256), SLOT3],
-        [live, faces[0], power, weights, frac, idx], [pltpu.VMEM((32, SLOTS), F32)],
+    c2, c3, pp, b3, mid, u_mid, fm_mid = call(
+        later_kernel,
+        [DENSE, DENSE, bf(128, 256), SLOT3, f32(32, 2048), f32(32, 2048), f32(8, 2048)],
+        [live, faces[0], power, weights, frac, idx, v0, wg, first],
+        [pltpu.VMEM((32, SLOTS), F32), g_space],
         flops=2 * 10**9,
     )
-    v1, r0, beside, *faces = call(
-        x_first_kernel, [DENSE, DENSE, f32(16, 2048)] + Y_FACES, [inner, u, v0, fh, *halo],
+    v1, r0, beside, fm, *faces = call(
+        x_first_kernel, [DENSE, DENSE, f32(16, 2048), f32(8, ZONES)] + Y_FACES,
+        [inner, mid, u, u_mid, fm, fm_mid, v0, fh, *halo],
         [pad, pltpu.VMEM((16, 2048), F32)],
     )
     halo = exchange_y(*faces)

time: 45.1 us -> 45.2 us (level)
    ppermute x2, starting transfers between devices: 6.7 us -> 5.97 us  [exchange_x(): below = lax.ppermute(high, 'gx', [(i, i + 1) for i in range(n - 1)])]
  transfers between devices with their start and end apart: 10 -> 10, of which waited for: 1 -> 1; matrix products, arithmetic and copies ran while one was open for 0% -> 0% of each run, Pallas kernels for 19% -> 20%
where the time goes in v6:
time: 45.2 us; the launch traced here: 44.9 us
  starting transfers between devices  30.3 us (67%)
  Pallas kernels  12.6 us (28%)
  between operations  1.46 us (3%)
  waiting for transfers between devices  0.49 us (1%)
    ppermute x3, starting transfers between devices, exchange_y(): above = lax.ppermute(low, 'yz', [(i, (i - 1) % n) for i in range(n)])  14.4 us
    pallas_call x9, Pallas kernels, call(): pl.pallas_call(kernel, out_shape=outs, in_specs=[in_spec] * len(args), ou...  12.6 us
    ppermute x2, starting transfers between devices, exchange_x(): above = lax.ppermute(low, 'gx', [(i + 1, i) for i in range(n - 1)])  9.92 us
    ppermute x2, starting transfers between devices, exchange_x(): below = lax.ppermute(high, 'gx', [(i, i + 1) for i in range(n - 1)])  5.97 us
  transfers between devices with their start and end apart: 10, of which 1 were waited for; matrix products, arithmetic and copies ran while one was open for 0% of the time, Pallas kernels for 20%

profile of v6, /device:TPU:6, one launch (start us, length us, event | category | flops | bytes accessed | tf_op | source)
XLA Modules:
  0.0 44.9 jit_solution(1308738304156288730)
XLA Ops:
  0.6 1.4 %shard_map.104 = (f32[32,4096]{1,0:T(8,128)S(1)}, f32[36,128]{1,0:T(8,128)S(1)}, f32[36,128]{1,0:T(8,128)S(1)}, f32[27,4,1024]{2,1,0:T(4,128)S(1)}, f32[4,1024]{...) custom-call(f32[864,128]{1,0:T(8,128)} %bitcast.13, ...), custom_call_target="tpu_custom_call" | custom-call | bytes 2690936 | tf_op jit(solution)/shard_map/pallas_call | solution.py:471
  2.0 0.0 collective-permute-start
  2.1 8.5 %collective-permute-start.1 = (f32[36,128]{1,0:T(8,128)S(1)}, f32[36,128]{1,0:T(8,128)S(1)}, u32[]{:S(2)}, u32[]{:S(2)}) collective-permute-start(f32[36,128]{1,0:T(8,128)S(1)} %get-tuple-element.60), channel_id=1, source_target_pairs={{0,15},{1,0},{2,1},{3,2},{4,3},{5,4},{6,5},{7,6},{8,7},{9,8},{10,9... | collective-permute-start | bytes 55304 | tf_op jit(solution)/shard_map/ppermute | solution.py:492
  11.2 1.7 %shard_map.105 = (f32[32,4096]{1,0:T(8,128)S(1)}, f32[32,4096]{1,0:T(8,128)S(1)}, f32[8,4096]{1,0:T(8,128)S(1)}, bf16[224,128]{1,0:T(8,128)(2,1)S(1)}, bf16[128,...) custom-call(f32[1,1024]{1,0:T(1,128)S(1)} %compare_select_fusion.live_ref, ...), custom_call_target="tpu_custom_call" | custom-call | flops 3000000000 | bytes 2928572 | tf_op jit(solution)/shard_map/pallas_call | solution.py:471
  12.9 0.0 collective-permute-done.yl_ref
  13.0 0.0 collective-permute-done.1.yh_ref
  13.0 0.2 shard_map.106
  13.1 3.5 %collective-permute-start.2 = (f32[144,128]{1,0:T(8,128)S(1)}, f32[144,128]{1,0:T(8,128)S(1)}, u32[]{:S(2)}, u32[]{:S(2)}) collective-permute-start(f32[144,128]{1,0:T(8,128)S(1)} %get-tuple-element.70), channel_id=1, source_target_pairs={{0,16},{16,32},{32,48},{48,64},{64,80},{80,96},{96,112},{112,128},... | collective-permute-start | bytes 221192 | tf_op jit(solution)/shard_map/ppermute | solution.py:484
  16.6 4.5 %collective-permute-start.3 = (f32[144,128]{1,0:T(8,128)S(1)}, f32[144,128]{1,0:T(8,128)S(1)}, u32[]{:S(2)}, u32[]{:S(2)}) collective-permute-start(f32[144,128]{1,0:T(8,128)S(1)} %get-tuple-element.62.after_ref), channel_id=1, source_target_pairs={{16,0},{32,16},{48,32},{64,48},{80,64},{96,80},{112,96},{128,112},... | collective-permute-start | bytes 221192 | tf_op jit(solution)/shard_map/ppermute | solution.py:485
  21.1 2.7 %shard_map.107 = (f32[32,4096]{1,0:T(8,128)S(1)}, f32[32,4096]{1,0:T(8,128)S(1)}, bf16[128,256]{1,0:T(8,128)(2,1)S(1)}, f32[4,32,1024]{2,1,0:T(8,128)S(1)}, f32[...) custom-call(f32[1,1024]{1,0:T(1,128)S(1)} %compare_select_fusion.live_ref, ...), custom_call_target="tpu_custom_call" | custom-call | flops 2000000000 | bytes 3670016 | tf_op jit(solution)/shard_map/pallas_call | solution.py:471
  23.9 0.0 collective-permute-done.2.xl_ref
  23.9 0.0 collective-permute-done.3.xh_ref
  23.9 0.3 shard_map.108
  24.1 0.0 collective-permute-start.4
  24.2 2.9 %collective-permute-start.5 = (f32[36,128]{1,0:T(8,128)S(1)}, f32[36,128]{1,0:T(8,128)S(1)}, u32[]{:S(2)}, u32[]{:S(2)}) collective-permute-start(f32[36,128]{1,0:T(8,128)S(1)} %get-tuple-element.80), channel_id=1, source_target_pairs={{0,15},{1,0},{2,1},{3,2},{4,3},{5,4},{6,5},{7,6},{8,7},{9,8},{10,9... | collective-permute-start | bytes 55304 | tf_op jit(solution)/shard_map/ppermute | solution.py:492
  27.1 1.0 %shard_map.109 = (f32[32,4096]{1,0:T(8,128)S(1)}, f32[32,4096]{1,0:T(8,128)S(1)}) custom-call(f32[32,4096]{1,0:T(8,128)S(1)} %get-tuple-element.48.v_ref.v0_ref, f32[32,4096]{1,0:T(8,128)S(1)} %get-tuple-element.71.v1_ref, f32[32,4096]{1,0:T(8,128)S(1)} %get-tuple-element.72.r_ref.r0_ref, f32[16,2048]{1,0:T(8,128)S(1)} %get-tuple-element.73.beside_ref, ...), custom_call_target="tpu_custom_call" | custom-call | flops 2000000000 | bytes 3686400 | tf_op jit(solution)/shard_map/pallas_call | solution.py:471
  28.1 0.5 %collective-permute-done.4.yl_ref = f32[36,128]{1,0:T(8,128)S(1)} collective-permute-done((f32[36,128]{1,0:T(8,128)S(1)}, f32[36,128]{1,0:T(8,128)S(1)}, u32[]{:S(2)}, u32[]{:S(2)}) %collective-permute-start.4) | collective-permute-done | bytes 18464 | tf_op jit(solution)/shard_map/ppermute | solution.py:491
  28.6 0.0 collective-permute-done.5.yh_ref
  28.6 0.2 shard_map.110
  28.8 0.0 collective-permute-start.6
  28.8 2.9 %collective-permute-start.7 = (f32[36,128]{1,0:T(8,128)S(1)}, f32[36,128]{1,0:T(8,128)S(1)}, u32[]{:S(2)}, u32[]{:S(2)}) collective-permute-start(f32[36,128]{1,0:T(8,128)S(1)} %get-tuple-element.88), channel_id=1, source_target_pairs={{0,15},{1,0},{2,1},{3,2},{4,3},{5,4},{6,5},{7,6},{8,7},{9,8},{10,9... | collective-permute-start | bytes 55304 | tf_op jit(solution)/shard_map/ppermute | solution.py:492
  31.8 2.5 %collective-permute-start.8 = (f32[72,128]{1,0:T(8,128)S(1)}, f32[72,128]{1,0:T(8,128)S(1)}, u32[]{:S(2)}, u32[]{:S(2)}) collective-permute-start(f32[72,128]{1,0:T(8,128)S(1)} %get-tuple-element.89), channel_id=1, source_target_pairs={{0,16},{16,32},{32,48},{48,64},{64,80},{80,96},{96,112},{112,128},... | collective-permute-start | bytes 110600 | tf_op jit(solution)/shard_map/ppermute | solution.py:484
  34.3 5.5 %collective-permute-start.9 = (f32[72,128]{1,0:T(8,128)S(1)}, f32[72,128]{1,0:T(8,128)S(1)}, u32[]{:S(2)}, u32[]{:S(2)}) collective-permute-start(f32[72,128]{1,0:T(8,128)S(1)} %get-tuple-element.90), channel_id=1, source_target_pairs={{16,0},{32,16},{48,32},{64,48},{80,64},{96,80},{112,96},{128,112},... | collective-permute-start | bytes 110600 | tf_op jit(solution)/shard_map/ppermute | solution.py:485
  39.7 3.3 %shard_map.111 = (f32[32,4096]{1,0:T(8,128)S(1)}, f32[27,4,1024]{2,1,0:T(4,128)S(1)}) custom-call(f32[32,4096]{1,0:T(8,128)S(1)} %get-tuple-element.48.v_ref.v0_ref, f32[32,4096]{1,0:T(8,128)S(1)} %get-tuple-element.81.v2_ref, f32[32,4096]{1,0:T(8,128)S(1)} %get-tuple-element.72.r_ref.r0_ref, f32[32,4096]{1,0:T(8,128)S(1)} %get-tuple-element.82.r1_ref, ...), custom_call_target="tpu_custom_call" | custom-call | flops 2000000000 | bytes 4939776 | tf_op jit(solution)/shard_map/pallas_call | solution.py:471
  43.1 0.0 collective-permute-done.6.yl_ref
  43.1 0.0 collective-permute-done.7.yh_ref
  43.1 0.0 collective-permute-done.8.xl_ref
  43.1 0.0 collective-permute-done.9.xh_ref
  43.1 1.8 %shard_map.112 = (f32[864,128]{1,0:T(8,128)}, f32[27,4,1024]{2,1,0:T(4,128)}) custom-call(f32[1,1024]{1,0:T(1,128)S(1)} %compare_select_fusion.live_ref, f32[32,4096]{1,0:T(8,128)S(1)} %get-tuple-element.85.u_ref, bf16[128,64]{1,0:T(8,128)(2,1)S(1)} %get-tuple-element.58.fh_ref, bf16[32,256]{1,0:T(8,128)(2,1)S(1)} %get-tuple-element.86.fs_ref, ...), custom_call_target="tpu_custom_call" | custom-call | bytes 2035712 | tf_op jit(solution)/shard_map/pallas_call | solution.py:471
  (1 shorter events, 0.0 us)
Async XLA Ops:
  2.0 10.9 %collective-permute-start = (f32[36,128]{1,0:T(8,128)S(1)}, f32[36,128]{1,0:T(8,128)S(1)}, u32[]{:S(2)}, u32[]{:S(2)}) collective-permute-start(f32[36,128]{1,0:T(8,128)S(1)} %get-tuple-element.59), channel_id=1, source_target_pairs={{0,1},{1,2},{2,3},{3,4},{4,5},{5,6},{6,7},{7,8},{8,9},{9,10},{10,1... | collective-permute-start | bytes 55304 | tf_op jit(solution)/shard_map/ppermute | solution.py:491
  2.1 10.9 %collective-permute-start.1 = (f32[36,128]{1,0:T(8,128)S(1)}, f32[36,128]{1,0:T(8,128)S(1)}, u32[]{:S(2)}, u32[]{:S(2)}) collective-permute-start(f32[36,128]{1,0:T(8,128)S(1)} %get-tuple-element.60), channel_id=1, source_target_pairs={{0,15},{1,0},{2,1},{3,2},{4,3},{5,4},{6,5},{7,6},{8,7},{9,8},{10,9... | collective-permute-start | bytes 55304 | tf_op jit(solution)/shard_map/ppermute | solution.py:492
  13.1 10.7 %collective-permute-start.2 = (f32[144,128]{1,0:T(8,128)S(1)}, f32[144,128]{1,0:T(8,128)S(1)}, u32[]{:S(2)}, u32[]{:S(2)}) collective-permute-start(f32[144,128]{1,0:T(8,128)S(1)} %get-tuple-element.70), channel_id=1, source_target_pairs={{0,16},{16,32},{32,48},{48,64},{64,80},{80,96},{96,112},{112,128},... | collective-permute-start | bytes 221192 | tf_op jit(solution)/shard_map/ppermute | solution.py:484
  16.6 7.2 %collective-permute-start.3 = (f32[144,128]{1,0:T(8,128)S(1)}, f32[144,128]{1,0:T(8,128)S(1)}, u32[]{:S(2)}, u32[]{:S(2)}) collective-permute-start(f32[144,128]{1,0:T(8,128)S(1)} %get-tuple-element.62.after_ref), channel_id=1, source_target_pairs={{16,0},{32,16},{48,32},{64,48},{80,64},{96,80},{112,96},{128,112},... | collective-permute-start | bytes 221192 | tf_op jit(solution)/shard_map/ppermute | solution.py:485
  24.1 4.4 %collective-permute-start.4 = (f32[36,128]{1,0:T(8,128)S(1)}, f32[36,128]{1,0:T(8,128)S(1)}, u32[]{:S(2)}, u32[]{:S(2)}) collective-permute-start(f32[36,128]{1,0:T(8,128)S(1)} %get-tuple-element.79), channel_id=1, source_target_pairs={{0,1},{1,2},{2,3},{3,4},{4,5},{5,6},{6,7},{7,8},{8,9},{9,10},{10,1... | collective-permute-start | bytes 55304 | tf_op jit(solution)/shard_map/ppermute | solution.py:491
  24.2 4.4 %collective-permute-start.5 = (f32[36,128]{1,0:T(8,128)S(1)}, f32[36,128]{1,0:T(8,128)S(1)}, u32[]{:S(2)}, u32[]{:S(2)}) collective-permute-start(f32[36,128]{1,0:T(8,128)S(1)} %get-tuple-element.80), channel_id=1, source_target_pairs={{0,15},{1,0},{2,1},{3,2},{4,3},{5,4},{6,5},{7,6},{8,7},{9,8},{10,9... | collective-permute-start | bytes 55304 | tf_op jit(solution)/shard_map/ppermute | solution.py:492
  28.8 14.3 %collective-permute-start.6 = (f32[36,128]{1,0:T(8,128)S(1)}, f32[36,128]{1,0:T(8,128)S(1)}, u32[]{:S(2)}, u32[]{:S(2)}) collective-permute-start(f32[36,128]{1,0:T(8,128)S(1)} %get-tuple-element.87), channel_id=1, source_target_pairs={{0,1},{1,2},{2,3},{3,4},{4,5},{5,6},{6,7},{7,8},{8,9},{9,10},{10,1... | collective-permute-start | bytes 55304 | tf_op jit(solution)/shard_map/ppermute | solution.py:491
  28.8 14.3 %collective-permute-start.7 = (f32[36,128]{1,0:T(8,128)S(1)}, f32[36,128]{1,0:T(8,128)S(1)}, u32[]{:S(2)}, u32[]{:S(2)}) collective-permute-start(f32[36,128]{1,0:T(8,128)S(1)} %get-tuple-element.88), channel_id=1, source_target_pairs={{0,15},{1,0},{2,1},{3,2},{4,3},{5,4},{6,5},{7,6},{8,7},{9,8},{10,9... | collective-permute-start | bytes 55304 | tf_op jit(solution)/shard_map/ppermute | solution.py:492
  31.8 11.3 %collective-permute-start.8 = (f32[72,128]{1,0:T(8,128)S(1)}, f32[72,128]{1,0:T(8,128)S(1)}, u32[]{:S(2)}, u32[]{:S(2)}) collective-permute-start(f32[72,128]{1,0:T(8,128)S(1)} %get-tuple-element.89), channel_id=1, source_target_pairs={{0,16},{16,32},{32,48},{48,64},{64,80},{80,96},{96,112},{112,128},... | collective-permute-start | bytes 110600 | tf_op jit(solution)/shard_map/ppermute | solution.py:484
  34.3 8.8 %collective-permute-start.9 = (f32[72,128]{1,0:T(8,128)S(1)}, f32[72,128]{1,0:T(8,128)S(1)}, u32[]{:S(2)}, u32[]{:S(2)}) collective-permute-start(f32[72,128]{1,0:T(8,128)S(1)} %get-tuple-element.90), channel_id=1, source_target_pairs={{16,0},{32,16},{48,32},{64,48},{80,64},{96,80},{112,96},{128,112},... | collective-permute-start | bytes 110600 | tf_op jit(solution)/shard_map/ppermute | solution.py:485

commit v7 on v6

--- a/solution.py
+++ b/solution.py
@@ -285,7 +285,7 @@
     return dot(fh_ref[32 * face:32 * face + 32, :], stack_right(pad_ref[:, first:last]))
 
 
-def halo_add(int_ref, fh_ref, pad_ref, rate_ref, along_x, along_y):
+def halo_add(int_ref, fh_ref, pad_ref, rate_ref, along_x, along_y, strided=False):
     x_low, x_high = [terms(fh_ref, pad_ref, face) for face in (0, 1)] if along_x else (None, None)
     y_low, y_high = [terms(fh_ref, pad_ref, face) for face in (2, 3)] if along_y else (None, None)
     for x in range(CX):
@@ -300,7 +300,10 @@
                 total += y_low[:, block(x)]
             if along_y and y == CY - 1:
                 total += y_high[:, block(x)]
-            rate_ref[:, block(r)] = total
+            if strided:
+                rate_ref[pl.ds(r, 27, stride=32), :] = total[0:27]
+            else:
+                rate_ref[:, block(r)] = total
 
 
 def x_faces(v_ref, xlo_ref, xhi_ref, first=0):
@@ -435,25 +438,26 @@
 
 def last_kernel(
     live_ref, u_ref, fh_ref, fs_ref, yl_ref, yh_ref, xl_ref, xh_ref, idx_ref, slots_ref,
-    field_hbm, out_hbm, pad_ref, whole_ref, field_ref, out_ref, sems,
+    field_hbm, out_hbm, pad_ref, field_ref, out_ref, sems,
 ):
     pad_ref[...] = jnp.zeros((16, 3072), F32)
     halo_x(xl_ref, xh_ref, pad_ref)
     halo_y(yl_ref, yh_ref, pad_ref)
     pad_ref[...] = (2.0 / 3.0) * pad_ref[...]
-    halo_add(u_ref, fh_ref, pad_ref, whole_ref, True, True)
-    for r in range(ROWS):
-        field_ref[pl.ds(r, 27, stride=32), :] = whole_ref[0:27, block(r)]
+    halo_add(u_ref, fh_ref, pad_ref, field_ref, True, True, strided=True)
     field_copy = pltpu.make_async_copy(field_ref, field_hbm, sems.at[0])
     field_copy.start()
     added = dot(fs_ref[...], stack_right(faces_to_slots(pad_ref, idx_ref[...])))
     added = jnp.where(live_ref[...] > 0.0, added, 0.0)
-    for d in range(27):
-        out_ref[d] = slots_ref[d] + added[d:d + 1]
-    out_copy = pltpu.make_async_copy(out_ref, out_hbm, sems.at[1])
-    out_copy.start()
-    field_copy.wait()
-    out_copy.wait()
+    copies = [field_copy]
+    for k in range(3):
+        for d in range(9 * k, 9 * k + 9):
+            out_ref[d] = slots_ref[d] + added[d:d + 1]
+        dofs = pl.ds(9 * k, 9)
+        copies.append(pltpu.make_async_copy(out_ref.at[dofs], out_hbm.at[dofs], sems.at[k + 1]))
+        copies[-1].start()
+    for copy in copies:
+        copy.wait()
 
 
 VMEM = pl.BlockSpec(memory_space=pltpu.VMEM)
@@ -566,8 +570,8 @@
         last_kernel,
         [jax.ShapeDtypeStruct((27 * ROWS, CZ), F32), jax.ShapeDtypeStruct((27, 4, SLOTS), F32)],
         [live, u, fh, fs, *y_halo, *x_halo, idx, slots],
-        [pad, pltpu.VMEM((32, ZONES), F32), pltpu.VMEM((27 * ROWS, CZ), F32),
-         pltpu.VMEM((27, 4, SLOTS), F32), pltpu.SemaphoreType.DMA((2,))],
+        [pad, pltpu.VMEM((27 * ROWS, CZ), F32), pltpu.VMEM((27, 4, SLOTS), F32),
+         pltpu.SemaphoreType.DMA((4,))],
         out_spec=ANY,
     )
     return field.reshape(state.shape), out.transpose(1, 0, 2).reshape(mix_weights.shape)

time: 45.2 us -> 45.2 us (level)
  no operation moved by 1% of the time
where the time goes in v7:
time: 45.2 us; the launch traced here: 44.9 us
  starting transfers between devices  30.3 us (67%)
  Pallas kernels  12.6 us (28%)
  between operations  1.46 us (3%)
  waiting for transfers between devices  0.49 us (1%)
    ppermute x3, starting transfers between devices, exchange_y(): above = lax.ppermute(low, 'yz', [(i, (i - 1) % n) for i in range(n)])  14.4 us
    pallas_call x9, Pallas kernels, call(): pl.pallas_call(kernel, out_shape=outs, in_specs=[in_spec] * len(args), ou...  12.6 us
    ppermute x2, starting transfers between devices, exchange_x(): above = lax.ppermute(low, 'gx', [(i + 1, i) for i in range(n - 1)])  9.92 us
    ppermute x2, starting transfers between devices, exchange_x(): below = lax.ppermute(high, 'gx', [(i, i + 1) for i in range(n - 1)])  5.97 us
  transfers between devices with their start and end apart: 10, of which 1 were waited for; matrix products, arithmetic and copies ran while one was open for 0% of the time, Pallas kernels for 20%

profile of v7, /device:TPU:6, one launch (start us, length us, event | category | flops | bytes accessed | tf_op | source)
XLA Modules:
  0.0 44.9 jit_solution(8643367262857256801)
XLA Ops:
  0.6 1.4 %shard_map.104 = (f32[32,4096]{1,0:T(8,128)S(1)}, f32[36,128]{1,0:T(8,128)S(1)}, f32[36,128]{1,0:T(8,128)S(1)}, f32[27,4,1024]{2,1,0:T(4,128)S(1)}, f32[4,1024]{...) custom-call(f32[864,128]{1,0:T(8,128)} %bitcast.13, ...), custom_call_target="tpu_custom_call" | custom-call | bytes 2690936 | tf_op jit(solution)/shard_map/pallas_call | solution.py:475
  2.0 0.0 collective-permute-start
  2.1 8.5 %collective-permute-start.1 = (f32[36,128]{1,0:T(8,128)S(1)}, f32[36,128]{1,0:T(8,128)S(1)}, u32[]{:S(2)}, u32[]{:S(2)}) collective-permute-start(f32[36,128]{1,0:T(8,128)S(1)} %get-tuple-element.60), channel_id=1, source_target_pairs={{0,15},{1,0},{2,1},{3,2},{4,3},{5,4},{6,5},{7,6},{8,7},{9,8},{10,9... | collective-permute-start | bytes 55304 | tf_op jit(solution)/shard_map/ppermute | solution.py:496
  11.2 1.7 %shard_map.105 = (f32[32,4096]{1,0:T(8,128)S(1)}, f32[32,4096]{1,0:T(8,128)S(1)}, f32[8,4096]{1,0:T(8,128)S(1)}, bf16[224,128]{1,0:T(8,128)(2,1)S(1)}, bf16[128,...) custom-call(f32[1,1024]{1,0:T(1,128)S(1)} %compare_select_fusion.live_ref, ...), custom_call_target="tpu_custom_call" | custom-call | flops 3000000000 | bytes 2928572 | tf_op jit(solution)/shard_map/pallas_call | solution.py:475
  12.9 0.0 collective-permute-done.yl_ref
  13.0 0.0 collective-permute-done.1.yh_ref
  13.0 0.2 shard_map.106
  13.1 3.5 %collective-permute-start.2 = (f32[144,128]{1,0:T(8,128)S(1)}, f32[144,128]{1,0:T(8,128)S(1)}, u32[]{:S(2)}, u32[]{:S(2)}) collective-permute-start(f32[144,128]{1,0:T(8,128)S(1)} %get-tuple-element.70), channel_id=1, source_target_pairs={{0,16},{16,32},{32,48},{48,64},{64,80},{80,96},{96,112},{112,128},... | collective-permute-start | bytes 221192 | tf_op jit(solution)/shard_map/ppermute | solution.py:488
  16.6 4.5 %collective-permute-start.3 = (f32[144,128]{1,0:T(8,128)S(1)}, f32[144,128]{1,0:T(8,128)S(1)}, u32[]{:S(2)}, u32[]{:S(2)}) collective-permute-start(f32[144,128]{1,0:T(8,128)S(1)} %get-tuple-element.62.after_ref), channel_id=1, source_target_pairs={{16,0},{32,16},{48,32},{64,48},{80,64},{96,80},{112,96},{128,112},... | collective-permute-start | bytes 221192 | tf_op jit(solution)/shard_map/ppermute | solution.py:489
  21.1 2.7 %shard_map.107 = (f32[32,4096]{1,0:T(8,128)S(1)}, f32[32,4096]{1,0:T(8,128)S(1)}, bf16[128,256]{1,0:T(8,128)(2,1)S(1)}, f32[4,32,1024]{2,1,0:T(8,128)S(1)}, f32[...) custom-call(f32[1,1024]{1,0:T(1,128)S(1)} %compare_select_fusion.live_ref, ...), custom_call_target="tpu_custom_call" | custom-call | flops 2000000000 | bytes 3670016 | tf_op jit(solution)/shard_map/pallas_call | solution.py:475
  23.9 0.0 collective-permute-done.2.xl_ref
  23.9 0.0 collective-permute-done.3.xh_ref
  23.9 0.3 shard_map.108
  24.1 0.0 collective-permute-start.4
  24.2 2.9 %collective-permute-start.5 = (f32[36,128]{1,0:T(8,128)S(1)}, f32[36,128]{1,0:T(8,128)S(1)}, u32[]{:S(2)}, u32[]{:S(2)}) collective-permute-start(f32[36,128]{1,0:T(8,128)S(1)} %get-tuple-element.80), channel_id=1, source_target_pairs={{0,15},{1,0},{2,1},{3,2},{4,3},{5,4},{6,5},{7,6},{8,7},{9,8},{10,9... | collective-permute-start | bytes 55304 | tf_op jit(solution)/shard_map/ppermute | solution.py:496
  27.1 1.0 %shard_map.109 = (f32[32,4096]{1,0:T(8,128)S(1)}, f32[32,4096]{1,0:T(8,128)S(1)}) custom-call(f32[32,4096]{1,0:T(8,128)S(1)} %get-tuple-element.48.v_ref.v0_ref, f32[32,4096]{1,0:T(8,128)S(1)} %get-tuple-element.71.v1_ref, f32[32,4096]{1,0:T(8,128)S(1)} %get-tuple-element.72.r_ref.r0_ref, f32[16,2048]{1,0:T(8,128)S(1)} %get-tuple-element.73.beside_ref, ...), custom_call_target="tpu_custom_call" | custom-call | flops 2000000000 | bytes 3686400 | tf_op jit(solution)/shard_map/pallas_call | solution.py:475
  28.1 0.5 %collective-permute-done.4.yl_ref = f32[36,128]{1,0:T(8,128)S(1)} collective-permute-done((f32[36,128]{1,0:T(8,128)S(1)}, f32[36,128]{1,0:T(8,128)S(1)}, u32[]{:S(2)}, u32[]{:S(2)}) %collective-permute-start.4) | collective-permute-done | bytes 18464 | tf_op jit(solution)/shard_map/ppermute | solution.py:495
  28.6 0.0 collective-permute-done.5.yh_ref
  28.6 0.2 shard_map.110
  28.8 0.0 collective-permute-start.6
  28.8 2.9 %collective-permute-start.7 = (f32[36,128]{1,0:T(8,128)S(1)}, f32[36,128]{1,0:T(8,128)S(1)}, u32[]{:S(2)}, u32[]{:S(2)}) collective-permute-start(f32[36,128]{1,0:T(8,128)S(1)} %get-tuple-element.88), channel_id=1, source_target_pairs={{0,15},{1,0},{2,1},{3,2},{4,3},{5,4},{6,5},{7,6},{8,7},{9,8},{10,9... | collective-permute-start | bytes 55304 | tf_op jit(solution)/shard_map/ppermute | solution.py:496
  31.8 2.5 %collective-permute-start.8 = (f32[72,128]{1,0:T(8,128)S(1)}, f32[72,128]{1,0:T(8,128)S(1)}, u32[]{:S(2)}, u32[]{:S(2)}) collective-permute-start(f32[72,128]{1,0:T(8,128)S(1)} %get-tuple-element.89), channel_id=1, source_target_pairs={{0,16},{16,32},{32,48},{48,64},{64,80},{80,96},{96,112},{112,128},... | collective-permute-start | bytes 110600 | tf_op jit(solution)/shard_map/ppermute | solution.py:488
  34.3 5.5 %collective-permute-start.9 = (f32[72,128]{1,0:T(8,128)S(1)}, f32[72,128]{1,0:T(8,128)S(1)}, u32[]{:S(2)}, u32[]{:S(2)}) collective-permute-start(f32[72,128]{1,0:T(8,128)S(1)} %get-tuple-element.90), channel_id=1, source_target_pairs={{16,0},{32,16},{48,32},{64,48},{80,64},{96,80},{112,96},{128,112},... | collective-permute-start | bytes 110600 | tf_op jit(solution)/shard_map/ppermute | solution.py:489
  39.7 3.3 %shard_map.111 = (f32[32,4096]{1,0:T(8,128)S(1)}, f32[27,4,1024]{2,1,0:T(4,128)S(1)}) custom-call(f32[32,4096]{1,0:T(8,128)S(1)} %get-tuple-element.48.v_ref.v0_ref, f32[32,4096]{1,0:T(8,128)S(1)} %get-tuple-element.81.v2_ref, f32[32,4096]{1,0:T(8,128)S(1)} %get-tuple-element.72.r_ref.r0_ref, f32[32,4096]{1,0:T(8,128)S(1)} %get-tuple-element.82.r1_ref, ...), custom_call_target="tpu_custom_call" | custom-call | flops 2000000000 | bytes 4939776 | tf_op jit(solution)/shard_map/pallas_call | solution.py:475
  43.1 0.0 collective-permute-done.6.yl_ref
  43.1 0.0 collective-permute-done.7.yh_ref
  43.1 0.0 collective-permute-done.8.xl_ref
  43.1 0.0 collective-permute-done.9.xh_ref
  43.1 1.8 %shard_map.112 = (f32[864,128]{1,0:T(8,128)}, f32[27,4,1024]{2,1,0:T(4,128)}) custom-call(f32[1,1024]{1,0:T(1,128)S(1)} %compare_select_fusion.live_ref, f32[32,4096]{1,0:T(8,128)S(1)} %get-tuple-element.85.u_ref, bf16[128,64]{1,0:T(8,128)(2,1)S(1)} %get-tuple-element.58.fh_ref, bf16[32,256]{1,0:T(8,128)(2,1)S(1)} %get-tuple-element.86.fs_ref, ...), custom_call_target="tpu_custom_call" | custom-call | bytes 2035712 | tf_op jit(solution)/shard_map/pallas_call | solution.py:475
  (1 shorter events, 0.0 us)
Async XLA Ops:
  2.0 10.9 %collective-permute-start = (f32[36,128]{1,0:T(8,128)S(1)}, f32[36,128]{1,0:T(8,128)S(1)}, u32[]{:S(2)}, u32[]{:S(2)}) collective-permute-start(f32[36,128]{1,0:T(8,128)S(1)} %get-tuple-element.59), channel_id=1, source_target_pairs={{0,1},{1,2},{2,3},{3,4},{4,5},{5,6},{6,7},{7,8},{8,9},{9,10},{10,1... | collective-permute-start | bytes 55304 | tf_op jit(solution)/shard_map/ppermute | solution.py:495
  2.1 10.9 %collective-permute-start.1 = (f32[36,128]{1,0:T(8,128)S(1)}, f32[36,128]{1,0:T(8,128)S(1)}, u32[]{:S(2)}, u32[]{:S(2)}) collective-permute-start(f32[36,128]{1,0:T(8,128)S(1)} %get-tuple-element.60), channel_id=1, source_target_pairs={{0,15},{1,0},{2,1},{3,2},{4,3},{5,4},{6,5},{7,6},{8,7},{9,8},{10,9... | collective-permute-start | bytes 55304 | tf_op jit(solution)/shard_map/ppermute | solution.py:496
  13.1 10.7 %collective-permute-start.2 = (f32[144,128]{1,0:T(8,128)S(1)}, f32[144,128]{1,0:T(8,128)S(1)}, u32[]{:S(2)}, u32[]{:S(2)}) collective-permute-start(f32[144,128]{1,0:T(8,128)S(1)} %get-tuple-element.70), channel_id=1, source_target_pairs={{0,16},{16,32},{32,48},{48,64},{64,80},{80,96},{96,112},{112,128},... | collective-permute-start | bytes 221192 | tf_op jit(solution)/shard_map/ppermute | solution.py:488
  16.6 7.2 %collective-permute-start.3 = (f32[144,128]{1,0:T(8,128)S(1)}, f32[144,128]{1,0:T(8,128)S(1)}, u32[]{:S(2)}, u32[]{:S(2)}) collective-permute-start(f32[144,128]{1,0:T(8,128)S(1)} %get-tuple-element.62.after_ref), channel_id=1, source_target_pairs={{16,0},{32,16},{48,32},{64,48},{80,64},{96,80},{112,96},{128,112},... | collective-permute-start | bytes 221192 | tf_op jit(solution)/shard_map/ppermute | solution.py:489
  24.1 4.4 %collective-permute-start.4 = (f32[36,128]{1,0:T(8,128)S(1)}, f32[36,128]{1,0:T(8,128)S(1)}, u32[]{:S(2)}, u32[]{:S(2)}) collective-permute-start(f32[36,128]{1,0:T(8,128)S(1)} %get-tuple-element.79), channel_id=1, source_target_pairs={{0,1},{1,2},{2,3},{3,4},{4,5},{5,6},{6,7},{7,8},{8,9},{9,10},{10,1... | collective-permute-start | bytes 55304 | tf_op jit(solution)/shard_map/ppermute | solution.py:495
  24.2 4.4 %collective-permute-start.5 = (f32[36,128]{1,0:T(8,128)S(1)}, f32[36,128]{1,0:T(8,128)S(1)}, u32[]{:S(2)}, u32[]{:S(2)}) collective-permute-start(f32[36,128]{1,0:T(8,128)S(1)} %get-tuple-element.80), channel_id=1, source_target_pairs={{0,15},{1,0},{2,1},{3,2},{4,3},{5,4},{6,5},{7,6},{8,7},{9,8},{10,9... | collective-permute-start | bytes 55304 | tf_op jit(solution)/shard_map/ppermute | solution.py:496
  28.8 14.3 %collective-permute-start.6 = (f32[36,128]{1,0:T(8,128)S(1)}, f32[36,128]{1,0:T(8,128)S(1)}, u32[]{:S(2)}, u32[]{:S(2)}) collective-permute-start(f32[36,128]{1,0:T(8,128)S(1)} %get-tuple-element.87), channel_id=1, source_target_pairs={{0,1},{1,2},{2,3},{3,4},{4,5},{5,6},{6,7},{7,8},{8,9},{9,10},{10,1... | collective-permute-start | bytes 55304 | tf_op jit(solution)/shard_map/ppermute | solution.py:495
  28.8 14.3 %collective-permute-start.7 = (f32[36,128]{1,0:T(8,128)S(1)}, f32[36,128]{1,0:T(8,128)S(1)}, u32[]{:S(2)}, u32[]{:S(2)}) collective-permute-start(f32[36,128]{1,0:T(8,128)S(1)} %get-tuple-element.88), channel_id=1, source_target_pairs={{0,15},{1,0},{2,1},{3,2},{4,3},{5,4},{6,5},{7,6},{8,7},{9,8},{10,9... | collective-permute-start | bytes 55304 | tf_op jit(solution)/shard_map/ppermute | solution.py:496
  31.8 11.3 %collective-permute-start.8 = (f32[72,128]{1,0:T(8,128)S(1)}, f32[72,128]{1,0:T(8,128)S(1)}, u32[]{:S(2)}, u32[]{:S(2)}) collective-permute-start(f32[72,128]{1,0:T(8,128)S(1)} %get-tuple-element.89), channel_id=1, source_target_pairs={{0,16},{16,32},{32,48},{48,64},{64,80},{80,96},{96,112},{112,128},... | collective-permute-start | bytes 110600 | tf_op jit(solution)/shard_map/ppermute | solution.py:488
  34.3 8.8 %collective-permute-start.9 = (f32[72,128]{1,0:T(8,128)S(1)}, f32[72,128]{1,0:T(8,128)S(1)}, u32[]{:S(2)}, u32[]{:S(2)}) collective-permute-start(f32[72,128]{1,0:T(8,128)S(1)} %get-tuple-element.90), channel_id=1, source_target_pairs={{16,0},{32,16},{48,32},{64,48},{80,64},{96,80},{112,96},{128,112},... | collective-permute-start | bytes 110600 | tf_op jit(solution)/shard_map/ppermute | solution.py:489
